TPU v7x, 32 devices: a whole 2x2x4 slice. The times are simulated.
32 devices in a mesh: seq: 8 (over z, y), head: 4 (over x, core).
Axes of the slice: x: 2, y: 2, z: 4, core: 2. Of those that a mesh axis runs over, the one named last changes fastest.
Arguments:
- tokens: bfloat16 [2, 4096, 2048], P(None, 'seq'), may hold values from -6 to 6
- gain_attn: float32 [2048], replicated, may hold values from 0.5 to 1.5
- query_weight: bfloat16 [2048, 256], P(None, 'head'), may hold values from -0.125 to 0.125
- key_weight: bfloat16 [2048, 256], P(None, 'head'), may hold values from -0.125 to 0.125
- value_weight: bfloat16 [2048, 2048], P(None, 'head'), may hold values from -0.125 to 0.125
- output_weight: bfloat16 [2048, 2048], P('head'), may hold values from -1 to 1
- gain_mlp: float32 [2048], replicated, may hold values from 0.5 to 1.5
- sigmoid_switch_matrix: bfloat16 [2048, 5632], P(None, 'head'), may hold values from -0.125 to 0.125
- up_weight: bfloat16 [2048, 5632], P(None, 'head'), may hold values from -0.125 to 0.125
- down_weight: bfloat16 [5632, 2048], P('head'), may hold values from -0.078125 to 0.078125
- segment_ids: int32 [2, 4096], P(None, 'seq'), may hold values from 0 to 3, never falling along the last dimension, each value on 1 to 2000 neighbouring positions
- cotangent: bfloat16 [2, 4096, 2048], P(None, 'seq'), may hold values from -6 to 6
Outputs:
- result: bfloat16 [2, 4096, 2048], P(None, 'seq')
- d_tokens: float32 [2, 4096, 2048], P(None, 'seq')
- d_gain_attn: float32 [2048], P('seq')
- query_weight_gradient: float32 [2048, 256], P('seq', 'head')
- key_weight_gradient: float32 [2048, 256], P('seq', 'head')
- value_weight_gradient: float32 [2048, 2048], P('seq', 'head')
- output_weight_gradient: float32 [2048, 2048], P('head', 'seq')
- d_gain_mlp: float32 [2048], P('seq')
- gate_weight_gradient: float32 [2048, 5632], P('seq', 'head')
- up_weight_gradient: float32 [2048, 5632], P('seq', 'head')
- down_weight_gradient: float32 [5632, 2048], P('head', 'seq')
Inputs may be any that keep to these rules, and one draw needn't show every extreme that they name: `segment_ids`: along each sequence the document numbers never fall; every number of the range occurs, on 1 to 2000 consecutive tokens, and some document has exactly 2000 tokens.
All inputs are finite; a program needn't handle non-finite values.
Results may differ from a plain program's by a relative error of at most 0.015.
Values sent between devices are 32-bit elements; how exact they have to be, the bound alone decides.
No kernel may reach another device: no remote copies, remote signals or barrier semaphores. Data moves between devices by JAX's collectives and lax.ppermute only.
A program may use at most 256 MiB of HBM per device.

v0:
```python
import math

import jax
import jax.numpy as jnp
from jax import lax
from jax.sharding import PartitionSpec as P

FEAT = 16
HEAD_V = 128


EPS = 1e-05
EXACT_PRECISION = lax.Precision.HIGHEST


def prefix(shard, axis, combine, identity, reverse):
    count, mine = (lax.axis_size(axis), lax.axis_index(axis))
    everything = jax.tree.map(lambda part: lax.all_gather(part, axis), shard)
    start = jax.tree.map(
        lambda part, zero: jnp.broadcast_to(jnp.asarray(zero, part.dtype), part.shape),
        shard,
        identity,
    )

    def turn(k, before):
        at = count - 1 - k if reverse else k
        reached = at > mine if reverse else at < mine
        new = combine(before, jax.tree.map(lambda part: part[at], everything))
        return jax.tree.map(lambda a, b: jnp.where(reached, a, b), new, before)

    return lax.fori_loop(0, count, turn, start)


def taylor(feats):
    feat_width = feats.shape[-1]
    constant = jnp.ones_like(feats[..., :1])
    linear = feats * feat_width ** (-0.25)
    outer_prod = feats[..., :, None] * feats[..., None, :]
    second = outer_prod.reshape(feats.shape[:-1] + (feat_width * feat_width,)) / math.sqrt(
        2.0 * feat_width
    )
    return jnp.concatenate([constant, linear, second], -1)


def taylor_back(feats, grad):
    feat_width = feats.shape[-1]
    linear = grad[..., 1 : 1 + feat_width] * feat_width ** (-0.25)
    second = grad[..., 1 + feat_width :].reshape(grad.shape[:-1] + (feat_width, feat_width))
    symmetric = second + jnp.swapaxes(second, -1, -2)
    return linear + jnp.einsum(
        "sihab,sihb->siha", symmetric, feats, precision=EXACT_PRECISION
    ) / math.sqrt(2.0 * feat_width)


def rms_parts(values, gain):
    scale = lax.rsqrt(jnp.mean(values * values, -1, keepdims=True) + EPS)
    normed = values * scale
    return (normed, scale, (normed * gain).astype(jnp.bfloat16))


def rms_back(normed, scale, gain, grad):
    d_normed = grad * gain
    d_values = scale * (d_normed - normed * jnp.mean(d_normed * normed, -1, keepdims=True))
    return (d_values, jnp.sum(grad * normed, (0, 1)))


def chain_join(earlier, later):
    early_state, early_norm, early_first, early_last = earlier
    late_state, late_norm, late_first, late_last = later
    empty = late_first < 0
    joined = (late_first == late_last) & (early_last == late_last)
    carry_on = jnp.where(empty | joined, 1.0, 0.0)
    joined_state = late_state + carry_on[:, None, None, None] * early_state
    joined_norm = late_norm + carry_on[:, None, None] * early_norm
    first_seg = jnp.where(early_first < 0, late_first, early_first)
    last_seg = jnp.where(empty, early_last, late_last)
    return (joined_state, joined_norm, first_seg, last_seg)


def pass_join(earlier, later):
    early_state, early_norm, early_pass = earlier
    late_state, late_norm, late_pass = later
    return (
        late_state + late_pass[:, None, None, None] * early_state,
        late_norm + late_pass[:, None, None] * early_norm,
        late_pass * early_pass,
    )


def local_parts(query_rows, key_proj, segments):
    block_len = query_rows.shape[1]
    kernel_dot = jnp.einsum(
        "sihf,sjhf->shij", query_rows, key_proj, preferred_element_type=jnp.float32
    ) / math.sqrt(query_rows.shape[-1])
    token_indices = jnp.arange(block_len)
    causal = token_indices[:, None] >= token_indices[None, :]
    same_doc = segments[:, :, None] == segments[:, None, :]
    visible = (causal[None] & same_doc)[:, None]
    scores = jnp.where(visible, 1.0 + kernel_dot + 0.5 * kernel_dot * kernel_dot, 0.0).astype(
        jnp.bfloat16
    )
    feat_query = taylor(query_rows.astype(jnp.float32))
    feat_key = taylor(key_proj.astype(jnp.float32))
    return (kernel_dot, visible, scores, feat_query, feat_key)


def attention_forward(value_proj, segments, parts):
    feat_query, feat_key = (parts[3], parts[4])
    scores = parts[2]
    numer_local = jnp.einsum(
        "shij,sjhe->sihe", scores, value_proj, preferred_element_type=jnp.float32
    )
    denom_local = jnp.swapaxes(jnp.sum(scores.astype(jnp.float32), -1), 1, 2)
    seg_float = segments.astype(jnp.float32)
    in_tail = (segments == segments[:, -1:]).astype(jnp.float32)
    key_tail = feat_key * in_tail[:, :, None, None]
    add_state = jnp.einsum(
        "sjhx,sjhe->shxe", key_tail, value_proj.astype(jnp.float32), precision=EXACT_PRECISION
    )
    add_norm = jnp.sum(key_tail, 1)
    first_seg = seg_float[:, 0]
    last_seg = seg_float[:, -1]
    identity = (
        jnp.zeros_like(add_state),
        jnp.zeros_like(add_norm),
        -jnp.ones_like(first_seg),
        -jnp.ones_like(last_seg),
    )
    prior = prefix((add_state, add_norm, first_seg, last_seg), "seq", chain_join, identity, False)
    uses_prior = (seg_float == prior[3][:, None]).astype(jnp.float32)
    numerator = numer_local + uses_prior[:, :, None, None] * jnp.einsum(
        "sihx,shxe->sihe", feat_query, prior[0], precision=EXACT_PRECISION
    )
    denominator = denom_local + uses_prior[:, :, None] * jnp.einsum(
        "sihx,shx->sih", feat_query, prior[1], precision=EXACT_PRECISION
    )
    return (numerator / denominator[..., None], denominator, prior)


def attention_backward(
    query_rows, key_proj, value_proj, segments, parts, ratio_factor, denominator, prior, d_mixed
):
    kernel_dot, visible, scores, feat_query, feat_key = parts
    prior_state, prior_norm, prior_last = (prior[0], prior[1], prior[3])
    seg_float = segments.astype(jnp.float32)
    uses_prior = (seg_float == prior_last[:, None]).astype(jnp.float32)
    in_tail = (segments == segments[:, -1:]).astype(jnp.float32)
    query_f = query_rows.astype(jnp.float32)
    key_f = key_proj.astype(jnp.float32)
    value_f = value_proj.astype(jnp.float32)
    d_numer = d_mixed / denominator[..., None]
    d_denom = -jnp.sum(d_mixed * ratio_factor, -1) / denominator
    d_numer_low = d_numer.astype(jnp.bfloat16)
    d_scores = jnp.einsum(
        "sihe,sjhe->shij", d_numer_low, value_proj, preferred_element_type=jnp.float32
    )
    d_scores = d_scores + jnp.swapaxes(d_denom, 1, 2)[..., None]
    d_scores = jnp.where(visible, d_scores, 0.0).astype(jnp.bfloat16)
    d_kernel = d_scores.astype(jnp.float32) * (1.0 + kernel_dot)
    dot_scale = 1.0 / math.sqrt(query_rows.shape[-1])
    query_gradient = (
        jnp.einsum("shij,sjhf->sihf", d_kernel, key_f, precision=EXACT_PRECISION) * dot_scale
    )
    key_gradient = (
        jnp.einsum("shij,sihf->sjhf", d_kernel, query_f, precision=EXACT_PRECISION) * dot_scale
    )
    value_gradient = jnp.einsum(
        "shij,sihe->sjhe", scores, d_numer_low, preferred_element_type=jnp.float32
    )
    derivative_of_mapped_question = uses_prior[:, :, None, None] * (
        jnp.einsum("sihe,shxe->sihx", d_numer, prior_state, precision=EXACT_PRECISION)
        + d_denom[..., None] * prior_norm[:, None]
    )
    query_used = feat_query * uses_prior[:, :, None, None]
    d_state_in = jnp.einsum("sihx,sihe->shxe", query_used, d_numer, precision=EXACT_PRECISION)
    d_norm_in = jnp.einsum("sihx,sih->shx", query_used, d_denom, precision=EXACT_PRECISION)
    prefix_running_state = (
        (segments[:, 0] == segments[:, -1]) & (seg_float[:, -1] == prior_last)
    ).astype(jnp.float32)
    identity = (
        jnp.zeros_like(d_state_in),
        jnp.zeros_like(d_norm_in),
        jnp.ones_like(prefix_running_state),
    )
    after = prefix((d_state_in, d_norm_in, prefix_running_state), "seq", pass_join, identity, True)
    later_state, later_norm = (after[0], after[1])
    d_feat_key = in_tail[:, :, None, None] * (
        jnp.einsum("sjhe,shxe->sjhx", value_f, later_state, precision=EXACT_PRECISION)
        + later_norm[:, None]
    )
    value_gradient = value_gradient + in_tail[:, :, None, None] * jnp.einsum(
        "sjhx,shxe->sjhe", feat_key, later_state, precision=EXACT_PRECISION
    )
    query_gradient = query_gradient + taylor_back(query_f, derivative_of_mapped_question)
    key_gradient = key_gradient + taylor_back(key_f, d_feat_key)
    return (
        query_gradient.astype(jnp.bfloat16),
        key_gradient.astype(jnp.bfloat16),
        value_gradient.astype(jnp.bfloat16),
    )


def per_device(
    tokens,
    gain_attn,
    query_weight,
    key_weight,
    value_weight,
    output_weight,
    gain_mlp,
    sigmoid_switch_matrix,
    up_weight,
    down_weight,
    segment_ids,
    cotangent,
):
    seq_count, tok_count, model_width = tokens.shape
    head_count = query_weight.shape[1] // FEAT
    resid = tokens.astype(jnp.float32)
    normed_attn, scale_attn, attention_hidden = rms_parts(resid, gain_attn)
    query_rows = (
        jnp.dot(attention_hidden, query_weight, preferred_element_type=jnp.float32)
        .astype(jnp.bfloat16)
        .reshape(seq_count, tok_count, head_count, FEAT)
    )
    key_proj = (
        jnp.dot(attention_hidden, key_weight, preferred_element_type=jnp.float32)
        .astype(jnp.bfloat16)
        .reshape(seq_count, tok_count, head_count, FEAT)
    )
    value_proj = (
        jnp.dot(attention_hidden, value_weight, preferred_element_type=jnp.float32)
        .astype(jnp.bfloat16)
        .reshape(seq_count, tok_count, head_count, HEAD_V)
    )
    parts = local_parts(query_rows, key_proj, segment_ids)
    ratio_factor, denominator, prior = attention_forward(value_proj, segment_ids, parts)
    blended_embedding = ratio_factor.reshape(seq_count, tok_count, head_count * HEAD_V).astype(
        jnp.bfloat16
    )
    branch_output = lax.psum(
        jnp.dot(blended_embedding, output_weight, preferred_element_type=jnp.float32), "head"
    )
    residual_middle = resid + branch_output
    normed_mlp, scale_mlp, feedforward_hidden = rms_parts(residual_middle, gain_mlp)
    gate_projected = jnp.dot(
        feedforward_hidden, sigmoid_switch_matrix, preferred_element_type=jnp.float32
    )
    up_projected = jnp.dot(feedforward_hidden, up_weight, preferred_element_type=jnp.float32)
    hidden_activation = (jax.nn.silu(gate_projected) * up_projected).astype(jnp.bfloat16)
    mlp_out = lax.psum(
        jnp.dot(hidden_activation, down_weight, preferred_element_type=jnp.float32), "head"
    )
    result = (residual_middle + mlp_out).astype(jnp.bfloat16)
    down_weight_gradient = jnp.einsum(
        "jrg,jrk->gk", hidden_activation, cotangent, preferred_element_type=jnp.float32
    )
    hidden_gradient = jnp.einsum(
        "mtw,iw->mti", cotangent, down_weight, preferred_element_type=jnp.float32
    )
    sigmoid_gate = jax.nn.sigmoid(gate_projected)
    gate_gradient = (
        hidden_gradient
        * up_projected
        * sigmoid_gate
        * (1.0 + gate_projected * (1.0 - sigmoid_gate))
    ).astype(jnp.bfloat16)
    expansion_derivative = (hidden_gradient * gate_projected * sigmoid_gate).astype(jnp.bfloat16)
    gate_weight_gradient = jnp.einsum(
        "oeu,oew->uw", feedforward_hidden, gate_gradient, preferred_element_type=jnp.float32
    )
    up_weight_gradient = jnp.einsum(
        "oeu,oew->uw", feedforward_hidden, expansion_derivative, preferred_element_type=jnp.float32
    )
    hidden_partial_gradient = jnp.einsum(
        "xoh,qh->xoq", gate_gradient, sigmoid_switch_matrix, preferred_element_type=jnp.float32
    )
    hidden_partial_gradient = hidden_partial_gradient + jnp.einsum(
        "xoh,qh->xoq", expansion_derivative, up_weight, preferred_element_type=jnp.float32
    )
    d_h_mlp = lax.psum(hidden_partial_gradient, "head")
    d_mid_norm, d_gain_mlp = rms_back(normed_mlp, scale_mlp, gain_mlp, d_h_mlp)
    d_resid_mid = cotangent.astype(jnp.float32) + d_mid_norm
    sublayer_derivative_sum = d_resid_mid.astype(jnp.bfloat16)
    output_weight_gradient = jnp.einsum(
        "alj,als->js",
        blended_embedding,
        sublayer_derivative_sum,
        preferred_element_type=jnp.float32,
    )
    d_mixed = jnp.einsum(
        "gph,jh->gpj", sublayer_derivative_sum, output_weight, preferred_element_type=jnp.float32
    ).reshape(seq_count, tok_count, head_count, HEAD_V)
    again = local_parts(query_rows, key_proj, segment_ids)
    query_gradient, key_gradient, value_gradient = attention_backward(
        query_rows,
        key_proj,
        value_proj,
        segment_ids,
        again,
        ratio_factor,
        denominator,
        prior,
        d_mixed,
    )
    query_gradient = query_gradient.reshape(seq_count, tok_count, head_count * FEAT)
    key_gradient = key_gradient.reshape(seq_count, tok_count, head_count * FEAT)
    value_gradient = value_gradient.reshape(seq_count, tok_count, head_count * HEAD_V)
    query_weight_gradient = jnp.einsum(
        "uba,ubr->ar", attention_hidden, query_gradient, preferred_element_type=jnp.float32
    )
    key_weight_gradient = jnp.einsum(
        "uba,ubr->ar", attention_hidden, key_gradient, preferred_element_type=jnp.float32
    )
    value_weight_gradient = jnp.einsum(
        "uba,ubr->ar", attention_hidden, value_gradient, preferred_element_type=jnp.float32
    )
    input_partial_gradient = jnp.einsum(
        "xbf,rf->xbr", query_gradient, query_weight, preferred_element_type=jnp.float32
    )
    input_partial_gradient = input_partial_gradient + jnp.einsum(
        "xbf,rf->xbr", key_gradient, key_weight, preferred_element_type=jnp.float32
    )
    input_partial_gradient = input_partial_gradient + jnp.einsum(
        "xbf,rf->xbr", value_gradient, value_weight, preferred_element_type=jnp.float32
    )
    d_h_attn = lax.psum(input_partial_gradient, "head")
    d_in_norm, d_gain_attn = rms_back(normed_attn, scale_attn, gain_attn, d_h_attn)
    d_tokens = d_resid_mid + d_in_norm
    reduced = tuple(
        (
            lax.psum_scatter(d_gain_attn, "seq", scatter_dimension=0, tiled=True),
            lax.psum_scatter(query_weight_gradient, "seq", scatter_dimension=0, tiled=True),
            lax.psum_scatter(key_weight_gradient, "seq", scatter_dimension=0, tiled=True),
            lax.psum_scatter(value_weight_gradient, "seq", scatter_dimension=0, tiled=True),
            lax.psum_scatter(output_weight_gradient, "seq", scatter_dimension=1, tiled=True),
            lax.psum_scatter(d_gain_mlp, "seq", scatter_dimension=0, tiled=True),
            lax.psum_scatter(gate_weight_gradient, "seq", scatter_dimension=0, tiled=True),
            lax.psum_scatter(up_weight_gradient, "seq", scatter_dimension=0, tiled=True),
            lax.psum_scatter(down_weight_gradient, "seq", scatter_dimension=1, tiled=True),
        )
    )
    return (result, d_tokens) + reduced


def solution(mesh):
    return jax.shard_map(
        per_device,
        mesh=mesh,
        in_specs=(
            P(None, "seq", None),
            P(),
            P(None, "head"),
            P(None, "head"),
            P(None, "head"),
            P("head", None),
            P(),
            P(None, "head"),
            P(None, "head"),
            P("head", None),
            P(None, "seq"),
            P(None, "seq", None),
        ),
        out_specs=(
            P(None, "seq", None),
            P(None, "seq", None),
            P("seq"),
            P("seq", "head"),
            P("seq", "head"),
            P("seq", "head"),
            P("head", "seq"),
            P("seq"),
            P("seq", "head"),
            P("seq", "head"),
            P("head", "seq"),
        ),
        check_vma=False,
    )
```

profile of v0, /device:TPU:0, one launch (start us, length us, event | category | flops | bytes accessed | tf_op | source)
XLA Modules:
  0.0 1967.5 jit_solution(17319426349213597809)
XLA Ops:
  28.3 23.6 %all-reduce.6 = (f32[16]{0:T(128)S(1)}, f32[16]{0:T(128)S(1)}) all-reduce(f32[16]{0:T(128)S(1)} %dynamic-update-slice, f32[16]{0:T(128)S(1)} %dynamic-update-slice.1), channel_id=3, replica_groups=mesh['seq'=8,'head'=4] {'seq'}, use_global_device_ids=true, to_apply=%add | all-reduce | flops 32 | bytes 256
  56.7 33.0 %all-gather.3 = f32[16,4,273]{2,1,0:T(4,128)} all-gather(f32[2,4,273]{2,1,0:T(4,128)S(1)} %multiply_reduce_fusion.3), channel_id=5, replica_groups=mesh['seq'=8,'head'=4] {'seq'}, dimensions={0}, use_global_device_ids=true | all-gather | bytes 78624 | tf_op jit(solution)/shard_map/all_gather | solution.py:18
  104.3 57.6 %all-gather.10.cloned.1.call-done = f32[16,4,273,128]{3,1,2,0:T(4,128)} async-done(((f32[2,4,273,128]{3,1,2,0:T(4,128)}), f32[16,4,273,128]{3,1,2,0:T(4,128)}) %all-gather.10.cloned.1.call-update) | async-done | bytes 8945680 | tf_op jit(solution)/shard_map/all_gather | solution.py:18
  161.9 25.9 %while.36 = (s32[]{:T(128)}, f32[2,4,273,128]{3,2,1,0:T(8,128)S(1)}, f32[2,4,273]{2,1,0:T(4,128)S(1)}, f32[2]{0:T(128)S(1)}, s32[]{:T(128)}, /*index=5*/f32[8,2,...) while((s32[]{:T(128)}, ...), condition=%wide.region_3.4_spmd.clone, body=%wide.region_2.3_spmd.clone.sunk | while | flops 1126966 | bytes 5617449 | solution.py:31
  193.7 8.6 fusion.110
  208.9 12.2 fusion.20
  221.2 139.0 %all-reduce.12.cloned.1.call-done = f32[2,512,2048]{2,1,0:T(8,128)} async-done(((f32[2,512,2048]{2,1,0:T(8,128)}), f32[2,512,2048]{2,1,0:T(8,128)}) %all-reduce.12.cloned.1.call-update) | async-done | bytes 8388624 | tf_op jit(solution)/shard_map/psum | solution.py:241
  369.2 11.8 fusion.26
  381.0 15.3 multiply_convert_fusion.2
  396.4 6.7 fusion.24
  403.1 11.6 fusion.51
  414.8 153.1 %all-reduce.14.cloned.1.call-done = f32[2,512,2048]{2,1,0:T(8,128)} async-done(((f32[2,512,2048]{2,1,0:T(8,128)}), f32[2,512,2048]{2,1,0:T(8,128)}) %all-reduce.14.cloned.1.call-update) | async-done | bytes 8388624 | tf_op jit(solution)/shard_map/psum | solution.py:281
  567.9 7.7 multiply_reduce_fusion
  594.7 22.2 %all-reduce.2 = f32[16]{0:T(128)S(1)} all-reduce(f32[16]{0:T(128)S(1)} %fusion.95), channel_id=7, replica_groups=mesh['seq'=8,'head'=4] {'seq'}, use_global_device_ids=true, to_apply=%add.2 | all-reduce | flops 16 | bytes 128
  617.0 11.7 fusion.22
  638.5 31.3 %all-gather.6 = f32[16,4,273]{2,1,0:T(4,128)S(1)} all-gather(f32[2,4,273]{2,1,0:T(4,128)S(1)} %bitcast.274), channel_id=8, replica_groups=mesh['seq'=8,'head'=4] {'seq'}, dimensions={0}, use_global_device_ids=true | all-gather | bytes 78624 | tf_op jit(solution)/shard_map/all_gather | solution.py:18
  687.0 40.7 %all-gather.12.cloned.1.call-done = f32[16,4,273,128]{3,1,2,0:T(4,128)} async-done(((f32[2,4,273,128]{3,1,2,0:T(4,128)}), f32[16,4,273,128]{3,1,2,0:T(4,128)}) %all-gather.12.cloned.1.call-update) | async-done | bytes 8945680 | tf_op jit(solution)/shard_map/all_gather | solution.py:18
  727.7 14.8 while.37
  772.5 7.9 convolution_bitcast_fusion.3
  784.9 12.2 convolution_bitcast_fusion.2
  797.2 12.1 convolution_bitcast_fusion.1
  809.3 11.4 convolution_bitcast_fusion
  820.7 6.9 convolution_bitcast_fusion.4
  828.3 226.5 %all-reduce.16.cloned.1.call-done = (f32[2,512,2048]{2,1,0:T(8,128)}, f32[2,512,2048]{2,1,0:T(8,128)}) async-done(((f32[2,512,2048]{2,1,0:T(8,128)}, f32[2,512,2048]{2,1,0:T(8,128)}), (f32[2,512,2048]{2,1,0:T(8,128)}, f32[2,512,2048]{2,1,0:T(8,128)})) %all-reduce.16.cloned.1.call-update) | async-done | bytes 16777232 | tf_op jit(solution)/shard_map/psum | solution.py:251
  1061.0 37.1 %all-reduce.5 = (f32[2048]{0:T(1024)S(1)}, f32[2048]{0:T(1024)S(1)}) all-reduce(f32[2048]{0:T(1024)S(1)} %get-tuple-element.421, f32[2048]{0:T(1024)S(1)} %copy-done.48), channel_id=9, replica_groups=mesh['seq'=8,'head'=4] {'seq'}, use_global_device_ids=true, to_apply=%region_16.17.clone | all-reduce | flops 4096 | bytes 32768
  1099.4 18.7 fusion.17
  1121.1 92.1 %reduce-scatter.14.cloned.1.call-done = f32[512,256]{1,0:T(8,128)} async-done(((f32[512,2048]{1,0:T(8,128)}), f32[512,256]{1,0:T(8,128)}) %reduce-scatter.14.cloned.1.call-update) | async-done | bytes 524304 | tf_op jit(solution)/shard_map/reduce_scatter | solution.py:336
  1213.2 66.1 %reduce-scatter.10.cloned.1.call-done = f32[256,64]{0,1:T(8,128)} async-done(((f32[2048,64]{0,1:T(8,128)}), f32[256,64]{0,1:T(8,128)}) %reduce-scatter.10.cloned.1.call-update) | async-done | bytes 65552 | tf_op jit(solution)/shard_map/reduce_scatter | solution.py:334
  1279.3 196.4 %reduce-scatter.16.cloned.1.call-done = f32[256,1408]{1,0:T(8,128)} async-done(((f32[2048,1408]{1,0:T(8,128)}), f32[256,1408]{1,0:T(8,128)}) %reduce-scatter.16.cloned.1.call-update) | async-done | bytes 1441808 | tf_op jit(solution)/shard_map/reduce_scatter | solution.py:338
  1475.6 196.3 %reduce-scatter.18.cloned.1.call-done = f32[256,1408]{1,0:T(8,128)} async-done(((f32[2048,1408]{1,0:T(8,128)}), f32[256,1408]{1,0:T(8,128)}) %reduce-scatter.18.cloned.1.call-update) | async-done | bytes 1441808 | tf_op jit(solution)/shard_map/reduce_scatter | solution.py:339
  1671.9 196.8 %reduce-scatter.20.cloned.1.call-done = f32[1408,256]{1,0:T(8,128)} async-done(((f32[1408,2048]{1,0:T(8,128)}), f32[1408,256]{1,0:T(8,128)}) %reduce-scatter.20.cloned.1.call-update) | async-done | bytes 1441808 | tf_op jit(solution)/shard_map/reduce_scatter | solution.py:340
  1868.8 91.7 %reduce-scatter.12.cloned.1.call-done = f32[256,512]{1,0:T(8,128)} async-done(((f32[2048,512]{1,0:T(8,128)}), f32[256,512]{1,0:T(8,128)}) %reduce-scatter.12.cloned.1.call-update) | async-done | bytes 524304 | tf_op jit(solution)/shard_map/reduce_scatter | solution.py:335
  (315 shorter events, 191.7 us)
Async XLA Ops:
  7.2 196.0 %copy-start = (bf16[512,2048]{1,0:T(8,128)(2,1)S(1)}, bf16[512,2048]{1,0:T(8,128)(2,1)}, u32[]{:S(2)}) copy-start(bf16[512,2048]{1,0:T(8,128)(2,1)} %param.21) | copy-start | bytes 6291460
  7.2 154.7 %all-gather.10.cloned.1.call-start = ((), (), s32[]{:S(2)}) async-start(), calls=%async_computation.16 | async-start | bytes 10063872 | tf_op jit(solution)/shard_map/all_gather | solution.py:18
  10.5 79.3 %copy-start.46 = (f32[2,512]{1,0:T(2,128)}, f32[2,512]{1,0:T(2,128)S(1)}, u32[]{:S(2)}) copy-start(f32[2,512]{1,0:T(2,128)S(1)} %add_rsqrt_fusion.1) | copy-start | bytes 12292
  18.2 35.1 %copy-start.24 = (f32[2,512,4,16]{1,3,2,0:T(8,128)}, f32[2,512,4,16]{1,3,2,0:T(8,128)S(1)}, u32[]{:S(2)}) copy-start(f32[2,512,4,16]{1,3,2,0:T(8,128)S(1)} %broadcast_multiply_fusion.1) | copy-start | bytes 786436
  22.1 31.2 %copy-start.37 = (f32[2,512]{1,0:T(2,128)}, f32[2,512]{1,0:T(2,128)S(1)}, u32[]{:S(2)}) copy-start(f32[2,512]{1,0:T(2,128)S(1)} %compare_convert_fusion.1) | copy-start | bytes 12292
  26.3 333.9 %all-reduce.12.cloned.1.call-start = ((), (), s32[]{:S(2)}) async-start(), calls=%async_computation.7 | async-start | bytes 16777216 | tf_op jit(solution)/shard_map/psum | solution.py:241
  27.9 24.1 %copy-start.58 = (f32[2]{0:T(128)}, f32[2]{0:T(128)S(1)}, u32[]{:S(2)}) copy-start(f32[2]{0:T(128)S(1)} %get-tuple-element.425) | copy-start | bytes 28
  53.4 36.4 %copy-start.4 = (bf16[2,512,2048]{2,1,0:T(8,128)(2,1)S(1)}, bf16[2,512,2048]{2,1,0:T(8,128)(2,1)}, u32[]{:S(2)}) copy-start(bf16[2,512,2048]{2,1,0:T(8,128)(2,1)} %param.16) | copy-start | bytes 12582916
  53.4 36.4 %copy-start.35 = (bf16[2048,64]{0,1:T(8,128)(2,1)S(1)}, bf16[2048,64]{0,1:T(8,128)(2,1)}, u32[]{:S(2)}) copy-start(bf16[2048,64]{0,1:T(8,128)(2,1)} %param.18) | copy-start | bytes 786436
  100.2 61.7 %copy-start.51 = (f32[2]{0:T(128)S(1)}, f32[2]{0:T(128)}, u32[]{:S(2)}) copy-start(f32[2]{0:T(128)} %custom-call.2) | copy-start | bytes 28
  187.8 14.5 copy-start.52
  208.9 359.1 %all-reduce.14.cloned.1.call-start = ((), (), s32[]{:S(2)}) async-start(), calls=%async_computation.8 | async-start | bytes 16777216 | tf_op jit(solution)/shard_map/psum | solution.py:281
  221.2 144.7 %copy-start.40 = (f32[2048]{0:T(1024)S(1)}, f32[2048]{0:T(1024)}, u32[]{:S(2)}) copy-start(f32[2048]{0:T(1024)} %param.22) | copy-start | bytes 24580
  369.2 11.8 copy-start.14
  369.2 27.2 %slice-start.6 = ((s8[5767168]{0:T(1024)(128)(4,1)}), s8[1572864]{0:T(1024)(128)(4,1)S(1)}, s32[]{:S(2)}) async-start(s8[5767168]{0:T(1024)(128)(4,1)} %bitcast.277), calls=%async_computation.25 | async-start | bytes 3145728
  381.0 15.3 slice-start.7
  414.8 312.9 %all-gather.12.cloned.1.call-start = ((), (), s32[]{:S(2)}) async-start(), calls=%async_computation.17 | async-start | bytes 10063872 | tf_op jit(solution)/shard_map/all_gather | solution.py:18
  594.4 460.4 %all-reduce.16.cloned.1.call-start = ((), (), s32[]{:S(2)}) async-start(), calls=%async_computation.18 | async-start | bytes 33554432 | tf_op jit(solution)/shard_map/psum | solution.py:251
  617.0 11.8 copy-start.12
  637.7 32.1 %copy-start.42 = (f32[2,4,512]{2,1,0:T(4,128)S(1)}, f32[2,4,512]{2,1,0:T(4,128)}, u32[]{:S(2)}) copy-start(f32[2,4,512]{2,1,0:T(4,128)} %get-tuple-element.467) | copy-start | bytes 49156
  637.7 32.1 %copy-start.23 = (f32[2,512,4,16]{1,3,2,0:T(8,128)S(1)}, f32[2,512,4,16]{1,3,2,0:T(8,128)}, u32[]{:S(2)}) copy-start(f32[2,512,4,16]{1,3,2,0:T(8,128)} %copy-done.22) | copy-start | bytes 786436
  637.7 35.7 %copy-start.19 = (bf16[2,512,512]{1,2,0:T(8,128)(2,1)S(1)}, bf16[2,512,512]{1,2,0:T(8,128)(2,1)}, u32[]{:S(2)}) copy-start(bf16[2,512,512]{1,2,0:T(8,128)(2,1)} %copy-done.17) | copy-start | bytes 3145732
  637.8 35.7 %copy-start.33 = (pred[2,512,512]{1,2,0:T(8,128)(4,1)S(1)}, pred[2,512,512]{1,2,0:T(8,128)(4,1)}, u32[]{:S(2)}) copy-start(pred[2,512,512]{1,2,0:T(8,128)(4,1)} %copy-done.32) | copy-start | bytes 1572868
  727.7 14.8 copy-start.38
  767.5 353.6 %reduce-scatter.8.cloned.1.call-start = ((), (), s32[]{:S(2)}) async-start(), calls=%async_computation.9 | async-start | bytes 589824 | tf_op jit(solution)/shard_map/reduce_scatter | solution.py:333
  772.5 440.7 %reduce-scatter.14.cloned.1.call-start = ((), (), s32[]{:S(2)}) async-start(), calls=%async_computation.12 | async-start | bytes 4718592 | tf_op jit(solution)/shard_map/reduce_scatter | solution.py:336
  780.5 498.8 %reduce-scatter.10.cloned.1.call-start = ((), (), s32[]{:S(2)}) async-start(), calls=%async_computation.10 | async-start | bytes 589824 | tf_op jit(solution)/shard_map/reduce_scatter | solution.py:334
  784.8 690.8 %reduce-scatter.16.cloned.1.call-start = ((), (), s32[]{:S(2)}) async-start(), calls=%async_computation.13 | async-start | bytes 12976128 | tf_op jit(solution)/shard_map/reduce_scatter | solution.py:338
  797.1 874.8 %reduce-scatter.18.cloned.1.call-start = ((), (), s32[]{:S(2)}) async-start(), calls=%async_computation.14 | async-start | bytes 12976128 | tf_op jit(solution)/shard_map/reduce_scatter | solution.py:339
  809.2 1059.5 %reduce-scatter.20.cloned.1.call-start = ((), (), s32[]{:S(2)}) async-start(), calls=%async_computation.15 | async-start | bytes 12976128 | tf_op jit(solution)/shard_map/reduce_scatter | solution.py:340
  820.7 1139.8 %reduce-scatter.12.cloned.1.call-start = ((), (), s32[]{:S(2)}) async-start(), calls=%async_computation.11 | async-start | bytes 4718592 | tf_op jit(solution)/shard_map/reduce_scatter | solution.py:335
  1099.4 861.1 %copy-start.1 = (bf16[512,2048]{1,0:T(8,128)(2,1)S(1)}, bf16[512,2048]{1,0:T(8,128)(2,1)}, u32[]{:S(2)}) copy-start(bf16[512,2048]{1,0:T(8,128)(2,1)} %param.21) | copy-start | bytes 6291460
  (55 other events, 272.0 us)
Sparse Core Ops, SparseCore 0:
  26.4 135.4 all-gather.9
  209.0 151.0 all-reduce.11
  414.9 153.0 all-reduce.13
  594.6 133.0 all-gather.11
  767.6 287.2 all-reduce.15
  1058.6 62.3 reduce-scatter.7
  1125.7 87.4 reduce-scatter.13
  1217.1 62.1 reduce-scatter.9
  1283.9 191.7 reduce-scatter.15
  1480.1 191.8 reduce-scatter.17
  1676.6 192.1 reduce-scatter.19
  1873.3 87.1 reduce-scatter.11
where the time goes:
time: 1980 us; the launch traced here: 1970 us
  waiting for transfers between devices  1460 us (74%)
  matrix products  219 us (11%)
  blocking collectives  147 us (7%)
  other arithmetic  81.3 us (4%)
  local copies, waits for them, and re-layouts  42.3 us (2%)
    psum x1, waiting for transfers between devices, per_device(): lax.psum(jnp.dot(hidden_activation, down_weight, preferred_element_type=j...  227 us
    reduce_scatter x1, waiting for transfers between devices, per_device(): lax.psum_scatter(down_weight_gradient, 'seq', scatter_dimension=1, tiled=...  197 us
    reduce_scatter x1, waiting for transfers between devices, per_device(): lax.psum_scatter(gate_weight_gradient, 'seq', scatter_dimension=0, tiled=...  196 us
    reduce_scatter x1, waiting for transfers between devices, per_device(): lax.psum_scatter(up_weight_gradient, 'seq', scatter_dimension=0, tiled=True)  196 us
    psum x1, waiting for transfers between devices, per_device(): d_h_mlp = lax.psum(hidden_partial_gradient, 'head')  153 us
    psum x1, waiting for transfers between devices, per_device(): lax.psum(jnp.dot(blended_embedding, output_weight, preferred_element_type...  139 us
    all_gather x2, waiting for transfers between devices, prefix(): everything = jax.tree.map(lambda part: lax.all_gather(part, axis), shard)  98.4 us
    reduce_scatter x1, waiting for transfers between devices, per_device(): lax.psum_scatter(output_weight_gradient, 'seq', scatter_dimension=1, tile...  92.1 us
  transfers between devices with their start and end apart: 12, of which 12 were waited for; matrix products, arithmetic and copies ran while one was open for 8% of the time, Pallas kernels for 0%

commit v1 on v0

v1 whole, which is shorter than its diff:
```python
import math

import jax
import jax.numpy as jnp
from jax import lax
from jax.sharding import PartitionSpec as P

FEAT = 16
HEAD_V = 128


EPS = 1e-05


PASSAGE_CEILING = 2000


def swap(part, bit):
    count = lax.axis_size("head")
    return lax.ppermute(part, "head", [(k, k ^ bit) for k in range(count)])


def shift(part, by):
    count = lax.axis_size("seq")
    pairs = [(k, k + by) for k in range(count) if 0 <= k + by < count]
    return jax.tree.map(lambda leaf: lax.ppermute(leaf, "seq", pairs), part)


def head_sum(own, other):
    total = own + swap(other, 1)
    bit = 2
    while bit < lax.axis_size("head"):
        total = total + swap(total, bit)
        bit *= 2
    return total


def weighted(factor, part):
    return jax.tree.map(lambda leaf: factor.reshape((-1,) + (1,) * (leaf.ndim - 1)) * leaf, part)


def add(first, second):
    return jax.tree.map(lambda a, b: a + b, first, second)


def window(part, carries, direction, reach):
    near, far = shift(part, direction), shift(part, 2 * direction)
    carry = shift(carries, direction)
    total = add(near, weighted(carry, far))
    product = shift(carries * carry, direction)
    width = 2
    while width < reach:
        total = add(total, weighted(product, shift(total, width * direction)))
        product = product * shift(product, width * direction)
        width *= 2
    return total


def columns_dot(left, right):
    return lax.dot_general(left, right, (((0,), (0,)), ((), ())), preferred_element_type=jnp.float32)


def line_sum(pieces, place, length, along):
    def piece(at):
        return lax.dynamic_index_in_dim(pieces, jnp.clip(at, 0, length - 1), 0, keepdims=False)

    right = left = None
    for step in range(1, length):
        go_right = piece(place + length - step)
        go_left = piece(place - length + step)
        if right is not None:
            go_right, go_left = go_right + right, go_left + left
        right = along(go_right, [(k, k + 1) for k in range(step)])
        left = along(go_left, [(k, k - 1) for k in range(length - step, length)])
    return piece(place) + right + left


def line_along(part, pairs):
    return lax.ppermute(part, "seq", [(2 * a + y, 2 * b + y) for a, b in pairs for y in range(2)])


def pair_along(part):
    return lax.ppermute(part, "seq", [(k, k ^ 1) for k in range(lax.axis_size("seq"))])


class Columns:
    def __init__(self, value):
        count = lax.axis_size("seq")
        self.value = value
        tokens, width = value.shape
        self.block = width // count
        parts = value.reshape(tokens, count // 2, 2, self.block)
        y = lax.axis_index("seq") % 2
        self.mine = lax.dynamic_index_in_dim(parts, y, 2, keepdims=False).reshape(tokens, width // 2)
        self.theirs = lax.dynamic_index_in_dim(parts, 1 - y, 2, keepdims=False).reshape(tokens, width // 2)


def pair_first(left, right):
    count = lax.axis_size("seq")
    if count > 8:
        return lax.psum_scatter(columns_dot(left.value, right), "seq", scatter_dimension=0, tiled=True)
    came = pair_along(columns_dot(left.theirs, right))
    halves = columns_dot(left.mine, right) + came
    pieces = halves.reshape(count // 2, left.block, right.shape[1])
    return line_sum(pieces, lax.axis_index("seq") // 2, count // 2, line_along)


def line_first(left, right):
    count = lax.axis_size("seq")
    if count > 8:
        return lax.psum_scatter(columns_dot(left.value, right), "seq", scatter_dimension=0, tiled=True)
    whole = columns_dot(left.value, right).reshape(count // 2, 2 * left.block, right.shape[1])
    pairs = line_sum(whole, lax.axis_index("seq") // 2, count // 2, line_along)
    pairs = pairs.reshape(2, left.block, right.shape[1])
    y = lax.axis_index("seq") % 2
    theirs = lax.dynamic_index_in_dim(pairs, 1 - y, 0, keepdims=False)
    return lax.dynamic_index_in_dim(pairs, y, 0, keepdims=False) + pair_along(theirs)


def taylor(feats):
    feat_width = feats.shape[-1]
    constant = jnp.ones_like(feats[..., :1])
    linear = feats * feat_width ** (-0.25)
    outer_prod = feats[..., :, None] * feats[..., None, :]
    second = outer_prod.reshape(feats.shape[:-1] + (feat_width * feat_width,)) / math.sqrt(
        2.0 * feat_width
    )
    return jnp.concatenate([constant, linear, second], -1)


def taylor_back(feats, grad):
    feat_width = feats.shape[-1]
    linear = grad[..., 1 : 1 + feat_width] * feat_width ** (-0.25)
    second = grad[..., 1 + feat_width :].reshape(grad.shape[:-1] + (feat_width, feat_width))
    symmetric = second + jnp.swapaxes(second, -1, -2)
    return linear + jnp.einsum("sihab,sihb->siha", symmetric, feats) / math.sqrt(2.0 * feat_width)


def rms_norm(values):
    scale = lax.rsqrt(jnp.mean(values * values, -1, keepdims=True) + EPS)
    return values * scale, scale


def rms_back(normed, scale, gain, grad):
    d_normed = grad * gain
    d_values = scale * (d_normed - normed * jnp.mean(d_normed * normed, -1, keepdims=True))
    return (d_values, jnp.sum(grad * normed, 0))


def local_parts(query_rows, key_proj, segments):
    block_len = query_rows.shape[1]
    kernel_dot = jnp.einsum(
        "sihf,sjhf->shij", query_rows, key_proj, preferred_element_type=jnp.float32
    ) / math.sqrt(query_rows.shape[-1])
    token_indices = jnp.arange(block_len)
    causal = token_indices[:, None] >= token_indices[None, :]
    same_doc = segments[:, :, None] == segments[:, None, :]
    visible = (causal[None] & same_doc)[:, None]
    scores = jnp.where(visible, 1.0 + kernel_dot + 0.5 * kernel_dot * kernel_dot, 0.0).astype(
        jnp.bfloat16
    )
    feat_query = taylor(query_rows.astype(jnp.float32))
    feat_key = taylor(key_proj.astype(jnp.float32))
    return (kernel_dot, visible, scores, feat_query, feat_key)


def attention_forward(value_proj, segments, parts, carried, uses_prior, reach):
    feat_query, feat_key = (parts[3], parts[4])
    scores = parts[2]
    in_tail = (segments == segments[:, -1:]).astype(jnp.float32)
    key_tail = feat_key * in_tail[:, :, None, None]
    add_state = jnp.einsum("sjhx,sjhe->shxe", key_tail, value_proj.astype(jnp.float32))
    add_norm = jnp.sum(key_tail, 1)
    prior = window((add_state, add_norm), carried, 1, reach)
    numer_local = jnp.einsum(
        "shij,sjhe->sihe", scores, value_proj, preferred_element_type=jnp.float32
    )
    denom_local = jnp.swapaxes(jnp.sum(scores.astype(jnp.float32), -1), 1, 2)
    numerator = numer_local + uses_prior[:, :, None, None] * jnp.einsum(
        "sihx,shxe->sihe", feat_query, prior[0]
    )
    denominator = denom_local + uses_prior[:, :, None] * jnp.einsum(
        "sihx,shx->sih", feat_query, prior[1]
    )
    return (numerator / denominator[..., None], denominator, prior)


def attention_backward(
    query_rows, key_proj, value_proj, segments, parts, ratio_factor, denominator, prior, d_mixed,
    carried, uses_prior, reach,
):
    kernel_dot, visible, scores, feat_query, feat_key = parts
    prior_state, prior_norm = prior
    in_tail = (segments == segments[:, -1:]).astype(jnp.float32)
    query_f = query_rows.astype(jnp.float32)
    key_f = key_proj.astype(jnp.float32)
    value_f = value_proj.astype(jnp.float32)
    d_numer = d_mixed / denominator[..., None]
    d_denom = -jnp.sum(d_mixed * ratio_factor, -1) / denominator
    query_used = feat_query * uses_prior[:, :, None, None]
    d_state_in = jnp.einsum("sihx,sihe->shxe", query_used, d_numer)
    d_norm_in = jnp.einsum("sihx,sih->shx", query_used, d_denom)
    later_state, later_norm = window((d_state_in, d_norm_in), carried, -1, reach)
    d_numer_low = d_numer.astype(jnp.bfloat16)
    d_scores = jnp.einsum(
        "sihe,sjhe->shij", d_numer_low, value_proj, preferred_element_type=jnp.float32
    )
    d_scores = d_scores + jnp.swapaxes(d_denom, 1, 2)[..., None]
    d_scores = jnp.where(visible, d_scores, 0.0).astype(jnp.bfloat16)
    d_kernel = d_scores.astype(jnp.float32) * (1.0 + kernel_dot)
    dot_scale = 1.0 / math.sqrt(query_rows.shape[-1])
    query_gradient = jnp.einsum("shij,sjhf->sihf", d_kernel, key_f) * dot_scale
    key_gradient = jnp.einsum("shij,sihf->sjhf", d_kernel, query_f) * dot_scale
    value_gradient = jnp.einsum(
        "shij,sihe->sjhe", scores, d_numer_low, preferred_element_type=jnp.float32
    )
    d_feat_query = uses_prior[:, :, None, None] * (
        jnp.einsum("sihe,shxe->sihx", d_numer, prior_state) + d_denom[..., None] * prior_norm[:, None]
    )
    query_gradient = query_gradient + taylor_back(query_f, d_feat_query)
    d_feat_key = in_tail[:, :, None, None] * (
        jnp.einsum("sjhe,shxe->sjhx", value_f, later_state) + later_norm[:, None]
    )
    value_gradient = value_gradient + in_tail[:, :, None, None] * jnp.einsum(
        "sjhx,shxe->sjhe", feat_key, later_state
    )
    key_gradient = key_gradient + taylor_back(key_f, d_feat_key)
    return (
        query_gradient.astype(jnp.bfloat16),
        key_gradient.astype(jnp.bfloat16),
        value_gradient.astype(jnp.bfloat16),
    )


CHUNKS = 2


def dot(left, right):
    return jnp.dot(left, right, preferred_element_type=jnp.float32)


def dot_t(left, right):
    return lax.dot_general(left, right, (((left.ndim - 1,), (1,)), ((), ())), preferred_element_type=jnp.float32)


def per_device(
    tokens,
    gain_attn,
    query_weight,
    key_weight,
    value_weight,
    output_weight,
    gain_mlp,
    sigmoid_switch_matrix,
    up_weight,
    down_weight,
    segment_ids,
    cotangent,
):
    seq_count, tok_count, model_width = tokens.shape
    head_count = query_weight.shape[1] // FEAT
    reach = min(lax.axis_size("seq") - 1, -(-(PASSAGE_CEILING - 1) // tok_count))
    core = lax.axis_index("head") % 2

    def relative(whole):
        own = lax.dynamic_index_in_dim(whole, core, 0, keepdims=False)
        other = lax.dynamic_index_in_dim(whole, 1 - core, 0, keepdims=False)
        return jnp.stack([own, other])

    def absolute(own, other):
        return jnp.stack([jnp.where(core == 0, own, other), jnp.where(core == 0, other, own)])

    tokens, cotangent, segments = relative(tokens), relative(cotangent), relative(segment_ids)
    seg_float = segments.astype(jnp.float32)
    prior_last = shift(seg_float[:, -1] + 1.0, 1) - 1.0
    carried = ((segments[:, 0] == segments[:, -1]) & (seg_float[:, -1] == prior_last)).astype(jnp.float32)
    uses_prior = (seg_float == prior_last[:, None]).astype(jnp.float32)

    resid = tokens.astype(jnp.float32)
    normed_attn, scale_attn = rms_norm(resid)
    h_attn = (normed_attn * gain_attn).astype(jnp.bfloat16)
    shape = (seq_count, tok_count, head_count)
    query_rows = dot(h_attn, query_weight).astype(jnp.bfloat16).reshape(shape + (FEAT,))
    key_proj = dot(h_attn, key_weight).astype(jnp.bfloat16).reshape(shape + (FEAT,))
    value_proj = dot(h_attn, value_weight).astype(jnp.bfloat16).reshape(shape + (HEAD_V,))
    parts = local_parts(query_rows, key_proj, segments)
    ratio, denominator, prior = attention_forward(value_proj, segments, parts, carried, uses_prior, reach)
    mixed = ratio.reshape(seq_count, tok_count, head_count * HEAD_V).astype(jnp.bfloat16)

    step = tok_count // CHUNKS
    spans = [slice(k * step, (k + 1) * step) for k in range(CHUNKS)]
    branches = [head_sum(dot(mixed[0, s], output_weight), dot(mixed[1, s], output_weight)) for s in spans]

    mids, normeds, scales, h_mlps, hiddens, d_gates, d_ups, d_hs = [], [], [], [], [], [], [], []
    cots = [cotangent[:, s].reshape(-1, model_width) for s in spans]
    for s, branch, cot in zip(spans, branches, cots):
        mid = resid[:, s] + jnp.stack([branch, swap(branch, 1)])
        normed, scale = rms_norm(mid)
        h_mlp = (normed * gain_mlp).astype(jnp.bfloat16).reshape(-1, model_width)
        gate, up = dot(h_mlp, sigmoid_switch_matrix), dot(h_mlp, up_weight)
        sigmoid = jax.nn.sigmoid(gate)
        hidden = (gate * sigmoid * up).astype(jnp.bfloat16)
        d_hidden = dot_t(cot, down_weight)
        d_gate = (d_hidden * up * sigmoid * (1.0 + gate * (1.0 - sigmoid))).astype(jnp.bfloat16)
        d_up = (d_hidden * gate * sigmoid).astype(jnp.bfloat16)
        d_parts = [
            dot_t(d_gate[p], sigmoid_switch_matrix) + dot_t(d_up[p], up_weight)
            for p in (slice(0, step), slice(step, 2 * step))
        ]
        d_hs.append(head_sum(*d_parts))
        for into, value in zip((mids, normeds, scales, h_mlps, hiddens, d_gates, d_ups),
                               (mid, normed[0], scale[0], h_mlp, hidden, d_gate, d_up)):
            into.append(value)

    def join(values):
        return jnp.concatenate(values, 0)

    cot_columns, h_columns = Columns(join(cots)), Columns(join(h_mlps))
    hidden_all, d_gate_all, d_up_all = join(hiddens), join(d_gates), join(d_ups)
    cut = (hidden_all.shape[1] * 6 // 11) // 128 * 128
    down_a = pair_first(cot_columns, hidden_all[:, :cut])
    down_b = line_first(cot_columns, hidden_all[:, cut:])
    gate_weight_gradient = pair_first(h_columns, d_gate_all)
    up_weight_gradient = pair_first(h_columns, d_up_all)

    d_mids, d_gain_mlp = [], 0.0
    for s, normed, scale, d_h in zip(spans, normeds, scales, d_hs):
        d_own, d_gain = rms_back(normed, scale, gain_mlp, d_h)
        d_gain_mlp = d_gain_mlp + d_gain
        d_mids.append(cotangent[:, s].astype(jnp.float32) + jnp.stack([d_own, swap(d_own, 1)]))
    d_resid_mid = jnp.concatenate(d_mids, 1)
    d_branch = d_resid_mid.astype(jnp.bfloat16)
    d_mixed = dot_t(d_branch, output_weight).reshape(shape + (HEAD_V,))

    mlp_outs = []
    for k, s in enumerate(spans):
        out = head_sum(dot(hiddens[k][:step], down_weight), dot(hiddens[k][step:], down_weight))
        mlp_outs.append((mids[k] + jnp.stack([out, swap(out, 1)])).astype(jnp.bfloat16))
    result = jnp.concatenate(mlp_outs, 1)

    out_rows = pair_first(Columns(d_branch.reshape(-1, model_width)), mixed.reshape(-1, mixed.shape[-1]))

    d_query, d_key, d_value = attention_backward(
        query_rows, key_proj, value_proj, segments, parts, ratio, denominator, prior, d_mixed,
        carried, uses_prior, reach,
    )
    d_query, d_key, d_value = (
        part.reshape(seq_count * tok_count, -1) for part in (d_query, d_key, d_value)
    )
    d_in = []
    for p in (0, 1):
        rows = slice(p * tok_count, (p + 1) * tok_count)
        d_in.append(
            dot_t(d_query[rows], query_weight) + dot_t(d_key[rows], key_weight) + dot_t(d_value[rows], value_weight)
        )
    d_tokens = []
    d_gain_attn = 0.0
    for s in spans:
        d_h = head_sum(d_in[0][s], d_in[1][s])
        d_own, d_gain = rms_back(normed_attn[0, s], scale_attn[0, s], gain_attn, d_h)
        d_gain_attn = d_gain_attn + d_gain
        d_own = d_own + d_resid_mid[0, s]
        d_tokens.append(jnp.stack([d_own, swap(d_own, 1)]))
    d_tokens = jnp.concatenate(d_tokens, 1)
    qkv_rows = pair_first(
        Columns(h_attn.reshape(-1, model_width)), jnp.concatenate([d_query, d_key, d_value], 1)
    )

    gains = jnp.stack([d_gain_attn, d_gain_mlp])
    gains = gains + swap(gains, 1)
    count = lax.axis_size("seq")
    if count > 8:
        gains = lax.psum_scatter(gains, "seq", scatter_dimension=1, tiled=True)
    else:
        y = lax.axis_index("seq") % 2
        gains = gains.reshape(2, count // 2, 2, -1).transpose(1, 2, 0, 3)
        mine = lax.dynamic_index_in_dim(gains, y, 1, keepdims=False)
        theirs = lax.dynamic_index_in_dim(gains, 1 - y, 1, keepdims=False)
        gains = line_sum(mine + pair_along(theirs), lax.axis_index("seq") // 2, count // 2, line_along)

    narrow = query_weight.shape[1]
    return (
        absolute(result[0], result[1]),
        absolute(d_tokens[0], d_tokens[1]),
        gains[0],
        qkv_rows[:, :narrow],
        qkv_rows[:, narrow : 2 * narrow],
        qkv_rows[:, 2 * narrow :],
        out_rows.T,
        gains[1],
        gate_weight_gradient,
        up_weight_gradient,
        jnp.concatenate([down_a.T, down_b.T], 0),
    )


def solution(mesh):
    return jax.shard_map(
        per_device,
        mesh=mesh,
        in_specs=(
            P(None, "seq", None),
            P(),
            P(None, "head"),
            P(None, "head"),
            P(None, "head"),
            P("head", None),
            P(),
            P(None, "head"),
            P(None, "head"),
            P("head", None),
            P(None, "seq"),
            P(None, "seq", None),
        ),
        out_specs=(
            P(None, "seq", None),
            P(None, "seq", None),
            P("seq"),
            P("seq", "head"),
            P("seq", "head"),
            P("seq", "head"),
            P("head", "seq"),
            P("seq"),
            P("seq", "head"),
            P("seq", "head"),
            P("head", "seq"),
        ),
        check_vma=False,
    )
```

time: 1980 us -> 1240 us (0.63)
  waiting for transfers between devices: 1460 us -> 360 us
  starting transfers between devices: 0.5 us -> 329 us
  local copies, waits for them, and re-layouts: 42.3 us -> 191 us
  blocking collectives: 147 us -> 0 us
  other arithmetic: 81.3 us -> 151 us
  matrix products: 219 us -> 195 us
    reduce_scatter x7 -> x0, waiting for transfers between devices: 842 us -> none  [the longest x1 197 us: per_device(): lax.psum_scatter(down_weight_gradient, 'seq', scatter_dimension=1, tiled=...]
    psum x3 -> x0, waiting for transfers between devices: 519 us -> none  [the longest x1 227 us: per_device(): lax.psum(jnp.dot(hidden_activation, down_weight, preferred_element_type=j...]
    ppermute x0 -> x91, waiting for transfers between devices: none -> 360 us  [the longest x25 154 us: swap(): return lax.ppermute(part, 'head', [(k, k ^ bit) for k in range(count)])]
    ppermute x0 -> x91, starting transfers between devices: none -> 329 us  [the longest x42 242 us: line_along(): lax.ppermute(part, 'seq', [(2 * a + y, 2 * b + y) for a, b in pairs for y...]
    all_gather x2 -> x0, waiting for transfers between devices: 98.4 us -> none  [prefix(): everything = jax.tree.map(lambda part: lax.all_gather(part, axis), shard)]
    unnamed x3 -> x0, blocking collectives: 83 us -> none
    all_gather x2 -> x0, blocking collectives: 64.4 us -> none  [prefix(): everything = jax.tree.map(lambda part: lax.all_gather(part, axis), shard)]
    add x2 -> x50, other arithmetic: 23.3 us -> 67.5 us  [the longest x24 26.1 us: line_sum(): go_right, go_left = (go_right + right, go_left + left)]
  transfers between devices with their start and end apart: 12 -> 91, of which waited for: 12 -> 31; matrix products, arithmetic and copies ran while one was open for 8% -> 36% of each run, Pallas kernels for 0% -> 0%
where the time goes in v1:
time: 1240 us; the launch traced here: 1230 us
  waiting for transfers between devices  360 us (29%)
  starting transfers between devices  329 us (27%)
  matrix products  195 us (16%)
  local copies, waits for them, and re-layouts  191 us (15%)
  other arithmetic  151 us (12%)
    ppermute x42, starting transfers between devices, line_along(): lax.ppermute(part, 'seq', [(2 * a + y, 2 * b + y) for a, b in pairs for y...  242 us
    ppermute x25, waiting for transfers between devices, swap(): return lax.ppermute(part, 'head', [(k, k ^ bit) for k in range(count)])  154 us
    ppermute x42, waiting for transfers between devices, line_along(): lax.ppermute(part, 'seq', [(2 * a + y, 2 * b + y) for a, b in pairs for y...  117 us
    ppermute x17, starting transfers between devices, shift(): return jax.tree.map(lambda leaf: lax.ppermute(leaf, 'seq', pairs), part)  68 us
    ppermute x17, waiting for transfers between devices, shift(): return jax.tree.map(lambda leaf: lax.ppermute(leaf, 'seq', pairs), part)  61.4 us
    dot_general x17, matrix products, dot_t(): lax.dot_general(left, right, (((left.ndim - 1,), (1,)), ((), ())), prefer...  60.4 us
    dot_general x15, matrix products, dot(): return jnp.dot(left, right, preferred_element_type=jnp.float32)  55.4 us
    dot_general x11, matrix products, columns_dot(): lax.dot_general(left, right, (((0,), (0,)), ((), ())), preferred_element_...  45.5 us
  transfers between devices with their start and end apart: 91, of which 31 were waited for; matrix products, arithmetic and copies ran while one was open for 36% of the time, Pallas kernels for 0%

profile of v1, /device:TPU:0, one launch (start us, length us, event | category | flops | bytes accessed | tf_op | source)
XLA Modules:
  0.0 1229.8 jit_solution(5812729551460180211)
XLA Ops:
  57.2 28.8 %collective-permute-start.5 = (f32[2,4,273,128]{3,1,2,0:T(4,128)S(1)}, f32[2,4,273,128]{3,1,2,0:T(4,128)S(1)}, u32[]{:S(2)}, u32[]{:S(2)}) collective-permute-start(f32[2,4,273,128]{3,1,2,0:T(4,128)S(1)} %multiply_add_fusion.3), channel_id=1, source_target_pairs={{0,8},{4,12},{8,16},{12,20},{16,24},{20,28},{1,9},{5,13},{9,17},{1... | collective-permute-start | bytes 3354632 | tf_op jit(solution)/shard_map/ppermute | solution.py:26
  95.3 13.0 %collective-permute-done.8 = f32[2,4,273]{2,1,0:T(4,128)S(1)} collective-permute-done((f32[2,4,273]{2,1,0:T(4,128)S(1)}, f32[2,4,273]{2,1,0:T(4,128)S(1)}, u32[]{:S(2)}, u32[]{:S(2)}) %collective-permute-start.8) | collective-permute-done | bytes 8768 | tf_op jit(solution)/shard_map/ppermute | solution.py:26
  130.4 11.8 reshape.460
  142.2 13.2 %copy.167 = f32[1024,4,2,256]{0,3,1,2:T(8,128)} copy(f32[1024,4,2,256]{3,2,1,0:T(2,128)} %reshape.460) | data formatting | bytes 16777216 | tf_op jit(solution)/shard_map/convert_element_type | solution.py:279
  187.6 25.3 %collective-permute-done.16 = f32[256,2048]{1,0:T(8,128)} collective-permute-done((f32[256,2048]{1,0:T(8,128)}, f32[256,2048]{1,0:T(8,128)}, u32[]{:S(2)}, u32[]{:S(2)}) %collective-permute-start.16) | collective-permute-done | bytes 2097184 | tf_op jit(solution)/shard_map/ppermute | solution.py:20
  243.4 8.6 multiply_convert_fusion.4
  274.0 7.4 multiply_convert_fusion.6
  341.7 17.4 %collective-permute-done.84 = f32[512,640]{1,0:T(8,128)S(1)} collective-permute-done((f32[512,640]{1,0:T(8,128)S(1)}, f32[512,640]{1,0:T(8,128)S(1)}, u32[]{:S(2)}, u32[]{:S(2)}) %collective-permute-start.84) | collective-permute-done | bytes 1310752 | tf_op jit(solution)/shard_map/ppermute | solution.py:79
  374.9 18.2 %collective-permute-done.85 = f32[512,640]{1,0:T(8,128)S(1)} collective-permute-done((f32[512,640]{1,0:T(8,128)S(1)}, f32[512,640]{1,0:T(8,128)S(1)}, u32[]{:S(2)}, u32[]{:S(2)}) %collective-permute-start.85) | collective-permute-done | bytes 1310752 | tf_op jit(solution)/shard_map/ppermute | solution.py:79
  396.3 8.9 collective-permute-done.77
  466.7 20.2 %collective-permute-done.13 = f32[256,2048]{1,0:T(8,128)} collective-permute-done((f32[256,2048]{1,0:T(8,128)}, f32[256,2048]{1,0:T(8,128)}, u32[]{:S(2)}, u32[]{:S(2)}) %collective-permute-start.13) | collective-permute-done | bytes 2097184 | tf_op jit(solution)/shard_map/ppermute | solution.py:20
  487.6 44.2 %collective-permute-done.19 = f32[256,2048]{1,0:T(8,128)} collective-permute-done((f32[256,2048]{1,0:T(8,128)}, f32[256,2048]{1,0:T(8,128)}, u32[]{:S(2)}, u32[]{:S(2)}) %collective-permute-start.19) | collective-permute-done | bytes 2097184 | tf_op jit(solution)/shard_map/ppermute | solution.py:20
  536.3 39.2 %collective-permute-done.25 = f32[256,2048]{1,0:T(8,128)} collective-permute-done((f32[256,2048]{1,0:T(8,128)}, f32[256,2048]{1,0:T(8,128)}, u32[]{:S(2)}, u32[]{:S(2)}) %collective-permute-start.25) | collective-permute-done | bytes 2097184 | tf_op jit(solution)/shard_map/ppermute | solution.py:20
  606.6 12.8 %collective-permute-done.89 = f32[512,640]{1,0:T(8,128)S(1)} collective-permute-done((f32[512,640]{1,0:T(8,128)S(1)}, f32[512,640]{1,0:T(8,128)S(1)}, u32[]{:S(2)}, u32[]{:S(2)}) %collective-permute-start.89) | collective-permute-done | bytes 1310752 | tf_op jit(solution)/shard_map/ppermute | solution.py:79
  623.0 11.0 collective-permute-done.83
  640.5 11.2 collective-permute-done.70
  686.9 7.8 convert_element_type.202
  714.2 9.8 constant_dynamic-slice_fusion.15
  723.9 10.8 copy.237
  772.0 10.6 copy.236
  794.6 39.6 %collective-permute-done.27 = f32[2,4,273,128]{3,1,2,0:T(4,128)S(1)} collective-permute-done((f32[2,4,273,128]{3,1,2,0:T(4,128)}, f32[2,4,273,128]{3,1,2,0:T(4,128)S(1)}, u32[]{:S(2)}, u32[]{:S(2)}) %collective-permute-start.27) | collective-permute-done | bytes 1118240 | tf_op jit(solution)/shard_map/ppermute | solution.py:26
  922.1 60.6 %collective-permute-start.58 = (f32[256,512]{0,1:T(8,128)S(1)}, f32[256,512]{0,1:T(8,128)S(1)}, u32[]{:S(2)}, u32[]{:S(2)}) collective-permute-start(f32[256,512]{0,1:T(8,128)S(1)} %bitcast_add_fusion.31), channel_id=1, source_target_pairs={{0,8},{4,12},{8,16},{12,20},{1,9},{5,13},{9,17},{13,21},{2,10},{6,... | collective-permute-start | bytes 1572872 | tf_op jit(solution)/shard_map/ppermute | solution.py:79
  1003.9 14.0 %collective-permute-start.59 = (f32[256,512]{0,1:T(8,128)S(1)}, f32[256,512]{0,1:T(8,128)S(1)}, u32[]{:S(2)}, u32[]{:S(2)}) collective-permute-start(f32[256,512]{0,1:T(8,128)S(1)} %bitcast_add_fusion.32), channel_id=1, source_target_pairs={{0,8},{4,12},{8,16},{12,20},{16,24},{20,28},{1,9},{5,13},{9,17},{1... | collective-permute-start | bytes 1572872 | tf_op jit(solution)/shard_map/ppermute | solution.py:79
  1018.8 9.1 collective-permute-done.62
  1029.1 10.0 collective-permute-done.59
  1048.8 24.0 %collective-permute-start.50 = (f32[256,640]{1,0:T(8,128)S(1)}, f32[256,640]{1,0:T(8,128)S(1)}, u32[]{:S(2)}, u32[]{:S(2)}) collective-permute-start(f32[256,640]{1,0:T(8,128)S(1)} %get-tuple-element.132), channel_id=1, source_target_pairs={{0,8},{4,12},{1,9},{5,13},{2,10},{6,14},{3,11},{7,15}} | collective-permute-start | bytes 1966088 | tf_op jit(solution)/shard_map/ppermute | solution.py:79
  1078.0 14.1 %collective-permute-done.69 = f32[256,1408]{1,0:T(8,128)S(1)} collective-permute-done((f32[256,1408]{1,0:T(8,128)}, f32[256,1408]{1,0:T(8,128)S(1)}, u32[]{:S(2)}, u32[]{:S(2)}) %collective-permute-start.69) | collective-permute-done | bytes 1441824 | tf_op jit(solution)/shard_map/ppermute | solution.py:79
  1097.1 15.1 %collective-permute-start.51 = (f32[256,640]{1,0:T(8,128)S(1)}, f32[256,640]{1,0:T(8,128)S(1)}, u32[]{:S(2)}, u32[]{:S(2)}) collective-permute-start(f32[256,640]{1,0:T(8,128)S(1)} %bitcast_add_fusion.26), channel_id=1, source_target_pairs={{0,8},{4,12},{8,16},{12,20},{1,9},{5,13},{9,17},{13,21},{2,10},{6,... | collective-permute-start | bytes 1966088 | tf_op jit(solution)/shard_map/ppermute | solution.py:79
  1112.2 17.9 %collective-permute-done.39 = f32[256,2048]{1,0:T(8,128)} collective-permute-done((f32[256,2048]{1,0:T(8,128)S(1)}, f32[256,2048]{1,0:T(8,128)}, u32[]{:S(2)}, u32[]{:S(2)}) %collective-permute-start.39) | collective-permute-done | bytes 2097184 | tf_op jit(solution)/shard_map/ppermute | solution.py:20
  1139.6 26.0 %collective-permute-start.43 = (f32[2,256]{1,0:T(2,128)S(1)}, f32[2,256]{1,0:T(2,128)S(1)}, u32[]{:S(2)}, u32[]{:S(2)}) collective-permute-start(f32[2,256]{1,0:T(2,128)S(1)} %bitcast.568), channel_id=1, source_target_pairs={{0,8},{4,12},{1,9},{5,13},{2,10},{6,14},{3,11},{7,15}} | collective-permute-start | bytes 6152 | tf_op jit(solution)/shard_map/ppermute | solution.py:79
  1171.1 8.7 fusion.40
  1181.9 14.2 %collective-permute-start.52 = (f32[256,640]{1,0:T(8,128)S(1)}, f32[256,640]{1,0:T(8,128)S(1)}, u32[]{:S(2)}, u32[]{:S(2)}) collective-permute-start(f32[256,640]{1,0:T(8,128)S(1)} %get-tuple-element.130), channel_id=1, source_target_pairs={{0,8},{4,12},{8,16},{12,20},{16,24},{20,28},{1,9},{5,13},{9,17},{1... | collective-permute-start | bytes 1966088 | tf_op jit(solution)/shard_map/ppermute | solution.py:79
  (791 shorter events, 642.3 us)
Async XLA Ops:
  120.0 64.9 %collective-permute-start.10 = (f32[256,2048]{1,0:T(8,128)}, f32[256,2048]{1,0:T(8,128)}, u32[]{:S(2)}, u32[]{:S(2)}) collective-permute-start(f32[256,2048]{1,0:T(8,128)} %convolution_add_fusion.3), channel_id=1, source_target_pairs={{0,2},{1,3},{2,0},{3,1},{4,6},{5,7},{6,4},{7,5},{8,10},{9,11},{10,... | collective-permute-start | bytes 6291464 | tf_op jit(solution)/shard_map/ppermute | solution.py:20
  123.5 89.4 %collective-permute-start.16 = (f32[256,2048]{1,0:T(8,128)}, f32[256,2048]{1,0:T(8,128)}, u32[]{:S(2)}, u32[]{:S(2)}) collective-permute-start(f32[256,2048]{1,0:T(8,128)} %convolution_add_fusion.2), channel_id=1, source_target_pairs={{0,2},{1,3},{2,0},{3,1},{4,6},{5,7},{6,4},{7,5},{8,10},{9,11},{10,... | collective-permute-start | bytes 6291464 | tf_op jit(solution)/shard_map/ppermute | solution.py:20
  293.0 66.2 %collective-permute-start.24 = (f32[256,2048]{1,0:T(8,128)}, f32[256,2048]{1,0:T(8,128)}, u32[]{:S(2)}, u32[]{:S(2)}) collective-permute-start(f32[256,2048]{1,0:T(8,128)} %convolution_add_fusion.4), channel_id=1, source_target_pairs={{0,1},{1,0},{2,3},{3,2},{4,5},{5,4},{6,7},{7,6},{8,9},{9,8},{10,11... | collective-permute-start | bytes 6291464 | tf_op jit(solution)/shard_map/ppermute | solution.py:20
  298.1 61.9 %collective-permute-start.21 = (f32[256,2048]{1,0:T(8,128)}, f32[256,2048]{1,0:T(8,128)}, u32[]{:S(2)}, u32[]{:S(2)}) collective-permute-start(f32[256,2048]{1,0:T(8,128)} %convolution_add_fusion.6), channel_id=1, source_target_pairs={{0,1},{1,0},{2,3},{3,2},{4,5},{5,4},{6,7},{7,6},{8,9},{9,8},{10,11... | collective-permute-start | bytes 6291464 | tf_op jit(solution)/shard_map/ppermute | solution.py:20
  324.3 92.2 %collective-permute-start.12 = (f32[256,2048]{1,0:T(8,128)}, f32[256,2048]{1,0:T(8,128)}, u32[]{:S(2)}, u32[]{:S(2)}) collective-permute-start(f32[256,2048]{1,0:T(8,128)} %fusion.91), channel_id=1, source_target_pairs={{0,1},{1,0},{2,3},{3,2},{4,5},{5,4},{6,7},{7,6},{8,9},{9,8},{10,11... | collective-permute-start | bytes 6291464 | tf_op jit(solution)/shard_map/ppermute | solution.py:20
  333.9 71.3 %collective-permute-start.77 = (f32[1024,768]{1,0:T(8,128)}, f32[1024,768]{1,0:T(8,128)}, u32[]{:S(2)}, u32[]{:S(2)}) collective-permute-start(f32[1024,768]{1,0:T(8,128)} %fusion.138), channel_id=1, source_target_pairs={{0,4},{4,0},{8,12},{12,8},{16,20},{20,16},{24,28},{28,24},{1,5},{5... | collective-permute-start | bytes 9437192 | tf_op jit(solution)/shard_map/ppermute | solution.py:83
  374.3 260.4 %collective-permute-start.63 = (f32[1024,1408]{1,0:T(8,128)}, f32[1024,1408]{1,0:T(8,128)}, u32[]{:S(2)}, u32[]{:S(2)}) collective-permute-start(f32[1024,1408]{1,0:T(8,128)} %fusion.46), channel_id=1, source_target_pairs={{0,4},{4,0},{8,12},{12,8},{16,20},{20,16},{24,28},{28,24},{1,5},{5... | collective-permute-start | bytes 17301512 | tf_op jit(solution)/shard_map/ppermute | solution.py:83
  434.5 217.1 %collective-permute-start.70 = (f32[1024,1408]{1,0:T(8,128)}, f32[1024,1408]{1,0:T(8,128)}, u32[]{:S(2)}, u32[]{:S(2)}) collective-permute-start(f32[1024,1408]{1,0:T(8,128)} %fusion.45), channel_id=1, source_target_pairs={{0,4},{4,0},{8,12},{12,8},{16,20},{20,16},{24,28},{28,24},{1,5},{5... | collective-permute-start | bytes 17301512 | tf_op jit(solution)/shard_map/ppermute | solution.py:83
  436.6 95.3 %collective-permute-start.19 = (f32[256,2048]{1,0:T(8,128)}, f32[256,2048]{1,0:T(8,128)}, u32[]{:S(2)}, u32[]{:S(2)}) collective-permute-start(f32[256,2048]{1,0:T(8,128)} %convolution_add_fusion.8), channel_id=1, source_target_pairs={{0,2},{1,3},{2,0},{3,1},{4,6},{5,7},{6,4},{7,5},{8,10},{9,11},{10,... | collective-permute-start | bytes 6291464 | tf_op jit(solution)/shard_map/ppermute | solution.py:20
  442.0 133.6 %collective-permute-start.25 = (f32[256,2048]{1,0:T(8,128)}, f32[256,2048]{1,0:T(8,128)}, u32[]{:S(2)}, u32[]{:S(2)}) collective-permute-start(f32[256,2048]{1,0:T(8,128)} %fusion.26), channel_id=1, source_target_pairs={{0,2},{1,3},{2,0},{3,1},{4,6},{5,7},{6,4},{7,5},{8,10},{9,11},{10,... | collective-permute-start | bytes 6291464 | tf_op jit(solution)/shard_map/ppermute | solution.py:20
  486.9 98.9 %collective-permute-start.82 = (f32[256,768]{0,1:T(8,128)S(1)}, f32[256,768]{0,1:T(8,128)S(1)}, u32[]{:S(2)}, u32[]{:S(2)}) collective-permute-start(f32[256,768]{0,1:T(8,128)S(1)} %bitcast_add_fusion.18), channel_id=1, source_target_pairs={{16,8},{20,12},{24,16},{28,20},{17,9},{21,13},{25,17},{29,21},{18,... | collective-permute-start | bytes 2359304 | tf_op jit(solution)/shard_map/ppermute | solution.py:79
  531.9 65.5 %collective-permute-start.86 = (f32[512,640]{1,0:T(8,128)S(1)}, f32[512,640]{1,0:T(8,128)S(1)}, u32[]{:S(2)}, u32[]{:S(2)}) collective-permute-start(f32[512,640]{1,0:T(8,128)S(1)} %copy-done.84), channel_id=1, source_target_pairs={{0,8},{4,12},{8,16},{12,20},{16,24},{20,28},{1,9},{5,13},{9,17},{1... | collective-permute-start | bytes 3932168 | tf_op jit(solution)/shard_map/ppermute | solution.py:79
  619.5 163.1 %collective-permute-start.30 = (f32[2]{0:T(128)}, f32[2]{0:T(128)}, u32[]{:S(2)}, u32[]{:S(2)}) collective-permute-start(f32[2]{0:T(128)} %get-tuple-element.172), channel_id=1, source_target_pairs={{4,0},{8,4},{12,8},{16,12},{20,16},{24,20},{28,24},{5,1},{9,5},{13... | collective-permute-start | bytes 32 | tf_op jit(solution)/shard_map/ppermute | solution.py:26
  634.0 116.3 %collective-permute-start.14 = (f32[256,2048]{1,0:T(8,128)}, f32[256,2048]{1,0:T(8,128)}, u32[]{:S(2)}, u32[]{:S(2)}) collective-permute-start(f32[256,2048]{1,0:T(8,128)} %add.605), channel_id=1, source_target_pairs={{0,1},{1,0},{2,3},{3,2},{4,5},{5,4},{6,7},{7,6},{8,9},{9,8},{10,11... | collective-permute-start | bytes 6291464 | tf_op jit(solution)/shard_map/ppermute | solution.py:20
  667.6 84.1 %collective-permute-start.20 = (f32[256,2048]{1,0:T(8,128)}, f32[256,2048]{1,0:T(8,128)}, u32[]{:S(2)}, u32[]{:S(2)}) collective-permute-start(f32[256,2048]{1,0:T(8,128)} %add.613), channel_id=1, source_target_pairs={{0,1},{1,0},{2,3},{3,2},{4,5},{5,4},{6,7},{7,6},{8,9},{9,8},{10,11... | collective-permute-start | bytes 6291464 | tf_op jit(solution)/shard_map/ppermute | solution.py:20
  671.2 119.0 %collective-permute-start.64 = (f32[256,1408]{1,0:T(8,128)}, f32[256,1408]{1,0:T(8,128)S(1)}, u32[]{:S(2)}, u32[]{:S(2)}) collective-permute-start(f32[256,1408]{1,0:T(8,128)} %get-tuple-element.91), channel_id=1, source_target_pairs={{0,8},{4,12},{1,9},{5,13},{2,10},{6,14},{3,11},{7,15}} | collective-permute-start | bytes 4325384 | tf_op jit(solution)/shard_map/ppermute | solution.py:79
  677.0 164.8 %collective-permute-start.71 = (f32[256,1408]{1,0:T(8,128)}, f32[256,1408]{1,0:T(8,128)}, u32[]{:S(2)}, u32[]{:S(2)}) collective-permute-start(f32[256,1408]{1,0:T(8,128)} %get-tuple-element.87), channel_id=1, source_target_pairs={{0,8},{4,12},{1,9},{5,13},{2,10},{6,14},{3,11},{7,15}} | collective-permute-start | bytes 4325384 | tf_op jit(solution)/shard_map/ppermute | solution.py:79
  761.6 84.8 %collective-permute-start.56 = (f32[1024,512]{1,0:T(8,128)}, f32[1024,512]{1,0:T(8,128)}, u32[]{:S(2)}, u32[]{:S(2)}) collective-permute-start(f32[1024,512]{1,0:T(8,128)} %fusion.69), channel_id=1, source_target_pairs={{0,4},{4,0},{8,12},{12,8},{16,20},{20,16},{24,28},{28,24},{1,5},{5... | collective-permute-start | bytes 6291464 | tf_op jit(solution)/shard_map/ppermute | solution.py:83
  790.2 123.4 %collective-permute-start.67 = (f32[256,1408]{1,0:T(8,128)}, f32[256,1408]{1,0:T(8,128)}, u32[]{:S(2)}, u32[]{:S(2)}) collective-permute-start(f32[256,1408]{1,0:T(8,128)} %get-tuple-element.92), channel_id=1, source_target_pairs={{24,16},{28,20},{25,17},{29,21},{26,18},{30,22},{27,19},{31,23}} | collective-permute-start | bytes 4325384 | tf_op jit(solution)/shard_map/ppermute | solution.py:79
  834.2 79.4 %collective-permute-start.74 = (f32[256,1408]{1,0:T(8,128)}, f32[256,1408]{1,0:T(8,128)}, u32[]{:S(2)}, u32[]{:S(2)}) collective-permute-start(f32[256,1408]{1,0:T(8,128)} %get-tuple-element.88), channel_id=1, source_target_pairs={{24,16},{28,20},{25,17},{29,21},{26,18},{30,22},{27,19},{31,23}} | collective-permute-start | bytes 4325384 | tf_op jit(solution)/shard_map/ppermute | solution.py:79
  836.2 78.0 %collective-permute-start.65 = (f32[256,1408]{1,0:T(8,128)}, f32[256,1408]{1,0:T(8,128)}, u32[]{:S(2)}, u32[]{:S(2)}) collective-permute-start(f32[256,1408]{1,0:T(8,128)} %bitcast_add_fusion.10), channel_id=1, source_target_pairs={{0,8},{4,12},{8,16},{12,20},{1,9},{5,13},{9,17},{13,21},{2,10},{6,... | collective-permute-start | bytes 4325384 | tf_op jit(solution)/shard_map/ppermute | solution.py:79
  846.5 71.7 %collective-permute-start.72 = (f32[256,1408]{1,0:T(8,128)}, f32[256,1408]{1,0:T(8,128)}, u32[]{:S(2)}, u32[]{:S(2)}) collective-permute-start(f32[256,1408]{1,0:T(8,128)} %bitcast_add_fusion.5), channel_id=1, source_target_pairs={{0,8},{4,12},{8,16},{12,20},{1,9},{5,13},{9,17},{13,21},{2,10},{6,... | collective-permute-start | bytes 4325384 | tf_op jit(solution)/shard_map/ppermute | solution.py:79
  913.6 88.9 %collective-permute-start.38 = (f32[256,2048]{1,0:T(8,128)S(1)}, f32[256,2048]{1,0:T(8,128)S(1)}, u32[]{:S(2)}, u32[]{:S(2)}) collective-permute-start(f32[256,2048]{1,0:T(8,128)S(1)} %get-tuple-element.113), channel_id=1, source_target_pairs={{0,1},{1,0},{2,3},{3,2},{4,5},{5,4},{6,7},{7,6},{8,9},{9,8},{10,11... | collective-permute-start | bytes 6291464 | tf_op jit(solution)/shard_map/ppermute | solution.py:20
  913.7 90.2 %collective-permute-start.35 = (f32[256,2048]{1,0:T(8,128)S(1)}, f32[256,2048]{1,0:T(8,128)S(1)}, u32[]{:S(2)}, u32[]{:S(2)}) collective-permute-start(f32[256,2048]{1,0:T(8,128)S(1)} %get-tuple-element.114), channel_id=1, source_target_pairs={{0,1},{1,0},{2,3},{3,2},{4,5},{5,4},{6,7},{7,6},{8,9},{9,8},{10,11... | collective-permute-start | bytes 6291464 | tf_op jit(solution)/shard_map/ppermute | solution.py:20
  918.2 123.2 %collective-permute-start.49 = (f32[1024,640]{1,0:T(8,128)}, f32[1024,640]{1,0:T(8,128)}, u32[]{:S(2)}, u32[]{:S(2)}) collective-permute-start(f32[1024,640]{1,0:T(8,128)} %fusion.101), channel_id=1, source_target_pairs={{0,4},{4,0},{8,12},{12,8},{16,20},{20,16},{24,28},{28,24},{1,5},{5... | collective-permute-start | bytes 7864328 | tf_op jit(solution)/shard_map/ppermute | solution.py:83
  921.2 78.1 %collective-permute-start.68 = (f32[256,1408]{1,0:T(8,128)S(1)}, f32[256,1408]{1,0:T(8,128)S(1)}, u32[]{:S(2)}, u32[]{:S(2)}) collective-permute-start(f32[256,1408]{1,0:T(8,128)S(1)} %get-tuple-element.90), channel_id=1, source_target_pairs={{16,8},{20,12},{24,16},{28,20},{17,9},{21,13},{25,17},{29,21},{18,... | collective-permute-start | bytes 4325384 | tf_op jit(solution)/shard_map/ppermute | solution.py:79
  922.1 71.2 %collective-permute-start.58 = (f32[256,512]{0,1:T(8,128)S(1)}, f32[256,512]{0,1:T(8,128)S(1)}, u32[]{:S(2)}, u32[]{:S(2)}) collective-permute-start(f32[256,512]{0,1:T(8,128)S(1)} %bitcast_add_fusion.31), channel_id=1, source_target_pairs={{0,8},{4,12},{8,16},{12,20},{1,9},{5,13},{9,17},{13,21},{2,10},{6,... | collective-permute-start | bytes 1572872 | tf_op jit(solution)/shard_map/ppermute | solution.py:79
  993.3 82.2 %collective-permute-start.66 = (f32[256,1408]{1,0:T(8,128)}, f32[256,1408]{1,0:T(8,128)}, u32[]{:S(2)}, u32[]{:S(2)}) collective-permute-start(f32[256,1408]{1,0:T(8,128)} %get-tuple-element.89), channel_id=1, source_target_pairs={{0,8},{4,12},{8,16},{12,20},{16,24},{20,28},{1,9},{5,13},{9,17},{1... | collective-permute-start | bytes 4325384 | tf_op jit(solution)/shard_map/ppermute | solution.py:79
  1027.8 64.3 %collective-permute-start.69 = (f32[256,1408]{1,0:T(8,128)}, f32[256,1408]{1,0:T(8,128)S(1)}, u32[]{:S(2)}, u32[]{:S(2)}) collective-permute-start(f32[256,1408]{1,0:T(8,128)} %bitcast_add_fusion.9), channel_id=1, source_target_pairs={{8,0},{12,4},{16,8},{20,12},{24,16},{28,20},{9,1},{13,5},{17,9},{2... | collective-permute-start | bytes 4325384 | tf_op jit(solution)/shard_map/ppermute | solution.py:79
  1041.4 88.7 %collective-permute-start.39 = (f32[256,2048]{1,0:T(8,128)S(1)}, f32[256,2048]{1,0:T(8,128)}, u32[]{:S(2)}, u32[]{:S(2)}) collective-permute-start(f32[256,2048]{1,0:T(8,128)S(1)} %get-tuple-element.111), channel_id=1, source_target_pairs={{0,2},{1,3},{2,0},{3,1},{4,6},{5,7},{6,4},{7,5},{8,10},{9,11},{10,... | collective-permute-start | bytes 6291464 | tf_op jit(solution)/shard_map/ppermute | solution.py:20
  1075.5 106.3 %collective-permute-start.73 = (f32[256,1408]{1,0:T(8,128)}, f32[256,1408]{1,0:T(8,128)}, u32[]{:S(2)}, u32[]{:S(2)}) collective-permute-start(f32[256,1408]{1,0:T(8,128)} %get-tuple-element.85), channel_id=1, source_target_pairs={{0,8},{4,12},{8,16},{12,20},{16,24},{20,28},{1,9},{5,13},{9,17},{1... | collective-permute-start | bytes 4325384 | tf_op jit(solution)/shard_map/ppermute | solution.py:79
  1092.1 103.9 %collective-permute-start.76 = (f32[256,1408]{1,0:T(8,128)}, f32[256,1408]{1,0:T(8,128)}, u32[]{:S(2)}, u32[]{:S(2)}) collective-permute-start(f32[256,1408]{1,0:T(8,128)} %bitcast_add_fusion.4), channel_id=1, source_target_pairs={{8,0},{12,4},{16,8},{20,12},{24,16},{28,20},{9,1},{13,5},{17,9},{2... | collective-permute-start | bytes 4325384 | tf_op jit(solution)/shard_map/ppermute | solution.py:79
  (256 other events, 5491.5 us)

commit v2 on v1

v2 whole, which is shorter than its diff:
```python
import functools
import math

import jax
import jax.numpy as jnp
from jax import lax
from jax.experimental import pallas as pl
from jax.experimental.pallas import tpu as pltpu
from jax.sharding import PartitionSpec as P

FEAT = 16
HEAD_V = 128
EPS = 1e-05
PASSAGE_CEILING = 2000

MAPPED = 160
NORM = MAPPED
META = MAPPED + 16
ROWS = META + 8
FIRST, LAST, CARRIED = META, META + 1, META + 2

LONG = pl.CostEstimate(flops=1 << 39, bytes_accessed=1 << 20, transcendentals=0)


def swap(part, bit):
    count = lax.axis_size("head")
    return lax.ppermute(part, "head", [(k, k ^ bit) for k in range(count)])


def shift(part, by):
    count = lax.axis_size("seq")
    return lax.ppermute(part, "seq", [(k, k + by) for k in range(count) if 0 <= k + by < count])


def dot(left, right):
    return jnp.dot(left, right, preferred_element_type=jnp.float32)


def dot_t(left, right):
    return lax.dot_general(left, right, (((1,), (1,)), ((), ())), preferred_element_type=jnp.float32)


def columns_dot(left, right):
    return lax.dot_general(left, right, (((0,), (0,)), ((), ())), preferred_element_type=jnp.float32)


class Order:
    def __init__(self):
        self.last = None

    def after(self, *values):
        if self.last is not None:
            leaves, tree = jax.tree.flatten(values)
            values = jax.tree.unflatten(tree, lax.optimization_barrier((*leaves, self.last))[:-1])
        return values if len(values) > 1 else values[0]

    def mark(self, value):
        self.last = jax.tree.leaves(value)[0]
        return value

    def run(self, work, *values):
        if len(values) == 1:
            return self.mark(work(self.after(values[0])))
        return self.mark(work(*self.after(*values)))


def features(feats):
    row = lax.broadcasted_iota(jnp.int32, (8, feats.shape[1]), 0)
    parts = [jnp.where(row == 0, 1.0, 0.0), feats * 0.5, feats * feats * (1.0 / math.sqrt(32.0))]
    for k in range(1, 8):
        parts.append(feats * jnp.concatenate([feats[k:], feats[:k]], 0) * 0.25)
    parts.append(feats[:8] * feats[8:] * 0.25)
    return jnp.concatenate(parts, 0)


def features_back(feats, grad):
    total = grad[8:24] * 0.5 + grad[24:40] * feats * (2.0 / math.sqrt(32.0))
    for k in range(1, 8):
        part = grad[24 + 16 * k : 40 + 16 * k] * 0.25
        back = part * feats
        total = total + part * jnp.concatenate([feats[k:], feats[:k]], 0)
        total = total + jnp.concatenate([back[16 - k :], back[: 16 - k]], 0)
    part = grad[152:160] * 0.25
    return total + jnp.concatenate([part * feats[8:], part * feats[:8]], 0)


def low(value):
    return value.astype(jnp.bfloat16)


def dot_general(left, right, a, b):
    return lax.dot_general(left, right, (((a,), (b,)), ((), ())), preferred_element_type=jnp.float32)


def put_state(out_ref, h, mapped, right, weights):
    mapped = low(mapped)
    out_ref[0, h, :MAPPED, :] = dot_general(mapped, right, 1, 0)
    norm = dot_general(weights, mapped, 0, 1)
    out_ref[0, h, NORM : NORM + 8, :] = norm[:, :128]
    out_ref[0, h, NORM + 8 : NORM + 16, :] = jnp.concatenate(
        [norm[:, 128:], jnp.zeros((8, 256 - MAPPED), jnp.float32)], 1
    )


def get_norm(ref, h):
    return low(jnp.concatenate([ref[0, h, NORM : NORM + 8, :], ref[0, h, NORM + 8 : NORM + 16, : MAPPED - 128]], 1))


def transposed(ref):
    return jnp.transpose(ref[0].astype(jnp.float32))


def state_kernel(key_ref, value_ref, row_ref, meta_ref, out_ref):
    heads = key_ref.shape[2] // FEAT
    row = row_ref[0]
    tail = jnp.where(row == row[:, row.shape[1] - 1 :], 1.0, 0.0)
    key_t = transposed(key_ref)
    ones = jnp.ones((key_ref.shape[1], 8), jnp.bfloat16)
    for h in range(heads):
        mapped = features(key_t[FEAT * h : FEAT * (h + 1)]) * tail
        put_state(out_ref, h, mapped, value_ref[0, :, HEAD_V * h : HEAD_V * (h + 1)], ones)
        out_ref[0, h, META:, :] = meta_ref[0]


def seen(row_ref, column_ref):
    row, column = row_ref[0], column_ref[0]
    shape = (column.shape[0], row.shape[1])
    causal = lax.broadcasted_iota(jnp.int32, shape, 0) >= lax.broadcasted_iota(jnp.int32, shape, 1)
    return causal & (column == row)


def forward_kernel(query_ref, key_ref, value_ref, row_ref, column_ref, prior_ref, mixed_ref, ratio_ref, denom_ref):
    heads = key_ref.shape[2] // FEAT
    visible = seen(row_ref, column_ref)
    uses = jnp.where(column_ref[0] == prior_ref[0, 0, LAST : LAST + 1, :1], 1.0, 0.0)
    query_t = transposed(query_ref)
    ones = jnp.ones((key_ref.shape[1], HEAD_V), jnp.bfloat16)
    for h in range(heads):
        narrow, wide = slice(FEAT * h, FEAT * (h + 1)), slice(HEAD_V * h, HEAD_V * (h + 1))
        kernel_dot = dot_general(query_ref[0, :, narrow], key_ref[0, :, narrow], 1, 1) * 0.25
        scores = low(jnp.where(visible, 1.0 + kernel_dot + 0.5 * kernel_dot * kernel_dot, 0.0))
        both = dot(scores, jnp.concatenate([value_ref[0, :, wide], ones], 1))
        mapped = low(features(query_t[narrow]))
        numerator = both[:, :HEAD_V] + uses * dot_general(mapped, low(prior_ref[0, h, :MAPPED, :]), 0, 0)
        denominator = both[:, HEAD_V : HEAD_V + 1] + uses * dot_general(mapped, get_norm(prior_ref, h), 0, 1)[:, :1]
        ratio = numerator / denominator
        mixed_ref[0, :, wide] = low(ratio)
        ratio_ref[0, :, wide] = ratio
        denom_ref[0, :, h : h + 1] = denominator


def numer_back(h, d_mixed_ref, ratio_ref, denom_ref):
    wide = slice(HEAD_V * h, HEAD_V * (h + 1))
    inverse = 1.0 / denom_ref[0, :, h : h + 1]
    d_mixed = d_mixed_ref[0, :, wide]
    d_denom = -jnp.sum(d_mixed * ratio_ref[0, :, wide], 1, keepdims=True) * inverse
    return low(d_mixed * inverse), d_denom


def state_back_kernel(query_ref, d_mixed_ref, ratio_ref, denom_ref, row_ref, prior_ref, meta_ref, out_ref):
    heads = query_ref.shape[2] // FEAT
    uses = jnp.where(row_ref[0] == prior_ref[0, 0, LAST : LAST + 1, :1], 1.0, 0.0)
    query_t = transposed(query_ref)
    for h in range(heads):
        d_numer, d_denom = numer_back(h, d_mixed_ref, ratio_ref, denom_ref)
        mapped = features(query_t[FEAT * h : FEAT * (h + 1)]) * uses
        put_state(out_ref, h, mapped, d_numer, low(jnp.broadcast_to(d_denom, (d_denom.shape[0], 8))))
        out_ref[0, h, META:, :] = meta_ref[0]


def backward_kernel(
    query_ref, key_ref, value_ref, row_ref, column_ref, d_mixed_ref, ratio_ref, denom_ref, prior_ref, later_ref,
    d_query_ref, d_key_ref, d_value_ref,
):
    heads = key_ref.shape[2] // FEAT
    visible = seen(row_ref, column_ref)
    row, column = row_ref[0], column_ref[0]
    uses = jnp.where(row == prior_ref[0, 0, LAST : LAST + 1, :1], 1.0, 0.0)
    end = row.shape[1] - 1
    tail = jnp.where(row == row[:, end:], 1.0, 0.0)
    tail_column = jnp.where(column == row[:, end:], 1.0, 0.0)
    query_t, key_t = transposed(query_ref), transposed(key_ref)
    d_queries, d_keys = [], []
    for h in range(heads):
        narrow, wide = slice(FEAT * h, FEAT * (h + 1)), slice(HEAD_V * h, HEAD_V * (h + 1))
        query, key, value = query_ref[0, :, narrow], key_ref[0, :, narrow], value_ref[0, :, wide]
        d_numer, d_denom = numer_back(h, d_mixed_ref, ratio_ref, denom_ref)
        kernel_dot = dot_general(query, key, 1, 1) * 0.25
        scores = low(jnp.where(visible, 1.0 + kernel_dot + 0.5 * kernel_dot * kernel_dot, 0.0))
        d_scores = low(jnp.where(visible, dot_general(d_numer, value, 1, 1) + d_denom, 0.0))
        d_kernel = low(d_scores.astype(jnp.float32) * (1.0 + kernel_dot))
        d_query = dot_general(key, d_kernel, 0, 1) * 0.25
        d_key = dot_general(query, d_kernel, 0, 0) * 0.25
        d_value = dot_general(scores, d_numer, 0, 0)

        wide_denom = low(jnp.broadcast_to(d_denom, (d_denom.shape[0], 8)))
        mapped_back = dot_general(low(prior_ref[0, h, :MAPPED, :]), d_numer, 1, 1)
        mapped_back = mapped_back + dot_general(get_norm(prior_ref, h), wide_denom, 0, 1) * 0.125
        d_queries.append(d_query + features_back(query_t[narrow], mapped_back * uses))

        later = low(later_ref[0, h, :MAPPED, :])
        mapped_back = dot_general(later, value, 1, 1)
        mapped_back = mapped_back + dot_general(
            get_norm(later_ref, h), jnp.ones((value.shape[0], 8), jnp.bfloat16), 0, 1
        ) * 0.125
        d_keys.append(d_key + features_back(key_t[narrow], mapped_back * tail))
        d_value = d_value + tail_column * dot_general(low(features(key_t[narrow])), later, 0, 0)
        d_value_ref[0, :, wide] = low(d_value)
    d_query_ref[0] = low(jnp.transpose(jnp.concatenate(d_queries, 0)))
    d_key_ref[0] = low(jnp.transpose(jnp.concatenate(d_keys, 0)))


def per_sequence(kernel, out_shapes, *arrays, after=()):
    def spec(shape):
        rest = (0,) * (len(shape) - 1)
        return pl.BlockSpec((1,) + tuple(shape[1:]), lambda s: (s,) + rest)

    def body(*refs):
        kernel(*refs[: len(arrays)], *refs[len(arrays) + len(after) :])

    outs = [jax.ShapeDtypeStruct(shape, dtype) for shape, dtype in out_shapes]
    result = pl.pallas_call(
        body,
        grid=(arrays[0].shape[0],),
        in_specs=[spec(a.shape) for a in arrays] + [pl.BlockSpec(memory_space=pl.ANY) for _ in after],
        out_specs=[spec(o.shape) for o in outs],
        out_shape=outs,
        cost_estimate=LONG,
        compiler_params=pltpu.CompilerParams(vmem_limit_bytes=48 << 20),
    )(*arrays, *after)
    return result if len(outs) > 1 else result[0]


def along_pair(part):
    return lax.ppermute(part, "seq", [(k, k ^ 1) for k in range(lax.axis_size("seq"))])


def along_line(parts):
    groups = [[k for k in range(8) if k % 2 == y] for y in range(2)]
    return lax.psum_scatter(parts, "seq", scatter_dimension=0, axis_index_groups=groups, tiled=True)


def scattered(left, right):
    rows, columns = jnp.concatenate(left, 0), jnp.concatenate(right, 0)
    return lax.psum_scatter(columns_dot(rows, columns), "seq", scatter_dimension=0, tiled=True)


def blocks_dot(left, right, where, span, came=None, after=()):
    parts = len(left)
    block = left[0].shape[1] // lax.axis_size("seq")
    count, width = where.shape[0], span[1] - span[0]

    def kernel(where_ref, *refs):
        lefts, rights, out_ref = refs[:parts], refs[parts : 2 * parts], refs[-1]
        total = refs[2 * parts][...] if came is not None else None
        for left_ref, right_ref in zip(lefts, rights):
            part = dot_general(left_ref[...], right_ref[:, span[0] : span[1]], 0, 0)
            total = part if total is None else total + part
        out_ref[...] = total

    specs = [pl.BlockSpec((l.shape[0], block), lambda k, where: (0, where[k])) for l in left]
    specs += [pl.BlockSpec(r.shape, lambda k, where: (0, 0)) for r in right]
    extra = []
    if came is not None:
        specs.append(pl.BlockSpec((block, width), lambda k, where: (k, 0)))
        extra.append(came)
    specs += [pl.BlockSpec(memory_space=pl.ANY) for _ in after]
    tokens = sum(l.shape[0] for l in left)
    return pl.pallas_call(
        kernel,
        grid_spec=pltpu.PrefetchScalarGridSpec(
            num_scalar_prefetch=1,
            grid=(count,),
            in_specs=specs,
            out_specs=pl.BlockSpec((block, width), lambda k, where: (k, 0)),
        ),
        out_shape=jax.ShapeDtypeStruct((count * block, width), jnp.float32),
        compiler_params=pltpu.CompilerParams(vmem_limit_bytes=40 << 20),
        cost_estimate=LONG,
    )(where, *left, *right, *extra, *after)


def add_after(pair, after):
    rows, width = pair[0].shape

    def kernel(a_ref, b_ref, *refs):
        refs[-1][...] = a_ref[...] + b_ref[...]

    spec = pl.BlockSpec((rows // 4, width), lambda k: (k, 0))
    return pl.pallas_call(
        kernel,
        grid=(4,),
        in_specs=[spec, spec] + [pl.BlockSpec(memory_space=pl.ANY) for _ in after],
        out_specs=spec,
        out_shape=jax.ShapeDtypeStruct((rows, width), jnp.float32),
        cost_estimate=LONG,
    )(*pair, *after)


def dot_after(left, right, after):
    rows, inner = left.shape
    width = right.shape[1]
    tile = width // 4

    def kernel(left_ref, right_ref, *refs):
        refs[-1][...] = dot(left_ref[...], right_ref[...])

    return pl.pallas_call(
        kernel,
        grid=(4,),
        in_specs=[pl.BlockSpec((rows, inner), lambda k: (0, 0)), pl.BlockSpec((inner, tile), lambda k: (0, k))]
        + [pl.BlockSpec(memory_space=pl.ANY) for _ in after],
        out_specs=pl.BlockSpec((rows, tile), lambda k: (0, k)),
        out_shape=jax.ShapeDtypeStruct((rows, width), jnp.float32),
        cost_estimate=LONG,
        compiler_params=pltpu.CompilerParams(vmem_limit_bytes=40 << 20),
    )(left, right, *after)


class PairFirst:
    def __init__(self, left, right, span, after=()):
        self.left, self.right, self.span = left, right, span
        self.sent = self.whole = self.both = right[0]
        self.plain = lax.axis_size("seq") != 8
        if not self.plain:
            y = lax.axis_index("seq") % 2
            self.places = (2 * jnp.arange(4) + y).astype(jnp.int32)
            theirs = (2 * jnp.arange(4) + 1 - y).astype(jnp.int32)
            self.sent = blocks_dot(left, right, theirs, span, after=after)
            self.came = along_pair(self.sent)

    def line(self, after=()):
        if self.plain:
            self.sum = scattered(self.left, [r[:, self.span[0] : self.span[1]] for r in self.right])
            return
        self.whole = blocks_dot(self.left, self.right, self.places, self.span, self.came, after)
        self.sum = along_line(self.whole)


class LineFirst:
    def __init__(self, left, right, span, after=()):
        self.left, self.right, self.span = left, right, span
        self.sent = self.whole = self.both = right[0]
        self.plain = lax.axis_size("seq") != 8
        if not self.plain:
            self.block = left[0].shape[1] // 8
            self.whole = blocks_dot(left, right, jnp.arange(8, dtype=jnp.int32), span, after=after)
            self.both = along_line(self.whole)

    def pair(self):
        if not self.plain:
            y = lax.axis_index("seq") % 2
            low, high = self.both[: self.block], self.both[self.block :]
            self.mine = pick_by(y, low, high)
            self.came = along_pair(pick_by(y, high, low))

    def end(self, after):
        if self.plain:
            self.sum = scattered(self.left, [r[:, self.span[0] : self.span[1]] for r in self.right])
        else:
            self.sum = add_after((self.mine, self.came), after)


def pick_by(bit, zero, one):
    return jnp.where(bit == 0, zero, one)


def rms_norm(values):
    scale = lax.rsqrt(jnp.mean(values * values, -1, keepdims=True) + EPS)
    return values * scale, scale


def rms_back(normed, scale, gain, grad):
    d_normed = grad * gain
    d_values = scale * (d_normed - normed * jnp.mean(d_normed * normed, -1, keepdims=True))
    return (d_values, jnp.sum(grad * normed, 0))


CUTS = (0, 256, 512)


def per_device(
    tokens,
    gain_attn,
    query_weight,
    key_weight,
    value_weight,
    output_weight,
    gain_mlp,
    sigmoid_switch_matrix,
    up_weight,
    down_weight,
    segment_ids,
    cotangent,
):
    seq_count, tok_count, model_width = tokens.shape
    narrow, wide = query_weight.shape[1], value_weight.shape[1]
    head_count = narrow // FEAT
    reach = min(lax.axis_size("seq") - 1, -(-(PASSAGE_CEILING - 1) // tok_count))
    assert reach <= 4
    core = lax.axis_index("head") % 2
    order = Order()
    run = order.run

    segments = segment_ids.astype(jnp.float32) + 1.0
    row, column = segments[:, None, :], segments[:, :, None]
    first, last = segments[:, 0], segments[:, -1]

    def meta(*values):
        at = jnp.arange(8)[None, :, None]
        total = jnp.zeros((seq_count, 8, 128), jnp.float32)
        for k, value in enumerate(values):
            total = jnp.where(at == k, value[:, None, None], total)
        return total

    resid = tokens.astype(jnp.float32)
    h_attn = (rms_norm(resid)[0] * gain_attn).astype(jnp.bfloat16)
    h_rows = h_attn.reshape(-1, model_width)

    def project(h_rows, weight):
        return dot(h_rows, weight).astype(jnp.bfloat16).reshape(seq_count, tok_count, -1)

    key_proj, value_proj = project(h_rows, key_weight), project(h_rows, value_weight)
    payload = ((seq_count, head_count, ROWS, HEAD_V), jnp.float32)
    state = run(
        functools.partial(per_sequence, state_kernel, [payload]), key_proj, value_proj, row, meta(first, last)
    )
    near, far = shift(state, 1), shift(state, 2)
    query_rows = run(project, h_rows, query_weight)
    spans = [slice(a, b) for a, b in zip(CUTS[:-1], CUTS[1:])]
    cots = run(lambda cot: [cot[:, s].reshape(-1, model_width) for s in spans], cotangent)

    def at_row(part, k):
        return part[:, :, k : k + 1, :1]

    index = jnp.arange(ROWS)[None, None, :, None]

    def join_two(near, far, first, last):
        carried_near = (
            (at_row(near, FIRST) == at_row(near, LAST)) & (at_row(near, LAST) == at_row(far, LAST))
        ).astype(jnp.float32)
        first, last = first[:, None, None, None], last[:, None, None, None]
        carried = ((first == last) & (last == at_row(near, LAST))).astype(jnp.float32)
        total = jnp.where(index < META, near + carried_near * far, near)
        return jnp.where(index == CARRIED, carried, total), carried_near, carried

    two, carried_near, carried = run(join_two, near, far, first, last)
    carried = carried[:, 0, 0, 0]

    def join_four(two, four, carried_near):
        return jnp.where(index < META, two + carried_near * at_row(four, CARRIED) * four, two)

    if reach > 2:
        four = shift(two, 2)

    d_hiddens = [run(dot_t, cot, down_weight) for cot in cots]

    prior = run(join_four, two, four, carried_near) if reach > 2 else two
    block = (seq_count, tok_count)
    mixed, ratio, denominator = run(
        functools.partial(
            per_sequence,
            forward_kernel,
            [(block + (wide,), jnp.bfloat16), (block + (wide,), jnp.float32), (block + (head_count,), jnp.float32)],
        ),
        query_rows, key_proj, value_proj, row, column, prior,
    )
    head_size = lax.axis_size("head")

    def exchange(parts):
        groups = [[k, k + 1] for k in range(0, head_size, 2)]
        return lax.all_to_all(parts, "head", 0, 0, axis_index_groups=groups, tiled=True)

    def spread(own):
        return exchange(jnp.stack([own, own]))

    def mine(both):
        return jnp.where(core == 0, both[0], both[1])

    def head_part(work, *values):
        def summed(*values):
            both = exchange(work(*values))
            return both[0] + both[1]

        chip = run(summed, *values)
        bit = 2
        while 2 * bit < head_size:
            chip = chip + swap(chip, bit)
            bit *= 2
        return chip, swap(chip, bit) if bit < head_size else jnp.zeros_like(chip)

    def total(pair):
        return pair[0] + pair[1]

    def joined(parts):
        return jnp.concatenate(parts, 0)

    def flat(part):
        return part.reshape(-1, part.shape[-1])

    def paired(part):
        return part.reshape(seq_count, -1, part.shape[-1])

    def branch_part(mixed, weight):
        return paired(dot(flat(mixed), weight))

    branches = [head_part(branch_part, mixed[:, s], output_weight) for s in spans]

    mids, normeds, scales, h_mlps, hiddens, d_gates, d_ups, d_hs = [], [], [], [], [], [], [], []

    def feed(h_mlp, d_hidden, gate_weight, up_weight):
        gate, up = dot(h_mlp, gate_weight), dot(h_mlp, up_weight)
        sigmoid = jax.nn.sigmoid(gate)
        hidden = (gate * sigmoid * up).astype(jnp.bfloat16)
        d_gate = (d_hidden * up * sigmoid * (1.0 + gate * (1.0 - sigmoid))).astype(jnp.bfloat16)
        d_up = (d_hidden * gate * sigmoid).astype(jnp.bfloat16)
        return hidden, d_gate, d_up

    def feed_back(d_gate, d_up, gate_weight, up_weight):
        return paired(dot_t(d_gate, gate_weight) + dot_t(d_up, up_weight))

    hidden_width = down_weight.shape[0]
    cut_b = (hidden_width * 3 // 11) // 128 * 128
    cut = (hidden_width * 6 // 11) // 128 * 128
    for k, s in enumerate(spans):
        branch = run(lambda pair: spread(total(pair)), branches[k])

        def middle(tokens, branch):
            mid = tokens.astype(jnp.float32) + branch
            normed, scale = rms_norm(mid)
            return mid, mine(normed), mine(scale), flat((normed * gain_mlp).astype(jnp.bfloat16))

        mid, normed, scale, h_mlp = run(middle, tokens[:, s], branch)
        hidden, d_gate, d_up = run(feed, h_mlp, d_hiddens[k], sigmoid_switch_matrix, up_weight)
        for into, value in zip((mids, normeds, scales, h_mlps, hiddens, d_gates, d_ups),
                               (mid, normed, scale, h_mlp, hidden, d_gate, d_up)):
            into.append(value)
        if k == len(spans) - 1:
            down_a = PairFirst(cots, hiddens, (cut_b, hidden_width))
        d_hs.append(head_part(feed_back, d_gate, d_up, sigmoid_switch_matrix, up_weight))

    down_b = LineFirst(cots, hiddens, (0, cut_b), [d_hs[-1][0]])
    gate_a = PairFirst(h_mlps, d_gates, (0, cut), [down_b.whole])

    def out_part(k, after):
        return head_part(lambda hidden, weight: paired(dot_after(hidden, weight, after)), hiddens[k], down_weight)

    d_mids, d_branches, d_mixeds = [], [], []

    def middle_back(k, after):
        def work(d_h, normed, scale):
            d_own, d_gain = rms_back(normed, scale, gain_mlp, d_h)
            return spread(d_own), d_gain

        d_norm, d_gain = run(work, add_after(d_hs[k], after), normeds[k], scales[k])

        def work(d_norm, cot, weight):
            d_mid = cot.astype(jnp.float32) + d_norm
            d_branch = flat(d_mid.astype(jnp.bfloat16))
            return mine(d_mid), d_branch, paired(dot_t(d_branch, weight))

        d_mid, d_branch, d_mixed = run(work, d_norm, cotangent[:, spans[k]], output_weight)
        d_mids.append(d_mid)
        d_branches.append(d_branch)
        d_mixeds.append(d_mixed)
        return d_gain

    results = []

    def outcome(k, pair, after):
        own = add_after(pair, after)
        results.append(run(lambda mid, own: (mid + spread(own)).astype(jnp.bfloat16), mids[k], own))

    d_gain_mlp = middle_back(0, [gate_a.sent])
    out_0 = out_part(0, [d_mixeds[0]])
    d_gain_mlp = d_gain_mlp + middle_back(1, [out_0[0]])

    d_mixed = jnp.concatenate(d_mixeds, 1)
    d_state = run(
        functools.partial(per_sequence, state_back_kernel, [payload]),
        query_rows, d_mixed, ratio, denominator, row, prior, meta(first, last, carried),
    )
    near, far = shift(d_state, -1), shift(d_state, -2)
    down_a.line([d_state])
    outcome(0, out_0, [down_a.whole])
    out_1 = out_part(1, [results[0]])
    gate_b = PairFirst(h_mlps, d_gates, (cut, hidden_width), [out_1[0], down_b.both])
    down_b.pair()
    gate_a.line([gate_b.sent])
    mixed_rows = [flat(mixed[:, s]) for s in spans]

    def join_two_back(near, far, carried):
        total = jnp.where(index < META, near + at_row(near, CARRIED) * far, near)
        return jnp.where(index == CARRIED, carried[:, None, None, None], total), at_row(near, CARRIED)

    two, carried_near = run(join_two_back, near, far, carried)
    if reach > 2:
        four = shift(two, -2)
    up_a = PairFirst(h_mlps, d_ups, (0, cut), [two, gate_a.whole, down_a.sum])
    outcome(1, out_1, [up_a.sent])
    result = run(lambda parts: jnp.concatenate(parts, 1), results)
    later = run(join_four, two, four, carried_near) if reach > 2 else two
    d_query, d_key, d_value = run(
        functools.partial(
            per_sequence,
            backward_kernel,
            [(block + (narrow,), jnp.bfloat16), (block + (narrow,), jnp.bfloat16), (block + (wide,), jnp.bfloat16)],
            after=[results[1]],
        ),
        query_rows, key_proj, value_proj, row, column, d_mixed, ratio, denominator, prior, later,
    )

    def in_back(d_query, d_key, d_value, query_weight, key_weight, value_weight):
        d_query, d_key, d_value = flat(d_query), flat(d_key), flat(d_value)
        return paired(dot_t(d_query, query_weight) + dot_t(d_key, key_weight) + dot_t(d_value, value_weight))

    d_hs = [
        head_part(in_back, d_query[:, s], d_key[:, s], d_value[:, s], query_weight, key_weight, value_weight)
        for s in spans
    ]
    gate_b.line([d_hs[-1][0]])
    up_b = PairFirst(h_mlps, d_ups, (cut, hidden_width), [gate_b.whole, gate_a.sum])
    down_b.end([up_b.sent])
    qkv_right = flat(jnp.concatenate([d_query, d_key, d_value], -1))

    d_tokens = []

    def first_back(k, after):
        def work(d_h, tokens, d_mid):
            normed, scale = rms_norm(mine(tokens).astype(jnp.float32))
            d_own, d_gain = rms_back(normed, scale, gain_attn, d_h)
            return spread(d_own + d_mid), d_gain

        d_part, d_gain = run(work, add_after(d_hs[k], after), tokens[:, spans[k]], d_mids[k])
        d_tokens.append(d_part)
        return d_gain

    d_gain_attn = first_back(0, [down_b.sum])
    up_a.line([d_tokens[0]])
    out = PairFirst(d_branches, mixed_rows, (0, wide), [up_a.whole, gate_b.sum])
    d_gain_attn = d_gain_attn + first_back(1, [out.sent])
    count = lax.axis_size("seq")

    def gain_blocks(d_gain_attn, d_gain_mlp):
        gains = jnp.sum(spread(jnp.stack([d_gain_attn, d_gain_mlp])), 0)
        if count != 8:
            return gains
        y = lax.axis_index("seq") % 2
        blocks = gains.reshape(2, 4, 2, -1).transpose(2, 1, 3, 0)
        return pick_by(y, blocks[0], blocks[1]), pick_by(y, blocks[1], blocks[0])

    gains = run(gain_blocks, d_gain_attn, d_gain_mlp)
    if count == 8:
        gains_came = along_pair(gains[1])
    up_b.line([d_tokens[1]])
    if count == 8:
        gains = run(lambda mine, came, _: (mine + came).reshape(-1, 2), gains[0], gains_came, up_b.whole)
        gains = along_line(gains)
    else:
        gains = lax.psum_scatter(gains, "seq", scatter_dimension=1, tiled=True).T
    qkv = PairFirst([h_rows], [qkv_right], (0, qkv_right.shape[1]), [up_b.whole, up_a.sum])
    out.line([qkv.sent, up_b.sum])
    qkv.line([out.whole, out.sum, gains])
    gains = gains.T
    d_tokens = jnp.concatenate(d_tokens, 1)
    down = jnp.concatenate([down_b.sum, down_a.sum], 1).T
    gate = jnp.concatenate([gate_a.sum, gate_b.sum], 1)
    up = jnp.concatenate([up_a.sum, up_b.sum], 1)
    return (
        result,
        d_tokens,
        gains[0],
        qkv.sum[:, :narrow],
        qkv.sum[:, narrow : 2 * narrow],
        qkv.sum[:, 2 * narrow :],
        out.sum.T,
        gains[1],
        gate,
        up,
        down,
    )


def solution(mesh):
    return jax.shard_map(
        per_device,
        mesh=mesh,
        in_specs=(
            P(None, "seq", None),
            P(),
            P(None, "head"),
            P(None, "head"),
            P(None, "head"),
            P("head", None),
            P(),
            P(None, "head"),
            P(None, "head"),
            P("head", None),
            P(None, "seq"),
            P(None, "seq", None),
        ),
        out_specs=(
            P(None, "seq", None),
            P(None, "seq", None),
            P("seq"),
            P("seq", "head"),
            P("seq", "head"),
            P("seq", "head"),
            P("head", "seq"),
            P("seq"),
            P("seq", "head"),
            P("seq", "head"),
            P("head", "seq"),
        ),
        check_vma=False,
    )
```

time: 1240 us -> 874 us (0.70)
  starting transfers between devices: 329 us -> 57.3 us
  matrix products: 195 us -> 66.5 us
  Pallas kernels: 0 us -> 128 us
  blocking collectives: 0 us -> 114 us
  waiting for transfers between devices: 360 us -> 274 us
  local copies, waits for them, and re-layouts: 191 us -> 122 us
  other arithmetic: 151 us -> 85.1 us
    ppermute x66 -> x15, starting transfers between devices: 315 us -> 41.2 us  [the longest x9 22.9 us: along_pair(): lax.ppermute(part, 'seq', [(k, k ^ 1) for k in range(lax.axis_size('seq'))])]
    pallas_call x0 -> x28, Pallas kernels: none -> 128 us  [the longest x15 67 us: blocks_dot(): pl.pallas_call(kernel, grid_spec=pltpu.PrefetchScalarGridSpec(num_scalar_...]
    all_to_all x0 -> x16, blocking collectives: none -> 114 us  [exchange(): lax.all_to_all(parts, 'head', 0, 0, axis_index_groups=groups, tiled=True)]
    dot_general x42 -> x14, matrix products: 140 us -> 37 us  [dot_t(): lax.dot_general(left, right, (((1,), (1,)), ((), ())), preferred_element_...]
    ppermute x25 -> x8, waiting for transfers between devices: 154 us -> 53.8 us  [swap(): return lax.ppermute(part, 'head', [(k, k ^ bit) for k in range(count)])]
    unnamed x401 -> x414, local copies, waits for them, and re-layouts: 42.3 us -> 103 us
    add x51 -> x12, other arithmetic: 67.5 us -> 10.4 us  [the longest x8 10.4 us: summed(): return both[0] + both[1]]
    reduce_scatter x0 -> x9, waiting for transfers between devices: none -> 53.6 us  [along_line(): lax.psum_scatter(parts, 'seq', scatter_dimension=0, axis_index_groups=gro...]
  transfers between devices with their start and end apart: 91 -> 33, of which waited for: 31 -> 14; matrix products, arithmetic and copies ran while one was open for 36% -> 18% of each run, Pallas kernels for 0% -> 14%
where the time goes in v2:
time: 874 us; the launch traced here: 864 us
  waiting for transfers between devices  274 us (31%)
  Pallas kernels  128 us (15%)
  local copies, waits for them, and re-layouts  122 us (14%)
  blocking collectives  114 us (13%)
  other arithmetic  85.1 us (10%)
  matrix products  66.5 us (8%)
  starting transfers between devices  57.3 us (7%)
  between operations  16.3 us (2%)
    ppermute x9, waiting for transfers between devices, along_pair(): lax.ppermute(part, 'seq', [(k, k ^ 1) for k in range(lax.axis_size('seq'))])  131 us
    all_to_all x16, blocking collectives, exchange(): lax.all_to_all(parts, 'head', 0, 0, axis_index_groups=groups, tiled=True)  114 us
    unnamed x414, local copies, waits for them, and re-layouts  103 us
    pallas_call x15, Pallas kernels, blocks_dot(): pl.pallas_call(kernel, grid_spec=pltpu.PrefetchScalarGridSpec(num_scalar_...  67 us
    ppermute x8, waiting for transfers between devices, swap(): return lax.ppermute(part, 'head', [(k, k ^ bit) for k in range(count)])  53.8 us
    reduce_scatter x9, waiting for transfers between devices, along_line(): lax.psum_scatter(parts, 'seq', scatter_dimension=0, axis_index_groups=gro...  53.6 us
    dot_general x14, matrix products, dot_t(): lax.dot_general(left, right, (((1,), (1,)), ((), ())), preferred_element_...  37 us
    ppermute x6, waiting for transfers between devices, shift(): lax.ppermute(part, 'seq', [(k, k + by) for k in range(count) if 0 <= k +...  36.2 us
  transfers between devices with their start and end apart: 33, of which 14 were waited for; matrix products, arithmetic and copies ran while one was open for 18% of the time, Pallas kernels for 14%

profile of v2, /device:TPU:0, one launch (start us, length us, event | category | flops | bytes accessed | tf_op | source)
XLA Modules:
  0.0 863.7 jit_solution(54169764891763712)
XLA Ops:
  21.3 5.9 collective-permute-start
  78.4 7.1 all_to_all.85
  92.5 7.1 all_to_all.86
  101.4 32.9 %collective-permute-done.3 = f32[256,2048]{1,0:T(8,128)S(1)} collective-permute-done((f32[256,2048]{1,0:T(8,128)S(1)}, f32[256,2048]{1,0:T(8,128)S(1)}, u32[]{:S(2)}, u32[]{:S(2)}) %collective-permute-start.3) | collective-permute-done | bytes 2097184 | tf_op jit(solution)/shard_map/ppermute | solution.py:27
  135.2 7.4 all_to_all.87
  151.2 7.2 multiply_convert_fusion.5
  158.4 6.5 fusion.66
  171.6 7.1 all_to_all.88
  182.7 7.4 all_to_all.89
  211.7 7.5 all_to_all.90
  245.9 14.8 %collective-permute-start.7 = (f32[1024,1024]{1,0:T(8,128)}, f32[1024,1024]{1,0:T(8,128)}, u32[]{:S(2)}, u32[]{:S(2)}) collective-permute-start(f32[1024,1024]{1,0:T(8,128)} %copy-done.85), channel_id=1, source_target_pairs={{0,4},{4,0},{8,12},{12,8},{16,20},{20,16},{24,28},{28,24},{1,5},{5... | collective-permute-start | bytes 12582920 | tf_op jit(solution)/shard_map/ppermute | solution.py:235
  276.3 7.2 all_to_all.91
  292.9 7.1 all_to_all.92
  311.3 7.4 all_to_all.93
  331.7 36.4 %collective-permute-done.7.refs_4_ = f32[1024,1024]{1,0:T(8,128)} collective-permute-done((f32[1024,1024]{1,0:T(8,128)}, f32[1024,1024]{1,0:T(8,128)}, u32[]{:S(2)}, u32[]{:S(2)}) %collective-permute-start.7) | collective-permute-done | bytes 4194336 | tf_op jit(solution)/shard_map/ppermute | solution.py:235
  382.6 7.6 all_to_all.94
  396.7 7.1 all_to_all.95
  406.3 29.2 %collective-permute-done.10 = f32[2,4,184,128]{3,2,1,0:T(8,128)} collective-permute-done((f32[2,4,184,128]{3,2,1,0:T(8,128)}, f32[2,4,184,128]{3,2,1,0:T(8,128)}, u32[]{:S(2)}, u32[]{:S(2)}) %collective-permute-start.10) | collective-permute-done | bytes 753696 | tf_op jit(solution)/shard_map/ppermute | solution.py:32
  479.2 7.6 all_to_all.96
  498.7 11.5 %shard_map.219 = (bf16[2,512,64]{2,1,0:T(8,128)(2,1)S(1)}, bf16[2,512,64]{2,1,0:T(8,128)(2,1)S(1)}, bf16[2,512,512]{2,1,0:T(8,128)(2,1)S(1)}) custom-call(bf16[2,512,64]{2,1,0:T(8,128)(2,1)S(1)} %bitcast.204, bf16[2,512,64]{2,1,0:T(8,128)(2,1)S(1)} %bitcast.201, bf16[2,512,512]{2,1,0:T(8,128)(2,1)S(1)} %bitcast.213, ...), custom_call_target="tpu_custom_call" | custom-call | flops 549755813888 | bytes 1048576 | tf_op jit(solution)/shard_map/pallas_call | solution.py:222
  515.3 7.1 all_to_all.97
  529.6 7.5 all_to_all.98
  561.7 11.8 %collective-permute-done.14.b_ref = f32[256,2048]{1,0:T(8,128)} collective-permute-done((f32[256,2048]{1,0:T(8,128)}, f32[256,2048]{1,0:T(8,128)}, u32[]{:S(2)}, u32[]{:S(2)}) %collective-permute-start.14) | collective-permute-done | bytes 2097184 | tf_op jit(solution)/shard_map/ppermute | solution.py:27
  582.7 8.4 all_to_all.99.refs_5_
  609.0 9.0 %collective-permute-done.17.b_ref = f32[256,2048]{1,0:T(8,128)} collective-permute-done((f32[256,2048]{1,0:T(8,128)}, f32[256,2048]{1,0:T(8,128)}, u32[]{:S(2)}, u32[]{:S(2)}) %collective-permute-start.17) | collective-permute-done | bytes 2097184 | tf_op jit(solution)/shard_map/ppermute | solution.py:27
  628.4 5.8 all-to-all-start.15
  634.3 6.9 collective-permute-done.20.refs_4_
  660.6 40.7 %collective-permute-done.19 = f32[4,256,2]{1,0,2:T(4,128)S(1)} collective-permute-done((f32[4,256,2]{1,0,2:T(4,128)S(1)}, f32[4,256,2]{1,0,2:T(4,128)S(1)}, u32[]{:S(2)}, u32[]{:S(2)}) %collective-permute-start.19) | collective-permute-done | bytes 8224 | tf_op jit(solution)/shard_map/ppermute | solution.py:235
  730.9 10.7 %reduce-scatter.18.cloned.1.call-done.refs_5_ = f32[256,2]{1,0:T(8,128)} async-done(((f32[1024,2]{1,0:T(8,128)}), f32[256,2]{1,0:T(8,128)}) %reduce-scatter.18.cloned.1.call-update) | async-done | bytes 2064 | tf_op jit(solution)/shard_map/reduce_scatter | solution.py:240
  741.6 46.6 %collective-permute-done.21.refs_2_ = f32[1024,640]{1,0:T(8,128)} collective-permute-done((f32[1024,640]{1,0:T(8,128)}, f32[1024,640]{1,0:T(8,128)}, u32[]{:S(2)}, u32[]{:S(2)}) %collective-permute-start.21) | collective-permute-done | bytes 2621472 | tf_op jit(solution)/shard_map/ppermute | solution.py:235
  804.3 8.6 pad_maximum_fusion
  815.8 36.5 %reduce-scatter.26.cloned.1.call-done = f32[256,640]{1,0:T(8,128)} async-done(((f32[1024,640]{1,0:T(8,128)}), f32[256,640]{1,0:T(8,128)}) %reduce-scatter.26.cloned.1.call-update) | async-done | bytes 655376 | tf_op jit(solution)/shard_map/reduce_scatter | solution.py:240
  (636 shorter events, 415.8 us)
Async XLA Ops:
  7.2 433.4 %reduce-scatter.10.cloned.1.call-start = ((), (), s32[]{:S(2)}) async-start(), calls=%async_computation.26 | async-start | bytes 3932160 | tf_op jit(solution)/shard_map/reduce_scatter | solution.py:240
  21.3 21.4 %collective-permute-start = (f32[2,4,184,128]{3,2,1,0:T(8,128)S(1)}, f32[2,4,184,128]{3,2,1,0:T(8,128)}, u32[]{:S(2)}, u32[]{:S(2)}) collective-permute-start(f32[2,4,184,128]{3,2,1,0:T(8,128)S(1)} %shard_map.203), channel_id=1, source_target_pairs={{0,4},{4,8},{8,12},{12,16},{16,20},{20,24},{24,28},{1,5},{5,9},{9,... | collective-permute-start | bytes 2261000 | tf_op jit(solution)/shard_map/ppermute | solution.py:32
  27.2 18.4 %collective-permute-start.1 = (f32[2,4,184,128]{3,2,1,0:T(8,128)S(1)}, f32[2,4,184,128]{3,2,1,0:T(8,128)}, u32[]{:S(2)}, u32[]{:S(2)}) collective-permute-start(f32[2,4,184,128]{3,2,1,0:T(8,128)S(1)} %shard_map.203), channel_id=1, source_target_pairs={{0,8},{4,12},{8,16},{12,20},{16,24},{20,28},{1,9},{5,13},{9,17},{1... | collective-permute-start | bytes 2261000 | tf_op jit(solution)/shard_map/ppermute | solution.py:32
  48.7 19.4 %collective-permute-start.2 = (f32[2,4,184,128]{3,2,1,0:T(8,128)S(1)}, f32[2,4,184,128]{3,2,1,0:T(8,128)S(1)}, u32[]{:S(2)}, u32[]{:S(2)}) collective-permute-start(f32[2,4,184,128]{3,2,1,0:T(8,128)S(1)} %fusion.43), channel_id=1, source_target_pairs={{0,8},{4,12},{8,16},{12,20},{16,24},{20,28},{1,9},{5,13},{9,17},{1... | collective-permute-start | bytes 2261000 | tf_op jit(solution)/shard_map/ppermute | solution.py:32
  85.8 48.5 %collective-permute-start.3 = (f32[256,2048]{1,0:T(8,128)S(1)}, f32[256,2048]{1,0:T(8,128)S(1)}, u32[]{:S(2)}, u32[]{:S(2)}) collective-permute-start(f32[256,2048]{1,0:T(8,128)S(1)} %fusion.34), channel_id=1, source_target_pairs={{0,2},{1,3},{2,0},{3,1},{4,6},{5,7},{6,4},{7,5},{8,10},{9,11},{10,... | collective-permute-start | bytes 6291464 | tf_op jit(solution)/shard_map/ppermute | solution.py:27
  99.8 82.1 %collective-permute-start.5 = (f32[256,2048]{1,0:T(8,128)S(1)}, f32[256,2048]{1,0:T(8,128)S(1)}, u32[]{:S(2)}, u32[]{:S(2)}) collective-permute-start(f32[256,2048]{1,0:T(8,128)S(1)} %fusion.33), channel_id=1, source_target_pairs={{0,2},{1,3},{2,0},{3,1},{4,6},{5,7},{6,4},{7,5},{8,10},{9,11},{10,... | collective-permute-start | bytes 6291464 | tf_op jit(solution)/shard_map/ppermute | solution.py:27
  180.4 87.2 %collective-permute-start.4 = (f32[256,2048]{1,0:T(8,128)}, f32[256,2048]{1,0:T(8,128)}, u32[]{:S(2)}, u32[]{:S(2)}) collective-permute-start(f32[256,2048]{1,0:T(8,128)} %fusion.32.a_ref), channel_id=1, source_target_pairs={{0,2},{1,3},{2,0},{3,1},{4,6},{5,7},{6,4},{7,5},{8,10},{9,11},{10,... | collective-permute-start | bytes 6291464 | tf_op jit(solution)/shard_map/ppermute | solution.py:27
  220.8 81.7 %collective-permute-start.8 = (f32[256,2048]{1,0:T(8,128)}, f32[256,2048]{1,0:T(8,128)}, u32[]{:S(2)}, u32[]{:S(2)}) collective-permute-start(f32[256,2048]{1,0:T(8,128)} %fusion.31.refs_4_.a_ref), channel_id=1, source_target_pairs={{0,2},{1,3},{2,0},{3,1},{4,6},{5,7},{6,4},{7,5},{8,10},{9,11},{10,... | collective-permute-start | bytes 6291464 | tf_op jit(solution)/shard_map/ppermute | solution.py:27
  245.8 214.3 %reduce-scatter.12.cloned.1.call-start = ((), (), s32[]{:S(2)}) async-start(), calls=%async_computation.27 | async-start | bytes 5242880 | tf_op jit(solution)/shard_map/reduce_scatter | solution.py:240
  245.9 122.2 %collective-permute-start.7 = (f32[1024,1024]{1,0:T(8,128)}, f32[1024,1024]{1,0:T(8,128)}, u32[]{:S(2)}, u32[]{:S(2)}) collective-permute-start(f32[1024,1024]{1,0:T(8,128)} %copy-done.85), channel_id=1, source_target_pairs={{0,4},{4,0},{8,12},{12,8},{16,20},{20,16},{24,28},{28,24},{1,5},{5... | collective-permute-start | bytes 12582920 | tf_op jit(solution)/shard_map/ppermute | solution.py:235
  260.7 192.7 %collective-permute-start.12 = (f32[1024,768]{1,0:T(8,128)}, f32[1024,768]{1,0:T(8,128)}, u32[]{:S(2)}, u32[]{:S(2)}) collective-permute-start(f32[1024,768]{1,0:T(8,128)} %copy-done.86), channel_id=1, source_target_pairs={{0,4},{4,0},{8,12},{12,8},{16,20},{20,16},{24,28},{28,24},{1,5},{5... | collective-permute-start | bytes 9437192 | tf_op jit(solution)/shard_map/ppermute | solution.py:235
  301.6 74.2 %collective-permute-start.6 = (f32[256,2048]{1,0:T(8,128)}, f32[256,2048]{1,0:T(8,128)}, u32[]{:S(2)}, u32[]{:S(2)}) collective-permute-start(f32[256,2048]{1,0:T(8,128)} %fusion.28.refs_0_.a_ref), channel_id=1, source_target_pairs={{0,2},{1,3},{2,0},{3,1},{4,6},{5,7},{6,4},{7,5},{8,10},{9,11},{10,... | collective-permute-start | bytes 6291464 | tf_op jit(solution)/shard_map/ppermute | solution.py:27
  329.2 106.3 %collective-permute-start.10 = (f32[2,4,184,128]{3,2,1,0:T(8,128)}, f32[2,4,184,128]{3,2,1,0:T(8,128)}, u32[]{:S(2)}, u32[]{:S(2)}) collective-permute-start(f32[2,4,184,128]{3,2,1,0:T(8,128)} %shard_map.211.refs_5_), channel_id=1, source_target_pairs={{4,0},{8,4},{12,8},{16,12},{20,16},{24,20},{28,24},{5,1},{9,5},{13... | collective-permute-start | bytes 2261000 | tf_op jit(solution)/shard_map/ppermute | solution.py:32
  330.4 105.0 %collective-permute-start.11 = (f32[2,4,184,128]{3,2,1,0:T(8,128)}, f32[2,4,184,128]{3,2,1,0:T(8,128)}, u32[]{:S(2)}, u32[]{:S(2)}) collective-permute-start(f32[2,4,184,128]{3,2,1,0:T(8,128)} %shard_map.211.refs_5_), channel_id=1, source_target_pairs={{8,0},{12,4},{16,8},{20,12},{24,16},{28,20},{9,1},{13,5},{17,9},{2... | collective-permute-start | bytes 2261000 | tf_op jit(solution)/shard_map/ppermute | solution.py:32
  375.8 171.2 %reduce-scatter.14.cloned.1.call-start = ((), (), s32[]{:S(2)}) async-start(), calls=%async_computation.28 | async-start | bytes 3932160 | tf_op jit(solution)/shard_map/reduce_scatter | solution.py:240
  405.6 67.0 %collective-permute-start.9 = (f32[256,2048]{1,0:T(8,128)}, f32[256,2048]{1,0:T(8,128)}, u32[]{:S(2)}, u32[]{:S(2)}) collective-permute-start(f32[256,2048]{1,0:T(8,128)} %fusion.25.refs_4_.a_ref), channel_id=1, source_target_pairs={{0,2},{1,3},{2,0},{3,1},{4,6},{5,7},{6,4},{7,5},{8,10},{9,11},{10,... | collective-permute-start | bytes 6291464 | tf_op jit(solution)/shard_map/ppermute | solution.py:27
  439.3 50.7 %collective-permute-start.13 = (f32[2,4,184,128]{3,2,1,0:T(8,128)}, f32[2,4,184,128]{3,2,1,0:T(8,128)}, u32[]{:S(2)}, u32[]{:S(2)}) collective-permute-start(f32[2,4,184,128]{3,2,1,0:T(8,128)} %fusion.44.refs_4_), channel_id=1, source_target_pairs={{8,0},{12,4},{16,8},{20,12},{24,16},{28,20},{9,1},{13,5},{17,9},{2... | collective-permute-start | bytes 2261000 | tf_op jit(solution)/shard_map/ppermute | solution.py:32
  450.4 88.4 %collective-permute-start.16 = (f32[1024,640]{1,0:T(8,128)}, f32[1024,640]{1,0:T(8,128)}, u32[]{:S(2)}, u32[]{:S(2)}) collective-permute-start(f32[1024,640]{1,0:T(8,128)} %shard_map.215.refs_5_), channel_id=1, source_target_pairs={{0,4},{4,0},{8,12},{12,8},{16,20},{20,16},{24,28},{28,24},{1,5},{5... | collective-permute-start | bytes 7864328 | tf_op jit(solution)/shard_map/ppermute | solution.py:235
  451.4 107.1 %collective-permute-start.15 = (f32[256,384]{1,0:T(8,128)}, f32[256,384]{1,0:T(8,128)}, u32[]{:S(2)}, u32[]{:S(2)}) collective-permute-start(f32[256,384]{1,0:T(8,128)} %get-tuple-element.334), channel_id=1, source_target_pairs={{0,4},{4,0},{8,12},{12,8},{16,20},{20,16},{24,28},{28,24},{1,5},{5... | collective-permute-start | bytes 1179656 | tf_op jit(solution)/shard_map/ppermute | solution.py:235
  460.1 140.6 %reduce-scatter.16.cloned.1.call-start = ((), (), s32[]{:S(2)}) async-start(), calls=%async_computation.29 | async-start | bytes 3276800 | tf_op jit(solution)/shard_map/reduce_scatter | solution.py:240
  470.1 121.0 %collective-permute-start.18 = (f32[1024,768]{1,0:T(8,128)}, f32[1024,768]{1,0:T(8,128)}, u32[]{:S(2)}, u32[]{:S(2)}) collective-permute-start(f32[1024,768]{1,0:T(8,128)} %shard_map.217.refs_0_), channel_id=1, source_target_pairs={{0,4},{4,0},{8,12},{12,8},{16,20},{20,16},{24,28},{28,24},{1,5},{5... | collective-permute-start | bytes 9437192 | tf_op jit(solution)/shard_map/ppermute | solution.py:235
  524.0 49.6 %collective-permute-start.14 = (f32[256,2048]{1,0:T(8,128)}, f32[256,2048]{1,0:T(8,128)}, u32[]{:S(2)}, u32[]{:S(2)}) collective-permute-start(f32[256,2048]{1,0:T(8,128)} %fusion.24.a_ref), channel_id=1, source_target_pairs={{0,2},{1,3},{2,0},{3,1},{4,6},{5,7},{6,4},{7,5},{8,10},{9,11},{10,... | collective-permute-start | bytes 6291464 | tf_op jit(solution)/shard_map/ppermute | solution.py:27
  538.8 79.3 %collective-permute-start.17 = (f32[256,2048]{1,0:T(8,128)}, f32[256,2048]{1,0:T(8,128)}, u32[]{:S(2)}, u32[]{:S(2)}) collective-permute-start(f32[256,2048]{1,0:T(8,128)} %fusion.23.refs_5_.a_ref), channel_id=1, source_target_pairs={{0,2},{1,3},{2,0},{3,1},{4,6},{5,7},{6,4},{7,5},{8,10},{9,11},{10,... | collective-permute-start | bytes 6291464 | tf_op jit(solution)/shard_map/ppermute | solution.py:27
  546.9 155.5 %reduce-scatter.20.cloned.1.call-start = ((), (), s32[]{:S(2)}) async-start(), calls=%async_computation.31 | async-start | bytes 3932160 | tf_op jit(solution)/shard_map/reduce_scatter | solution.py:240
  558.5 82.6 %collective-permute-start.20 = (f32[1024,640]{1,0:T(8,128)}, f32[1024,640]{1,0:T(8,128)}, u32[]{:S(2)}, u32[]{:S(2)}) collective-permute-start(f32[1024,640]{1,0:T(8,128)} %shard_map.221.refs_0_), channel_id=1, source_target_pairs={{0,4},{4,0},{8,12},{12,8},{16,20},{20,16},{24,28},{28,24},{1,5},{5... | collective-permute-start | bytes 7864328 | tf_op jit(solution)/shard_map/ppermute | solution.py:235
  634.2 83.1 %reduce-scatter.22.cloned.1.call-start = ((), (), s32[]{:S(2)}) async-start(), calls=%async_computation.32 | async-start | bytes 3276800 | tf_op jit(solution)/shard_map/reduce_scatter | solution.py:240
  651.9 89.6 %reduce-scatter.18.cloned.1.call-start = ((), (), s32[]{:S(2)}) async-start(), calls=%async_computation.30 | async-start | bytes 655360 | tf_op jit(solution)/shard_map/reduce_scatter | solution.py:240
  654.6 59.1 %collective-permute-start.22 = (f32[1024,512]{1,0:T(8,128)}, f32[1024,512]{1,0:T(8,128)}, u32[]{:S(2)}, u32[]{:S(2)}) collective-permute-start(f32[1024,512]{1,0:T(8,128)} %shard_map.225.refs_0_), channel_id=1, source_target_pairs={{0,4},{4,0},{8,12},{12,8},{16,20},{20,16},{24,28},{28,24},{1,5},{5... | collective-permute-start | bytes 6291464 | tf_op jit(solution)/shard_map/ppermute | solution.py:235
  658.8 42.5 %collective-permute-start.19 = (f32[4,256,2]{1,0,2:T(4,128)S(1)}, f32[4,256,2]{1,0,2:T(4,128)S(1)}, u32[]{:S(2)}, u32[]{:S(2)}) collective-permute-start(f32[4,256,2]{1,0,2:T(4,128)S(1)} %bitcast.230), channel_id=1, source_target_pairs={{0,4},{4,0},{8,12},{12,8},{16,20},{20,16},{24,28},{28,24},{1,5},{5... | collective-permute-start | bytes 24584 | tf_op jit(solution)/shard_map/ppermute | solution.py:235
  702.3 85.9 %reduce-scatter.24.cloned.1.call-start = ((), (), s32[]{:S(2)}) async-start(), calls=%async_computation.33 | async-start | bytes 2621440 | tf_op jit(solution)/shard_map/reduce_scatter | solution.py:240
  729.0 123.3 %reduce-scatter.26.cloned.1.call-start = ((), (), s32[]{:S(2)}) async-start(), calls=%async_computation.34 | async-start | bytes 3276800 | tf_op jit(solution)/shard_map/reduce_scatter | solution.py:240
  729.4 58.8 %collective-permute-start.21 = (f32[1024,640]{1,0:T(8,128)}, f32[1024,640]{1,0:T(8,128)}, u32[]{:S(2)}, u32[]{:S(2)}) collective-permute-start(f32[1024,640]{1,0:T(8,128)} %copy-done.87), channel_id=1, source_target_pairs={{0,4},{4,0},{8,12},{12,8},{16,20},{20,16},{24,28},{28,24},{1,5},{5... | collective-permute-start | bytes 7864328 | tf_op jit(solution)/shard_map/ppermute | solution.py:235
  (205 other events, 1684.3 us)
Sparse Core Ops, SparseCore 0:
  245.9 74.9 reduce-scatter.9
  375.9 83.1 reduce-scatter.11
  461.6 66.7 reduce-scatter.13
  547.0 53.5 reduce-scatter.15
  602.9 59.9 reduce-scatter.19
  665.1 52.0 reduce-scatter.21
  720.2 21.3 reduce-scatter.17
  744.0 41.9 reduce-scatter.23
  800.2 52.0 reduce-scatter.25

commit v3 on v2

--- a/solution.py
+++ b/solution.py
@@ -17,7 +17,7 @@
 NORM = MAPPED
 META = MAPPED + 16
 ROWS = META + 8
-FIRST, LAST, CARRIED = META, META + 1, META + 2
+FIRST, LAST, CARRIED, NEXT = META, META + 1, META + 2, META + 3
 
 LONG = pl.CostEstimate(flops=1 << 39, bytes_accessed=1 << 20, transcendentals=0)
 
@@ -102,8 +102,11 @@
     )
 
 
-def get_norm(ref, h):
-    return low(jnp.concatenate([ref[0, h, NORM : NORM + 8, :], ref[0, h, NORM + 8 : NORM + 16, : MAPPED - 128]], 1))
+def get_state(refs, h):
+    two, four = refs
+    joined = two[0, h] + two[0, h, NEXT : NEXT + 1, :1] * four[0, h, CARRIED : CARRIED + 1, :1] * four[0, h]
+    norm = jnp.concatenate([joined[NORM : NORM + 8], joined[NORM + 8 : NORM + 16, : MAPPED - 128]], 1)
+    return low(joined[:MAPPED]), low(norm)
 
 
 def transposed(ref):
@@ -129,7 +132,9 @@
     return causal & (column == row)
 
 
-def forward_kernel(query_ref, key_ref, value_ref, row_ref, column_ref, prior_ref, mixed_ref, ratio_ref, denom_ref):
+def forward_kernel(
+    query_ref, key_ref, value_ref, row_ref, column_ref, prior_ref, prior_four_ref, mixed_ref, ratio_ref, denom_ref
+):
     heads = key_ref.shape[2] // FEAT
     visible = seen(row_ref, column_ref)
     uses = jnp.where(column_ref[0] == prior_ref[0, 0, LAST : LAST + 1, :1], 1.0, 0.0)
@@ -141,8 +146,9 @@
         scores = low(jnp.where(visible, 1.0 + kernel_dot + 0.5 * kernel_dot * kernel_dot, 0.0))
         both = dot(scores, jnp.concatenate([value_ref[0, :, wide], ones], 1))
         mapped = low(features(query_t[narrow]))
-        numerator = both[:, :HEAD_V] + uses * dot_general(mapped, low(prior_ref[0, h, :MAPPED, :]), 0, 0)
-        denominator = both[:, HEAD_V : HEAD_V + 1] + uses * dot_general(mapped, get_norm(prior_ref, h), 0, 1)[:, :1]
+        state, norm = get_state((prior_ref, prior_four_ref), h)
+        numerator = both[:, :HEAD_V] + uses * dot_general(mapped, state, 0, 0)
+        denominator = both[:, HEAD_V : HEAD_V + 1] + uses * dot_general(mapped, norm, 0, 1)[:, :1]
         ratio = numerator / denominator
         mixed_ref[0, :, wide] = low(ratio)
         ratio_ref[0, :, wide] = ratio
@@ -168,9 +174,18 @@
         out_ref[0, h, META:, :] = meta_ref[0]
 
 
+def join_back_kernel(near_ref, far_ref, carried_ref, out_ref):
+    for h in range(near_ref.shape[1]):
+        near, far = near_ref[0, h], far_ref[0, h]
+        at = lax.broadcasted_iota(jnp.int32, near.shape, 0)
+        total = jnp.where(at < META, near + near[CARRIED : CARRIED + 1, :1] * far, near)
+        total = jnp.where(at == NEXT, near[CARRIED : CARRIED + 1, :1], total)
+        out_ref[0, h] = jnp.where(at == CARRIED, carried_ref[0], total)
+
+
 def backward_kernel(
-    query_ref, key_ref, value_ref, row_ref, column_ref, d_mixed_ref, ratio_ref, denom_ref, prior_ref, later_ref,
-    d_query_ref, d_key_ref, d_value_ref,
+    query_ref, key_ref, value_ref, row_ref, column_ref, d_mixed_ref, ratio_ref, denom_ref, prior_ref, prior_four_ref,
+    later_ref, later_four_ref, d_query_ref, d_key_ref, d_value_ref,
 ):
     heads = key_ref.shape[2] // FEAT
     visible = seen(row_ref, column_ref)
@@ -194,15 +209,14 @@
         d_value = dot_general(scores, d_numer, 0, 0)
 
         wide_denom = low(jnp.broadcast_to(d_denom, (d_denom.shape[0], 8)))
-        mapped_back = dot_general(low(prior_ref[0, h, :MAPPED, :]), d_numer, 1, 1)
-        mapped_back = mapped_back + dot_general(get_norm(prior_ref, h), wide_denom, 0, 1) * 0.125
+        state, norm = get_state((prior_ref, prior_four_ref), h)
+        mapped_back = dot_general(state, d_numer, 1, 1)
+        mapped_back = mapped_back + dot_general(norm, wide_denom, 0, 1) * 0.125
         d_queries.append(d_query + features_back(query_t[narrow], mapped_back * uses))
 
-        later = low(later_ref[0, h, :MAPPED, :])
+        later, norm = get_state((later_ref, later_four_ref), h)
         mapped_back = dot_general(later, value, 1, 1)
-        mapped_back = mapped_back + dot_general(
-            get_norm(later_ref, h), jnp.ones((value.shape[0], 8), jnp.bfloat16), 0, 1
-        ) * 0.125
+        mapped_back = mapped_back + dot_general(norm, jnp.ones((value.shape[0], 8), jnp.bfloat16), 0, 1) * 0.125
         d_keys.append(d_key + features_back(key_t[narrow], mapped_back * tail))
         d_value = d_value + tail_column * dot_general(low(features(key_t[narrow])), later, 0, 0)
         d_value_ref[0, :, wide] = low(d_value)
@@ -245,27 +259,45 @@
     return lax.psum_scatter(columns_dot(rows, columns), "seq", scatter_dimension=0, tiled=True)
 
 
-def blocks_dot(left, right, where, span, came=None, after=()):
-    parts = len(left)
-    block = left[0].shape[1] // lax.axis_size("seq")
+def named(k, where):
+    return 0, where[k]
+
+
+def blocks_dot(terms, where, span, came=None, after=()):
+    parts = len(terms)
+    block = terms[0][0].shape[1] // lax.axis_size("seq")
     count, width = where.shape[0], span[1] - span[0]
 
+    wide = [t[3].dtype != jnp.bfloat16 for t in terms]
+    scratch = [pltpu.VMEM((t[3].shape[0], width), jnp.bfloat16) for t, w in zip(terms, wide) if w]
+
     def kernel(where_ref, *refs):
-        lefts, rights, out_ref = refs[:parts], refs[parts : 2 * parts], refs[-1]
+        lefts, rights = refs[:parts], refs[parts : 2 * parts]
+        out_ref, narrow = refs[len(refs) - 1 - len(scratch)], list(refs[len(refs) - len(scratch) :])
         total = refs[2 * parts][...] if came is not None else None
-        for left_ref, right_ref in zip(lefts, rights):
-            part = dot_general(left_ref[...], right_ref[:, span[0] : span[1]], 0, 0)
+        for n in range(parts):
+            left_ref, columns = lefts[n], slice(*terms[n][4])
+            if wide[n]:
+                kept_ref = narrow.pop(0)
+
+                @pl.when(pl.program_id(0) == 0)
+                def _():
+                    kept_ref[...] = low(rights[n][:, columns])
+
+                right = kept_ref[...]
+            else:
+                right = rights[n][:, columns]
+            part = dot_general(low(left_ref[...]), right, 0, 0)
             total = part if total is None else total + part
         out_ref[...] = total
 
-    specs = [pl.BlockSpec((l.shape[0], block), lambda k, where: (0, where[k])) for l in left]
-    specs += [pl.BlockSpec(r.shape, lambda k, where: (0, 0)) for r in right]
+    specs = [pl.BlockSpec((rows, block), at) for _, rows, at, _, _ in terms]
+    specs += [pl.BlockSpec(right.shape, lambda k, where: (0, 0)) for _, _, _, right, _ in terms]
     extra = []
     if came is not None:
         specs.append(pl.BlockSpec((block, width), lambda k, where: (k, 0)))
         extra.append(came)
     specs += [pl.BlockSpec(memory_space=pl.ANY) for _ in after]
-    tokens = sum(l.shape[0] for l in left)
     return pl.pallas_call(
         kernel,
         grid_spec=pltpu.PrefetchScalarGridSpec(
@@ -273,28 +305,76 @@
             grid=(count,),
             in_specs=specs,
             out_specs=pl.BlockSpec((block, width), lambda k, where: (k, 0)),
+            scratch_shapes=scratch,
         ),
         out_shape=jax.ShapeDtypeStruct((count * block, width), jnp.float32),
-        compiler_params=pltpu.CompilerParams(vmem_limit_bytes=40 << 20),
+        compiler_params=pltpu.CompilerParams(vmem_limit_bytes=44 << 20),
         cost_estimate=LONG,
-    )(where, *left, *right, *extra, *after)
+    )(where, *[t[0] for t in terms], *[t[3] for t in terms], *extra, *after)
+
+
+def own_terms(left, right, span):
+    return [(l, l.shape[0], named, r, span) for l, r in zip(left, right)]
+
+
+def pair_places(y):
+    return (2 * jnp.arange(4) + y).astype(jnp.int32)
+
+
+def picked_columns(chunks, where, after=()):
+    block = chunks[0].shape[1] // 8
+    rows = [c.shape[0] for c in chunks]
+
+    def kernel(where_ref, *refs):
+        at = 0
+        for ref, count in zip(refs, rows):
+            refs[-1][at : at + count] = ref[...].astype(jnp.float32)
+            at += count
+
+    return pl.pallas_call(
+        kernel,
+        grid_spec=pltpu.PrefetchScalarGridSpec(
+            num_scalar_prefetch=1,
+            grid=(where.shape[0],),
+            in_specs=[pl.BlockSpec((count, block), named) for count in rows]
+            + [pl.BlockSpec(memory_space=pl.ANY) for _ in after],
+            out_specs=pl.BlockSpec((sum(rows), block), lambda k, where: (0, k)),
+        ),
+        out_shape=jax.ShapeDtypeStruct((sum(rows), where.shape[0] * block), jnp.float32),
+        cost_estimate=LONG,
+    )(where, *chunks, *after)
 
 
 def add_after(pair, after):
     rows, width = pair[0].shape
+    steps = 4 if rows % 32 == 0 else 1
 
     def kernel(a_ref, b_ref, *refs):
         refs[-1][...] = a_ref[...] + b_ref[...]
 
-    spec = pl.BlockSpec((rows // 4, width), lambda k: (k, 0))
+    spec = pl.BlockSpec((rows // steps, width), lambda k: (k, 0))
     return pl.pallas_call(
         kernel,
-        grid=(4,),
+        grid=(steps,),
         in_specs=[spec, spec] + [pl.BlockSpec(memory_space=pl.ANY) for _ in after],
         out_specs=spec,
         out_shape=jax.ShapeDtypeStruct((rows, width), jnp.float32),
         cost_estimate=LONG,
     )(*pair, *after)
+
+
+def transposed_after(value, after):
+    def kernel(in_ref, *refs):
+        refs[-1][...] = jnp.transpose(in_ref[...])
+
+    return pl.pallas_call(
+        kernel,
+        grid=(1,),
+        in_specs=[pl.BlockSpec(value.shape, lambda k: (0, 0))] + [pl.BlockSpec(memory_space=pl.ANY) for _ in after],
+        out_specs=pl.BlockSpec(value.shape[::-1], lambda k: (0, 0)),
+        out_shape=jax.ShapeDtypeStruct(value.shape[::-1], value.dtype),
+        cost_estimate=LONG,
+    )(value, *after)
 
 
 def dot_after(left, right, after):
@@ -317,6 +397,26 @@
     )(left, right, *after)
 
 
+def dots_after(lefts, rights, after):
+    rows, width, count = lefts[0].shape[0], rights[0].shape[0], len(lefts)
+    tile = width // 4
+
+    def kernel(*refs):
+        refs[-1][...] = sum(dot_t(refs[k][...], refs[count + k][...]) for k in range(count))
+
+    return pl.pallas_call(
+        kernel,
+        grid=(4,),
+        in_specs=[pl.BlockSpec(left.shape, lambda k: (0, 0)) for left in lefts]
+        + [pl.BlockSpec((tile, right.shape[1]), lambda k: (k, 0)) for right in rights]
+        + [pl.BlockSpec(memory_space=pl.ANY) for _ in after],
+        out_specs=pl.BlockSpec((rows, tile), lambda k: (0, k)),
+        out_shape=jax.ShapeDtypeStruct((rows, width), jnp.float32),
+        cost_estimate=LONG,
+        compiler_params=pltpu.CompilerParams(vmem_limit_bytes=40 << 20),
+    )(*lefts, *rights, *after)
+
+
 class PairFirst:
     def __init__(self, left, right, span, after=()):
         self.left, self.right, self.span = left, right, span
@@ -324,16 +424,42 @@
         self.plain = lax.axis_size("seq") != 8
         if not self.plain:
             y = lax.axis_index("seq") % 2
-            self.places = (2 * jnp.arange(4) + y).astype(jnp.int32)
-            theirs = (2 * jnp.arange(4) + 1 - y).astype(jnp.int32)
-            self.sent = blocks_dot(left, right, theirs, span, after=after)
+            self.places = pair_places(y)
+            self.sent = blocks_dot(own_terms(left, right, span), pair_places(1 - y), span, after=after)
             self.came = along_pair(self.sent)
 
     def line(self, after=()):
         if self.plain:
             self.sum = scattered(self.left, [r[:, self.span[0] : self.span[1]] for r in self.right])
             return
-        self.whole = blocks_dot(self.left, self.right, self.places, self.span, self.came, after)
+        self.whole = blocks_dot(own_terms(self.left, self.right, self.span), self.places, self.span, self.came, after)
+        self.sum = along_line(self.whole)
+
+
+class FactorsFirst:
+    def __init__(self, left, span, after=()):
+        self.left, self.span, self.right, self.came = left, span, [], []
+        self.left_came = self.whole = self.sent = left[0]
+        self.plain = lax.axis_size("seq") != 8
+        if not self.plain:
+            y = lax.axis_index("seq") % 2
+            self.places = pair_places(y)
+            self.left_came = along_pair(picked_columns(left, pair_places(1 - y), after))
+
+    def add(self, right):
+        self.right.append(right)
+        if not self.plain:
+            self.sent = right[:, self.span[0] : self.span[1]].astype(jnp.float32)
+            self.came.append(along_pair(self.sent))
+
+    def line(self, after=()):
+        if self.plain:
+            self.sum = scattered(self.left, [r[:, self.span[0] : self.span[1]] for r in self.right])
+            return
+        terms, width = own_terms(self.left, self.right, self.span), self.span[1] - self.span[0]
+        for n, came in enumerate(self.came):
+            terms.append((self.left_came, came.shape[0], lambda k, where, n=n: (n, k), came, (0, width)))
+        self.whole = blocks_dot(terms, self.places, self.span, after=after)
         self.sum = along_line(self.whole)
 
 
@@ -344,21 +470,20 @@
         self.plain = lax.axis_size("seq") != 8
         if not self.plain:
             self.block = left[0].shape[1] // 8
-            self.whole = blocks_dot(left, right, jnp.arange(8, dtype=jnp.int32), span, after=after)
+            y = lax.axis_index("seq") % 2
+            both = 2 * jnp.arange(4)[:, None] + jnp.stack([y, 1 - y])[None, :]
+            self.whole = blocks_dot(own_terms(left, right, span), both.reshape(8).astype(jnp.int32), span, after=after)
             self.both = along_line(self.whole)
 
     def pair(self):
         if not self.plain:
-            y = lax.axis_index("seq") % 2
-            low, high = self.both[: self.block], self.both[self.block :]
-            self.mine = pick_by(y, low, high)
-            self.came = along_pair(pick_by(y, high, low))
+            self.came = along_pair(self.both[self.block :])
 
     def end(self, after):
         if self.plain:
             self.sum = scattered(self.left, [r[:, self.span[0] : self.span[1]] for r in self.right])
         else:
-            self.sum = add_after((self.mine, self.came), after)
+            self.sum = add_after((self.both[: self.block], self.came), after)
 
 
 def pick_by(bit, zero, one):
@@ -442,20 +567,20 @@
         first, last = first[:, None, None, None], last[:, None, None, None]
         carried = ((first == last) & (last == at_row(near, LAST))).astype(jnp.float32)
         total = jnp.where(index < META, near + carried_near * far, near)
-        return jnp.where(index == CARRIED, carried, total), carried_near, carried
-
-    two, carried_near, carried = run(join_two, near, far, first, last)
+        total = jnp.where(index == NEXT, carried_near, total)
+        return jnp.where(index == CARRIED, carried, total), carried
+
+    hidden_width = down_weight.shape[0]
+    cut_b = (hidden_width * 3 // 11) // 128 * 128
+    cut = (hidden_width * 6 // 11) // 128 * 128
+    down_a = FactorsFirst(cots, (cut_b, hidden_width), [query_rows])
+    prior_two, carried = run(join_two, near, far, first, last)
     carried = carried[:, 0, 0, 0]
 
-    def join_four(two, four, carried_near):
-        return jnp.where(index < META, two + carried_near * at_row(four, CARRIED) * four, two)
-
-    if reach > 2:
-        four = shift(two, 2)
+    prior_four = shift(prior_two, 2) if reach > 2 else jnp.zeros_like(prior_two)
 
     d_hiddens = [run(dot_t, cot, down_weight) for cot in cots]
 
-    prior = run(join_four, two, four, carried_near) if reach > 2 else two
     block = (seq_count, tok_count)
     mixed, ratio, denominator = run(
         functools.partial(
@@ -463,7 +588,7 @@
             forward_kernel,
             [(block + (wide,), jnp.bfloat16), (block + (wide,), jnp.float32), (block + (head_count,), jnp.float32)],
         ),
-        query_rows, key_proj, value_proj, row, column, prior,
+        query_rows, key_proj, value_proj, row, column, prior_two, prior_four,
     )
     head_size = lax.axis_size("head")
 
@@ -516,12 +641,9 @@
         d_up = (d_hidden * gate * sigmoid).astype(jnp.bfloat16)
         return hidden, d_gate, d_up
 
-    def feed_back(d_gate, d_up, gate_weight, up_weight):
-        return paired(dot_t(d_gate, gate_weight) + dot_t(d_up, up_weight))
-
-    hidden_width = down_weight.shape[0]
-    cut_b = (hidden_width * 3 // 11) // 128 * 128
-    cut = (hidden_width * 6 // 11) // 128 * 128
+    def feed_back(d_gate, d_up, gate_weight, up_weight, after):
+        return paired(dots_after((d_gate, d_up), (gate_weight, up_weight), after))
+
     for k, s in enumerate(spans):
         branch = run(lambda pair: spread(total(pair)), branches[k])
 
@@ -535,12 +657,14 @@
         for into, value in zip((mids, normeds, scales, h_mlps, hiddens, d_gates, d_ups),
                                (mid, normed, scale, h_mlp, hidden, d_gate, d_up)):
             into.append(value)
+        down_a.add(hidden)
+        begun = [down_a.left_came]
         if k == len(spans) - 1:
-            down_a = PairFirst(cots, hiddens, (cut_b, hidden_width))
-        d_hs.append(head_part(feed_back, d_gate, d_up, sigmoid_switch_matrix, up_weight))
-
-    down_b = LineFirst(cots, hiddens, (0, cut_b), [d_hs[-1][0]])
-    gate_a = PairFirst(h_mlps, d_gates, (0, cut), [down_b.whole])
+            gate_a = PairFirst(h_mlps, d_gates, (0, cut), [down_a.sent])
+            down_b = LineFirst(cots, hiddens, (0, cut_b), [gate_a.sent])
+            begun = [down_b.whole]
+        d_hs.append(head_part(feed_back, d_gate, d_up, sigmoid_switch_matrix, up_weight, begun))
+
 
     def out_part(k, after):
         return head_part(lambda hidden, weight: paired(dot_after(hidden, weight, after)), hiddens[k], down_weight)
@@ -571,74 +695,75 @@
         own = add_after(pair, after)
         results.append(run(lambda mid, own: (mid + spread(own)).astype(jnp.bfloat16), mids[k], own))
 
-    d_gain_mlp = middle_back(0, [gate_a.sent])
-    out_0 = out_part(0, [d_mixeds[0]])
+    d_gain_mlp = middle_back(0, [d_hs[1][0]])
+    down_a.line([d_mixeds[0]])
+    out_0 = out_part(0, [down_a.whole, down_b.both])
     d_gain_mlp = d_gain_mlp + middle_back(1, [out_0[0]])
 
     d_mixed = jnp.concatenate(d_mixeds, 1)
     d_state = run(
         functools.partial(per_sequence, state_back_kernel, [payload]),
-        query_rows, d_mixed, ratio, denominator, row, prior, meta(first, last, carried),
+        query_rows, d_mixed, ratio, denominator, row, prior_two, meta(first, last, carried),
     )
     near, far = shift(d_state, -1), shift(d_state, -2)
-    down_a.line([d_state])
-    outcome(0, out_0, [down_a.whole])
-    out_1 = out_part(1, [results[0]])
-    gate_b = PairFirst(h_mlps, d_gates, (cut, hidden_width), [out_1[0], down_b.both])
+    gate_b = PairFirst(h_mlps, d_gates, (cut, hidden_width), [d_state])
     down_b.pair()
-    gate_a.line([gate_b.sent])
+    outcome(0, out_0, [gate_b.sent])
+    gate_a.line([results[0]])
+    up_a = PairFirst(h_mlps, d_ups, (0, cut), [gate_a.whole, down_a.sum])
+    out_1 = out_part(1, [up_a.sent])
     mixed_rows = [flat(mixed[:, s]) for s in spans]
 
-    def join_two_back(near, far, carried):
-        total = jnp.where(index < META, near + at_row(near, CARRIED) * far, near)
-        return jnp.where(index == CARRIED, carried[:, None, None, None], total), at_row(near, CARRIED)
-
-    two, carried_near = run(join_two_back, near, far, carried)
-    if reach > 2:
-        four = shift(two, -2)
-    up_a = PairFirst(h_mlps, d_ups, (0, cut), [two, gate_a.whole, down_a.sum])
-    outcome(1, out_1, [up_a.sent])
-    result = run(lambda parts: jnp.concatenate(parts, 1), results)
-    later = run(join_four, two, four, carried_near) if reach > 2 else two
+    two = per_sequence(
+        join_back_kernel, [payload], near, far, jnp.broadcast_to(carried[:, None, None], (seq_count, 1, HEAD_V)),
+        after=[out_1[0]],
+    )
+    four = shift(two, -2) if reach > 2 else jnp.zeros_like(two)
+    gate_b.line([two])
+    up_b = PairFirst(h_mlps, d_ups, (cut, hidden_width), [gate_b.whole, gate_a.sum])
     d_query, d_key, d_value = run(
         functools.partial(
             per_sequence,
             backward_kernel,
             [(block + (narrow,), jnp.bfloat16), (block + (narrow,), jnp.bfloat16), (block + (wide,), jnp.bfloat16)],
-            after=[results[1]],
+            after=[up_b.sent],
         ),
-        query_rows, key_proj, value_proj, row, column, d_mixed, ratio, denominator, prior, later,
+        query_rows, key_proj, value_proj, row, column, d_mixed, ratio, denominator, prior_two, prior_four,
+        two, four,
     )
 
-    def in_back(d_query, d_key, d_value, query_weight, key_weight, value_weight):
-        d_query, d_key, d_value = flat(d_query), flat(d_key), flat(d_value)
-        return paired(dot_t(d_query, query_weight) + dot_t(d_key, key_weight) + dot_t(d_value, value_weight))
-
-    d_hs = [
-        head_part(in_back, d_query[:, s], d_key[:, s], d_value[:, s], query_weight, key_weight, value_weight)
-        for s in spans
-    ]
-    gate_b.line([d_hs[-1][0]])
-    up_b = PairFirst(h_mlps, d_ups, (cut, hidden_width), [gate_b.whole, gate_a.sum])
-    down_b.end([up_b.sent])
+    def in_part(k, after):
+        def work(*parts):
+            return paired(dots_after([flat(p) for p in parts], (query_weight, key_weight, value_weight), after))
+
+        s = spans[k]
+        return head_part(work, d_query[:, s], d_key[:, s], d_value[:, s])
+
+    up_a.line([d_query])
+    outcome(1, out_1, [up_a.whole])
+    out = PairFirst(d_branches, mixed_rows, (0, wide), [results[1], gate_b.sum])
+    in_0 = in_part(0, [out.sent])
+    down_b.end([in_0[0]])
+    in_1 = in_part(1, [down_b.sum])
+    up_b.line([in_1[0]])
     qkv_right = flat(jnp.concatenate([d_query, d_key, d_value], -1))
 
     d_tokens = []
 
-    def first_back(k, after):
+    def first_back(k, pair, after):
         def work(d_h, tokens, d_mid):
             normed, scale = rms_norm(mine(tokens).astype(jnp.float32))
             d_own, d_gain = rms_back(normed, scale, gain_attn, d_h)
             return spread(d_own + d_mid), d_gain
 
-        d_part, d_gain = run(work, add_after(d_hs[k], after), tokens[:, spans[k]], d_mids[k])
+        d_part, d_gain = run(work, add_after(pair, after), tokens[:, spans[k]], d_mids[k])
         d_tokens.append(d_part)
         return d_gain
 
-    d_gain_attn = first_back(0, [down_b.sum])
-    up_a.line([d_tokens[0]])
-    out = PairFirst(d_branches, mixed_rows, (0, wide), [up_a.whole, gate_b.sum])
-    d_gain_attn = d_gain_attn + first_back(1, [out.sent])
+    qkv = PairFirst([h_rows], [qkv_right], (0, qkv_right.shape[1]), [up_b.whole, up_a.sum])
+    d_gain_attn = first_back(0, in_0, [qkv.sent])
+    out.line([d_tokens[0]])
+    d_gain_attn = d_gain_attn + first_back(1, in_1, [out.whole, up_b.sum])
     count = lax.axis_size("seq")
 
     def gain_blocks(d_gain_attn, d_gain_mlp):
@@ -646,22 +771,20 @@
         if count != 8:
             return gains
         y = lax.axis_index("seq") % 2
-        blocks = gains.reshape(2, 4, 2, -1).transpose(2, 1, 3, 0)
+        blocks = gains.reshape(2, 4, 2, -1).transpose(2, 1, 0, 3).reshape(2, 8, -1)
         return pick_by(y, blocks[0], blocks[1]), pick_by(y, blocks[1], blocks[0])
 
     gains = run(gain_blocks, d_gain_attn, d_gain_mlp)
     if count == 8:
         gains_came = along_pair(gains[1])
-    up_b.line([d_tokens[1]])
     if count == 8:
-        gains = run(lambda mine, came, _: (mine + came).reshape(-1, 2), gains[0], gains_came, up_b.whole)
-        gains = along_line(gains)
+        gains = along_line(add_after((gains[0], gains_came), [d_tokens[1]]))
     else:
-        gains = lax.psum_scatter(gains, "seq", scatter_dimension=1, tiled=True).T
-    qkv = PairFirst([h_rows], [qkv_right], (0, qkv_right.shape[1]), [up_b.whole, up_a.sum])
-    out.line([qkv.sent, up_b.sum])
-    qkv.line([out.whole, out.sum, gains])
-    gains = gains.T
+        gains = lax.psum_scatter(gains, "seq", scatter_dimension=1, tiled=True)
+    qkv.line([gains])
+    output_weight_gradient = transposed_after(out.sum, [qkv.whole])
+    qkv = qkv.sum
+    result = jnp.concatenate(results, 1)
     d_tokens = jnp.concatenate(d_tokens, 1)
     down = jnp.concatenate([down_b.sum, down_a.sum], 1).T
     gate = jnp.concatenate([gate_a.sum, gate_b.sum], 1)
@@ -670,10 +793,10 @@
         result,
         d_tokens,
         gains[0],
-        qkv.sum[:, :narrow],
-        qkv.sum[:, narrow : 2 * narrow],
-        qkv.sum[:, 2 * narrow :],
-        out.sum.T,
+        qkv[:, :narrow],
+        qkv[:, narrow : 2 * narrow],
+        qkv[:, 2 * narrow :],
+        output_weight_gradient,
         gains[1],
         gate,
         up,

time: 874 us -> 789 us (0.903)
  waiting for transfers between devices: 274 us -> 175 us
  Pallas kernels: 128 us -> 178 us
  local copies, waits for them, and re-layouts: 122 us -> 94.9 us
  matrix products: 66.5 us -> 46.1 us
  other arithmetic: 85.1 us -> 95.8 us
    ppermute x9 -> x11, waiting for transfers between devices: 131 us -> 5.98 us  [along_pair(): lax.ppermute(part, 'seq', [(k, k ^ 1) for k in range(lax.axis_size('seq'))])]
    pallas_call x7 -> x14, Pallas kernels: 28.7 us -> 62.3 us  [the longest x8 30.3 us: add_after(): pl.pallas_call(kernel, grid=(steps,), in_specs=[spec, spec] + [pl.BlockSp...]
    unnamed x414 -> x381, local copies, waits for them, and re-layouts: 103 us -> 71.7 us
    dot_general x14 -> x4, matrix products: 37 us -> 12.6 us  [dot_t(): lax.dot_general(left, right, (((1,), (1,)), ((), ())), preferred_element_...]
    all_to_all x16 -> x14, blocking collectives: 114 us -> 97.8 us  [exchange(): lax.all_to_all(parts, 'head', 0, 0, axis_index_groups=groups, tiled=True)]
    all_to_all x1 -> x3, starting transfers between devices: 5.82 us -> 17.2 us  [exchange(): lax.all_to_all(parts, 'head', 0, 0, axis_index_groups=groups, tiled=True)]
    unnamed x0 -> x1, blocking collectives: none -> 11.1 us
    pallas_call x15 -> x14, Pallas kernels: 67 us -> 77.7 us  [blocks_dot(): pl.pallas_call(kernel, grid_spec=pltpu.PrefetchScalarGridSpec(num_scalar_...]
  transfers between devices with their start and end apart: 33 -> 36, of which waited for: 14 -> 15; matrix products, arithmetic and copies ran while one was open for 18% -> 20% of each run, Pallas kernels for 14% -> 23%
where the time goes in v3:
time: 789 us; the launch traced here: 779 us
  Pallas kernels  178 us (23%)
  waiting for transfers between devices  175 us (22%)
  blocking collectives  109 us (14%)
  other arithmetic  95.8 us (12%)
  local copies, waits for them, and re-layouts  94.9 us (12%)
  starting transfers between devices  64 us (8%)
  matrix products  46.1 us (6%)
  between operations  16.9 us (2%)
    all_to_all x14, blocking collectives, exchange(): lax.all_to_all(parts, 'head', 0, 0, axis_index_groups=groups, tiled=True)  97.8 us
    pallas_call x14, Pallas kernels, blocks_dot(): pl.pallas_call(kernel, grid_spec=pltpu.PrefetchScalarGridSpec(num_scalar_...  77.7 us
    unnamed x381, local copies, waits for them, and re-layouts  71.7 us
    ppermute x8, waiting for transfers between devices, swap(): return lax.ppermute(part, 'head', [(k, k ^ bit) for k in range(count)])  57.4 us
    reduce_scatter x8, waiting for transfers between devices, along_line(): lax.psum_scatter(parts, 'seq', scatter_dimension=0, axis_index_groups=gro...  56.8 us
    ppermute x6, waiting for transfers between devices, shift(): lax.ppermute(part, 'seq', [(k, k + by) for k in range(count) if 0 <= k +...  43.9 us
    dot_general x9, matrix products, dot(): return jnp.dot(left, right, preferred_element_type=jnp.float32)  33.5 us
    pallas_call x8, Pallas kernels, add_after(): pl.pallas_call(kernel, grid=(steps,), in_specs=[spec, spec] + [pl.BlockSp...  30.3 us
  transfers between devices with their start and end apart: 36, of which 15 were waited for; matrix products, arithmetic and copies ran while one was open for 20% of the time, Pallas kernels for 23%

profile of v3, /device:TPU:0, one launch (start us, length us, event | category | flops | bytes accessed | tf_op | source)
XLA Modules:
  0.0 779.2 jit_solution(1745175960544311014)
XLA Ops:
  91.9 7.1 all_to_all.85
  105.9 7.1 all_to_all.86
  116.1 31.7 %collective-permute-done.3 = f32[256,2048]{1,0:T(8,128)S(1)} collective-permute-done((f32[256,2048]{1,0:T(8,128)S(1)}, f32[256,2048]{1,0:T(8,128)S(1)}, u32[]{:S(2)}, u32[]{:S(2)}) %collective-permute-start.3) | collective-permute-done | bytes 2097184 | tf_op jit(solution)/shard_map/ppermute | solution.py:27
  148.5 7.4 all_to_all.87
  158.8 7.2 fusion.63
  172.2 6.5 collective-permute-start.7
  180.9 9.4 %shard_map.206 = f32[512,2048]{1,0:T(8,128)S(1)} custom-call(bf16[512,1408]{1,0:T(8,128)(2,1)S(1)} %get-tuple-element.149.refs_0_.refs_2_, bf16[512,1408]{1,0:T(8,128)(2,1)S(1)} %get-tuple-element.150.refs_1_.refs_2_, bf16[2048,1408]{1,0:T(8,128)(2,1)} %refs_2_.1, bf16[2048,1408]{1,0:T(8,128)(2,1)} %refs_3_.3, ...), custom_call_target="tpu_custom_call" | custom-call | flops 549755813888 | bytes 1048576 | tf_op jit(solution)/shard_map/pallas_call | solution.py:407
  190.3 7.1 all_to_all.88
  203.5 7.6 all_to_all.89
  245.9 9.3 %shard_map.209 = f32[512,2048]{1,0:T(8,128)S(1)} custom-call(bf16[512,1408]{1,0:T(8,128)(2,1)S(1)} %copy-done.115, bf16[512,1408]{1,0:T(8,128)(2,1)S(1)} %copy-done.105, bf16[2048,1408]{1,0:T(8,128)(2,1)} %refs_2_.1, bf16[2048,1408]{1,0:T(8,128)(2,1)} %refs_3_.3, f32[2048,384]{1,0:T(8,128)S(1)} %copy-done.6), custom_call_target="tpu_custom_call" | custom-call | flops 549755813888 | bytes 1048576 | tf_op jit(solution)/shard_map/pallas_call | solution.py:407
  255.2 7.1 all_to_all.90
  275.6 7.4 all_to_all.91
  289.8 10.3 %shard_map.211.refs_0_ = f32[1024,1024]{1,0:T(8,128)} custom-call(s32[4]{0:T(128)S(1)} %broadcast_add_fusion.1.where_ref, bf16[512,2048]{1,0:T(8,128)(2,1)S(1)} %bitcast.166, bf16[512,2048]{1,0:T(8,128)(2,1)S(1)} %bitcast.162, f32[1024,1024]{1,0:T(8,128)} %collective-permute-done.4.refs_4_.refs_2_.refs_3_, ...), custom_call_target="tpu_custom_call" | custom-call | flops 549755813888 | bytes 1048576 | tf_op jit(solution)/shard_map/pallas_call | solution.py:301
  308.4 6.1 shard_map.212
  314.5 7.1 all_to_all.92
  333.1 7.2 all_to_all.93
  362.7 8.5 %collective-permute-done.9.b_ref = f32[256,2048]{1,0:T(8,128)} collective-permute-done((f32[256,2048]{1,0:T(8,128)}, f32[256,2048]{1,0:T(8,128)}, u32[]{:S(2)}, u32[]{:S(2)}) %collective-permute-start.9) | collective-permute-done | bytes 2097184 | tf_op jit(solution)/shard_map/ppermute | solution.py:27
  379.6 7.6 all_to_all.94
  390.3 6.0 shard_map.217.refs_4_
  418.8 7.1 all_to_all.95
  434.8 5.9 shard_map.221.refs_4_
  440.7 38.9 %collective-permute-done.16.refs_11_ = f32[2,4,184,128]{3,2,1,0:T(8,128)} collective-permute-done((f32[2,4,184,128]{3,2,1,0:T(8,128)}, f32[2,4,184,128]{3,2,1,0:T(8,128)}, u32[]{:S(2)}, u32[]{:S(2)}) %collective-permute-start.16) | collective-permute-done | bytes 753696 | tf_op jit(solution)/shard_map/ppermute | solution.py:32
  493.1 12.3 %shard_map.223 = (bf16[2,512,64]{2,1,0:T(8,128)(2,1)S(1)}, bf16[2,512,64]{2,1,0:T(8,128)(2,1)S(1)}, bf16[2,512,512]{2,1,0:T(8,128)(2,1)S(1)}) custom-call(bf16[2,512,64]{2,1,0:T(8,128)(2,1)S(1)} %bitcast.181, bf16[2,512,64]{2,1,0:T(8,128)(2,1)S(1)} %bitcast.177, bf16[2,512,512]{2,1,0:T(8,128)(2,1)} %bitcast.187, f32[2,1,512]{2,1,0:T(1,128)S(1)} %copy-done.86, ...), custom_call_target="tpu_custom_call" | custom-call | flops 549755813888 | bytes 1048576 | tf_op jit(solution)/shard_map/pallas_call | solution.py:236
  510.6 6.1 shard_map.224.refs_0_
  560.4 7.1 all_to_all.96
  578.7 7.1 all_to_all.97
  628.3 5.9 all-to-all-start.14
  645.6 16.5 %collective-permute-done.21.b_ref = f32[256,2048]{1,0:T(8,128)} collective-permute-done((f32[256,2048]{1,0:T(8,128)}, f32[256,2048]{1,0:T(8,128)}, u32[]{:S(2)}, u32[]{:S(2)}) %collective-permute-start.21) | collective-permute-done | bytes 2097184 | tf_op jit(solution)/shard_map/ppermute | solution.py:27
  687.5 8.0 %pad_maximum_fusion = f32[2,512,2048]{2,1,0:T(8,128)} fusion(f32[2,256,2048]{2,1,0:T(8,128)} %all-to-all-done.15.refs_0_, f32[2,256,2048]{2,1,0:T(8,128)} %all-to-all-done.14.refs_5_), kind=kLoop, calls=%fused_computation.5 | loop fusion | flops 2097152 | bytes 16777216 | tf_op jit(solution)/shard_map/concatenate | solution.py:788
  699.4 11.1 %all-reduce = f32[8,256]{1,0:T(8,128)S(1)} all-reduce(f32[8,256]{1,0:T(8,128)} %shard_map.235), channel_id=8, replica_groups={{0,8,16,24},{4,12,20,28},{1,9,17,25},{5,13,21,29},{2,10,18,26},{6,14,22..., use_global_device_ids=true, to_apply=%region_20.21.clone | all-reduce | flops 2048 | bytes 16384
  711.1 6.1 shard_map.236.refs_0_
  719.4 48.1 %reduce-scatter.21.cloned.1.call-done = f32[256,640]{1,0:T(8,128)} async-done(((f32[1024,640]{1,0:T(8,128)}), f32[256,640]{1,0:T(8,128)}) %reduce-scatter.21.cloned.1.call-update) | async-done | bytes 655376 | tf_op jit(solution)/shard_map/reduce_scatter | solution.py:254
  (603 shorter events, 414.5 us)
Async XLA Ops:
  7.2 297.9 %reduce-scatter.9.cloned.1.call-start = ((), (), s32[]{:S(2)}) async-start(), calls=%async_computation.25 | async-start | bytes 3932160 | tf_op jit(solution)/shard_map/reduce_scatter | solution.py:254
  24.2 34.0 %collective-permute-start = (f32[2,4,184,128]{3,2,1,0:T(8,128)}, f32[2,4,184,128]{3,2,1,0:T(8,128)}, u32[]{:S(2)}, u32[]{:S(2)}) collective-permute-start(f32[2,4,184,128]{3,2,1,0:T(8,128)} %shard_map.203), channel_id=1, source_target_pairs={{0,4},{4,8},{8,12},{12,16},{16,20},{20,24},{24,28},{1,5},{5,9},{9,... | collective-permute-start | bytes 2261000 | tf_op jit(solution)/shard_map/ppermute | solution.py:32
  30.0 28.3 %collective-permute-start.1 = (f32[2,4,184,128]{3,2,1,0:T(8,128)}, f32[2,4,184,128]{3,2,1,0:T(8,128)}, u32[]{:S(2)}, u32[]{:S(2)}) collective-permute-start(f32[2,4,184,128]{3,2,1,0:T(8,128)} %shard_map.203), channel_id=1, source_target_pairs={{0,8},{4,12},{8,16},{12,20},{16,24},{20,28},{1,9},{5,13},{9,17},{1... | collective-permute-start | bytes 2261000 | tf_op jit(solution)/shard_map/ppermute | solution.py:32
  48.2 132.7 %collective-permute-start.4 = (f32[1024,1024]{1,0:T(8,128)}, f32[1024,1024]{1,0:T(8,128)}, u32[]{:S(2)}, u32[]{:S(2)}) collective-permute-start(f32[1024,1024]{1,0:T(8,128)} %shard_map.205), channel_id=1, source_target_pairs={{0,4},{4,0},{8,12},{12,8},{16,20},{20,16},{24,28},{28,24},{1,5},{5... | collective-permute-start | bytes 12582920 | tf_op jit(solution)/shard_map/ppermute | solution.py:249
  61.5 18.2 %collective-permute-start.2 = (f32[2,4,184,128]{3,2,1,0:T(8,128)S(1)}, f32[2,4,184,128]{3,2,1,0:T(8,128)S(1)}, u32[]{:S(2)}, u32[]{:S(2)}) collective-permute-start(f32[2,4,184,128]{3,2,1,0:T(8,128)S(1)} %fusion.44.refs_5_.refs_8_), channel_id=1, source_target_pairs={{0,8},{4,12},{8,16},{12,20},{16,24},{20,28},{1,9},{5,13},{9,17},{1... | collective-permute-start | bytes 2261000 | tf_op jit(solution)/shard_map/ppermute | solution.py:32
  99.2 48.5 %collective-permute-start.3 = (f32[256,2048]{1,0:T(8,128)S(1)}, f32[256,2048]{1,0:T(8,128)S(1)}, u32[]{:S(2)}, u32[]{:S(2)}) collective-permute-start(f32[256,2048]{1,0:T(8,128)S(1)} %fusion.34), channel_id=1, source_target_pairs={{0,2},{1,3},{2,0},{3,1},{4,6},{5,7},{6,4},{7,5},{8,10},{9,11},{10,... | collective-permute-start | bytes 6291464 | tf_op jit(solution)/shard_map/ppermute | solution.py:27
  114.6 86.0 %collective-permute-start.6 = (f32[256,2048]{1,0:T(8,128)}, f32[256,2048]{1,0:T(8,128)}, u32[]{:S(2)}, u32[]{:S(2)}) collective-permute-start(f32[256,2048]{1,0:T(8,128)} %fusion.33), channel_id=1, source_target_pairs={{0,2},{1,3},{2,0},{3,1},{4,6},{5,7},{6,4},{7,5},{8,10},{9,11},{10,... | collective-permute-start | bytes 6291464 | tf_op jit(solution)/shard_map/ppermute | solution.py:27
  172.2 115.1 %collective-permute-start.7 = (f32[512,1024]{1,0:T(8,128)}, f32[512,1024]{1,0:T(8,128)}, u32[]{:S(2)}, u32[]{:S(2)}) collective-permute-start(f32[512,1024]{1,0:T(8,128)} %slice_convert_fusion), channel_id=1, source_target_pairs={{0,4},{4,0},{8,12},{12,8},{16,20},{20,16},{24,28},{28,24},{1,5},{5... | collective-permute-start | bytes 6291464 | tf_op jit(solution)/shard_map/ppermute | solution.py:249
  199.1 67.9 %collective-permute-start.5 = (f32[256,2048]{1,0:T(8,128)}, f32[256,2048]{1,0:T(8,128)}, u32[]{:S(2)}, u32[]{:S(2)}) collective-permute-start(f32[256,2048]{1,0:T(8,128)} %fusion.32.a_ref), channel_id=1, source_target_pairs={{0,2},{1,3},{2,0},{3,1},{4,6},{5,7},{6,4},{7,5},{8,10},{9,11},{10,... | collective-permute-start | bytes 6291464 | tf_op jit(solution)/shard_map/ppermute | solution.py:27
  228.0 59.3 %collective-permute-start.8 = (f32[512,1024]{1,0:T(8,128)}, f32[512,1024]{1,0:T(8,128)}, u32[]{:S(2)}, u32[]{:S(2)}) collective-permute-start(f32[512,1024]{1,0:T(8,128)} %slice_convert_fusion.1.refs_4_), channel_id=1, source_target_pairs={{0,4},{4,0},{8,12},{12,8},{16,20},{20,16},{24,28},{28,24},{1,5},{5... | collective-permute-start | bytes 6291464 | tf_op jit(solution)/shard_map/ppermute | solution.py:249
  233.9 154.3 %collective-permute-start.11 = (f32[1024,768]{1,0:T(8,128)}, f32[1024,768]{1,0:T(8,128)}, u32[]{:S(2)}, u32[]{:S(2)}) collective-permute-start(f32[1024,768]{1,0:T(8,128)} %shard_map.207.refs_4_), channel_id=1, source_target_pairs={{0,4},{4,0},{8,12},{12,8},{16,20},{20,16},{24,28},{28,24},{1,5},{5... | collective-permute-start | bytes 9437192 | tf_op jit(solution)/shard_map/ppermute | solution.py:249
  241.3 159.2 %reduce-scatter.11.cloned.1.call-start = ((), (), s32[]{:S(2)}) async-start(), calls=%async_computation.26 | async-start | bytes 5242880 | tf_op jit(solution)/shard_map/reduce_scatter | solution.py:254
  264.0 60.4 %collective-permute-start.10 = (f32[256,2048]{1,0:T(8,128)}, f32[256,2048]{1,0:T(8,128)}, u32[]{:S(2)}, u32[]{:S(2)}) collective-permute-start(f32[256,2048]{1,0:T(8,128)} %fusion.31.refs_0_.a_ref), channel_id=1, source_target_pairs={{0,2},{1,3},{2,0},{3,1},{4,6},{5,7},{6,4},{7,5},{8,10},{9,11},{10,... | collective-permute-start | bytes 6291464 | tf_op jit(solution)/shard_map/ppermute | solution.py:27
  305.0 178.3 %reduce-scatter.13.cloned.1.call-start = ((), (), s32[]{:S(2)}) async-start(), calls=%async_computation.27 | async-start | bytes 3932160 | tf_op jit(solution)/shard_map/reduce_scatter | solution.py:254
  323.3 48.0 %collective-permute-start.9 = (f32[256,2048]{1,0:T(8,128)}, f32[256,2048]{1,0:T(8,128)}, u32[]{:S(2)}, u32[]{:S(2)}) collective-permute-start(f32[256,2048]{1,0:T(8,128)} %fusion.28.refs_0_.a_ref), channel_id=1, source_target_pairs={{0,2},{1,3},{2,0},{3,1},{4,6},{5,7},{6,4},{7,5},{8,10},{9,11},{10,... | collective-permute-start | bytes 6291464 | tf_op jit(solution)/shard_map/ppermute | solution.py:27
  355.9 71.7 %collective-permute-start.14 = (f32[2,4,184,128]{3,2,1,0:T(8,128)}, f32[2,4,184,128]{3,2,1,0:T(8,128)}, u32[]{:S(2)}, u32[]{:S(2)}) collective-permute-start(f32[2,4,184,128]{3,2,1,0:T(8,128)} %shard_map.214.refs_4_), channel_id=1, source_target_pairs={{4,0},{8,4},{12,8},{16,12},{20,16},{24,20},{28,24},{5,1},{9,5},{13... | collective-permute-start | bytes 2261000 | tf_op jit(solution)/shard_map/ppermute | solution.py:32
  357.1 72.5 %collective-permute-start.15 = (f32[2,4,184,128]{3,2,1,0:T(8,128)}, f32[2,4,184,128]{3,2,1,0:T(8,128)}, u32[]{:S(2)}, u32[]{:S(2)}) collective-permute-start(f32[2,4,184,128]{3,2,1,0:T(8,128)} %shard_map.214.refs_4_), channel_id=1, source_target_pairs={{8,0},{12,4},{16,8},{20,12},{24,16},{28,20},{9,1},{13,5},{17,9},{2... | collective-permute-start | bytes 2261000 | tf_op jit(solution)/shard_map/ppermute | solution.py:32
  358.4 76.4 %collective-permute-start.17 = (f32[1024,640]{1,0:T(8,128)}, f32[1024,640]{1,0:T(8,128)}, u32[]{:S(2)}, u32[]{:S(2)}) collective-permute-start(f32[1024,640]{1,0:T(8,128)} %shard_map.215.refs_0_), channel_id=1, source_target_pairs={{0,4},{4,0},{8,12},{12,8},{16,20},{20,16},{24,28},{28,24},{1,5},{5... | collective-permute-start | bytes 7864328 | tf_op jit(solution)/shard_map/ppermute | solution.py:249
  371.2 198.4 %collective-permute-start.20 = (f32[256,384]{1,0:T(8,128)}, f32[256,384]{1,0:T(8,128)}, u32[]{:S(2)}, u32[]{:S(2)}) collective-permute-start(f32[256,384]{1,0:T(8,128)} %get-tuple-element.313), channel_id=1, source_target_pairs={{0,4},{4,0},{8,12},{12,8},{16,20},{20,16},{24,28},{28,24},{1,5},{5... | collective-permute-start | bytes 1179656 | tf_op jit(solution)/shard_map/ppermute | solution.py:249
  397.6 147.8 %reduce-scatter.15.cloned.1.call-start = ((), (), s32[]{:S(2)}) async-start(), calls=%async_computation.28 | async-start | bytes 3276800 | tf_op jit(solution)/shard_map/reduce_scatter | solution.py:254
  409.1 101.6 %collective-permute-start.13 = (f32[1024,768]{1,0:T(8,128)}, f32[1024,768]{1,0:T(8,128)}, u32[]{:S(2)}, u32[]{:S(2)}) collective-permute-start(f32[1024,768]{1,0:T(8,128)} %shard_map.218.refs_0_), channel_id=1, source_target_pairs={{0,4},{4,0},{8,12},{12,8},{16,20},{20,16},{24,28},{28,24},{1,5},{5... | collective-permute-start | bytes 9437192 | tf_op jit(solution)/shard_map/ppermute | solution.py:249
  427.6 89.9 %collective-permute-start.12 = (f32[256,2048]{1,0:T(8,128)}, f32[256,2048]{1,0:T(8,128)}, u32[]{:S(2)}, u32[]{:S(2)}) collective-permute-start(f32[256,2048]{1,0:T(8,128)} %fusion.25.refs_3_.a_ref), channel_id=1, source_target_pairs={{0,2},{1,3},{2,0},{3,1},{4,6},{5,7},{6,4},{7,5},{8,10},{9,11},{10,... | collective-permute-start | bytes 6291464 | tf_op jit(solution)/shard_map/ppermute | solution.py:27
  432.0 47.6 %collective-permute-start.16 = (f32[2,4,184,128]{3,2,1,0:T(8,128)}, f32[2,4,184,128]{3,2,1,0:T(8,128)}, u32[]{:S(2)}, u32[]{:S(2)}) collective-permute-start(f32[2,4,184,128]{3,2,1,0:T(8,128)} %shard_map.220.refs_5_.refs_10_), channel_id=1, source_target_pairs={{8,0},{12,4},{16,8},{20,12},{24,16},{28,20},{9,1},{13,5},{17,9},{2... | collective-permute-start | bytes 2261000 | tf_op jit(solution)/shard_map/ppermute | solution.py:32
  491.9 104.1 %collective-permute-start.19 = (f32[1024,640]{1,0:T(8,128)}, f32[1024,640]{1,0:T(8,128)}, u32[]{:S(2)}, u32[]{:S(2)}) collective-permute-start(f32[1024,640]{1,0:T(8,128)} %shard_map.222.refs_12_), channel_id=1, source_target_pairs={{0,4},{4,0},{8,12},{12,8},{16,20},{20,16},{24,28},{28,24},{1,5},{5... | collective-permute-start | bytes 7864328 | tf_op jit(solution)/shard_map/ppermute | solution.py:249
  532.1 75.5 %reduce-scatter.17.cloned.1.call-start = ((), (), s32[]{:S(2)}) async-start(), calls=%async_computation.29 | async-start | bytes 3932160 | tf_op jit(solution)/shard_map/reduce_scatter | solution.py:254
  545.4 116.7 %reduce-scatter.19.cloned.1.call-start = ((), (), s32[]{:S(2)}) async-start(), calls=%async_computation.30 | async-start | bytes 3276800 | tf_op jit(solution)/shard_map/reduce_scatter | solution.py:254
  554.8 79.5 %collective-permute-start.22 = (f32[1024,512]{1,0:T(8,128)}, f32[1024,512]{1,0:T(8,128)}, u32[]{:S(2)}, u32[]{:S(2)}) collective-permute-start(f32[1024,512]{1,0:T(8,128)} %shard_map.226.refs_6_), channel_id=1, source_target_pairs={{0,4},{4,0},{8,12},{12,8},{16,20},{20,16},{24,28},{28,24},{1,5},{5... | collective-permute-start | bytes 6291464 | tf_op jit(solution)/shard_map/ppermute | solution.py:249
  569.1 48.8 %collective-permute-start.18 = (f32[256,2048]{1,0:T(8,128)}, f32[256,2048]{1,0:T(8,128)}, u32[]{:S(2)}, u32[]{:S(2)}) collective-permute-start(f32[256,2048]{1,0:T(8,128)} %fusion.24.refs_0_.a_ref), channel_id=1, source_target_pairs={{0,2},{1,3},{2,0},{3,1},{4,6},{5,7},{6,4},{7,5},{8,10},{9,11},{10,... | collective-permute-start | bytes 6291464 | tf_op jit(solution)/shard_map/ppermute | solution.py:27
  587.5 74.6 %collective-permute-start.21 = (f32[256,2048]{1,0:T(8,128)}, f32[256,2048]{1,0:T(8,128)}, u32[]{:S(2)}, u32[]{:S(2)}) collective-permute-start(f32[256,2048]{1,0:T(8,128)} %fusion.23.refs_5_.a_ref), channel_id=1, source_target_pairs={{0,2},{1,3},{2,0},{3,1},{4,6},{5,7},{6,4},{7,5},{8,10},{9,11},{10,... | collective-permute-start | bytes 6291464 | tf_op jit(solution)/shard_map/ppermute | solution.py:27
  615.7 95.3 %collective-permute-start.24 = (f32[1024,640]{1,0:T(8,128)}, f32[1024,640]{1,0:T(8,128)}, u32[]{:S(2)}, u32[]{:S(2)}) collective-permute-start(f32[1024,640]{1,0:T(8,128)} %shard_map.231.refs_0_), channel_id=1, source_target_pairs={{0,4},{4,0},{8,12},{12,8},{16,20},{20,16},{24,28},{28,24},{1,5},{5... | collective-permute-start | bytes 7864328 | tf_op jit(solution)/shard_map/ppermute | solution.py:249
  634.2 83.0 %reduce-scatter.23.cloned.1.call-start = ((), (), s32[]{:S(2)}) async-start(), calls=%async_computation.32 | async-start | bytes 2621440 | tf_op jit(solution)/shard_map/reduce_scatter | solution.py:254
  677.6 89.9 %reduce-scatter.21.cloned.1.call-start = ((), (), s32[]{:S(2)}) async-start(), calls=%async_computation.31 | async-start | bytes 3276800 | tf_op jit(solution)/shard_map/reduce_scatter | solution.py:254
  (191 other events, 1098.4 us)
Sparse Core Ops, SparseCore 0:
  241.4 61.4 reduce-scatter.8
  305.2 95.2 reduce-scatter.10
  403.4 79.8 reduce-scatter.12
  485.6 51.7 reduce-scatter.14
  545.5 62.0 reduce-scatter.16
  609.9 52.1 reduce-scatter.18
  664.5 43.8 reduce-scatter.22
  717.3 50.1 reduce-scatter.20

commit v4 on v3

--- a/solution.py
+++ b/solution.py
@@ -345,36 +345,39 @@
     )(where, *chunks, *after)
 
 
-def add_after(pair, after):
-    rows, width = pair[0].shape
+def add_after(terms, after):
+    rows, width = terms[0].shape
     steps = 4 if rows % 32 == 0 else 1
 
-    def kernel(a_ref, b_ref, *refs):
-        refs[-1][...] = a_ref[...] + b_ref[...]
+    def kernel(*refs):
+        refs[-1][...] = sum(ref[...] for ref in refs[: len(terms)])
 
     spec = pl.BlockSpec((rows // steps, width), lambda k: (k, 0))
     return pl.pallas_call(
         kernel,
         grid=(steps,),
-        in_specs=[spec, spec] + [pl.BlockSpec(memory_space=pl.ANY) for _ in after],
+        in_specs=[spec] * len(terms) + [pl.BlockSpec(memory_space=pl.ANY) for _ in after],
         out_specs=spec,
         out_shape=jax.ShapeDtypeStruct((rows, width), jnp.float32),
         cost_estimate=LONG,
-    )(*pair, *after)
-
-
-def transposed_after(value, after):
-    def kernel(in_ref, *refs):
-        refs[-1][...] = jnp.transpose(in_ref[...])
+    )(*terms, *after)
+
+
+def transposed_after(terms, after):
+    value = terms[0]
+
+    def kernel(*refs):
+        refs[-1][...] = jnp.transpose(sum(ref[...] for ref in refs[: len(terms)]))
 
     return pl.pallas_call(
         kernel,
         grid=(1,),
-        in_specs=[pl.BlockSpec(value.shape, lambda k: (0, 0))] + [pl.BlockSpec(memory_space=pl.ANY) for _ in after],
+        in_specs=[pl.BlockSpec(value.shape, lambda k: (0, 0)) for _ in terms]
+        + [pl.BlockSpec(memory_space=pl.ANY) for _ in after],
         out_specs=pl.BlockSpec(value.shape[::-1], lambda k: (0, 0)),
         out_shape=jax.ShapeDtypeStruct(value.shape[::-1], value.dtype),
         cost_estimate=LONG,
-    )(value, *after)
+    )(*terms, *after)
 
 
 def dot_after(left, right, after):
@@ -424,15 +427,16 @@
         self.plain = lax.axis_size("seq") != 8
         if not self.plain:
             y = lax.axis_index("seq") % 2
-            self.places = pair_places(y)
-            self.sent = blocks_dot(own_terms(left, right, span), pair_places(1 - y), span, after=after)
+            self.places, theirs = pair_places(y), pair_places(1 - y)
+            self.sent = blocks_dot(own_terms(left, right, span), theirs, span, after=after)
             self.came = along_pair(self.sent)
 
     def line(self, after=()):
         if self.plain:
             self.sum = scattered(self.left, [r[:, self.span[0] : self.span[1]] for r in self.right])
             return
-        self.whole = blocks_dot(own_terms(self.left, self.right, self.span), self.places, self.span, self.came, after)
+        terms = own_terms(self.left, self.right, self.span)
+        self.whole = blocks_dot(terms, self.places, self.span, self.came, after)
         self.sum = along_line(self.whole)
 
 
@@ -475,9 +479,9 @@
             self.whole = blocks_dot(own_terms(left, right, span), both.reshape(8).astype(jnp.int32), span, after=after)
             self.both = along_line(self.whole)
 
-    def pair(self):
+    def pair(self, after):
         if not self.plain:
-            self.came = along_pair(self.both[self.block :])
+            self.came = along_pair(add_after((self.both[self.block :],), after))
 
     def end(self, after):
         if self.plain:
@@ -660,9 +664,9 @@
         down_a.add(hidden)
         begun = [down_a.left_came]
         if k == len(spans) - 1:
-            gate_a = PairFirst(h_mlps, d_gates, (0, cut), [down_a.sent])
-            down_b = LineFirst(cots, hiddens, (0, cut_b), [gate_a.sent])
-            begun = [down_b.whole]
+            down_b = LineFirst(cots, hiddens, (0, cut_b), [down_a.sent])
+            gate_a = PairFirst(h_mlps, d_gates, (0, cut), [down_b.whole])
+            begun = [gate_a.sent]
         d_hs.append(head_part(feed_back, d_gate, d_up, sigmoid_switch_matrix, up_weight, begun))
 
 
@@ -695,10 +699,10 @@
         own = add_after(pair, after)
         results.append(run(lambda mid, own: (mid + spread(own)).astype(jnp.bfloat16), mids[k], own))
 
-    d_gain_mlp = middle_back(0, [d_hs[1][0]])
-    down_a.line([d_mixeds[0]])
-    out_0 = out_part(0, [down_a.whole, down_b.both])
-    d_gain_mlp = d_gain_mlp + middle_back(1, [out_0[0]])
+    down_a.line([d_hs[1][0]])
+    d_gain_mlp = middle_back(0, [down_a.whole, down_b.both])
+    gate_b = PairFirst(h_mlps, d_gates, (cut, hidden_width), [d_mixeds[0]])
+    d_gain_mlp = d_gain_mlp + middle_back(1, [gate_b.sent])
 
     d_mixed = jnp.concatenate(d_mixeds, 1)
     d_state = run(
@@ -706,27 +710,24 @@
         query_rows, d_mixed, ratio, denominator, row, prior_two, meta(first, last, carried),
     )
     near, far = shift(d_state, -1), shift(d_state, -2)
-    gate_b = PairFirst(h_mlps, d_gates, (cut, hidden_width), [d_state])
-    down_b.pair()
-    outcome(0, out_0, [gate_b.sent])
-    gate_a.line([results[0]])
+    gate_a.line([d_state])
     up_a = PairFirst(h_mlps, d_ups, (0, cut), [gate_a.whole, down_a.sum])
-    out_1 = out_part(1, [up_a.sent])
+    gate_b.line([up_a.sent])
     mixed_rows = [flat(mixed[:, s]) for s in spans]
 
     two = per_sequence(
         join_back_kernel, [payload], near, far, jnp.broadcast_to(carried[:, None, None], (seq_count, 1, HEAD_V)),
-        after=[out_1[0]],
+        after=[gate_b.whole],
     )
     four = shift(two, -2) if reach > 2 else jnp.zeros_like(two)
-    gate_b.line([two])
-    up_b = PairFirst(h_mlps, d_ups, (cut, hidden_width), [gate_b.whole, gate_a.sum])
+    out_0 = out_part(0, [two])
+    up_b = PairFirst(h_mlps, d_ups, (cut, hidden_width), [out_0[0]])
     d_query, d_key, d_value = run(
         functools.partial(
             per_sequence,
             backward_kernel,
             [(block + (narrow,), jnp.bfloat16), (block + (narrow,), jnp.bfloat16), (block + (wide,), jnp.bfloat16)],
-            after=[up_b.sent],
+            after=[up_b.sent, gate_a.sum],
         ),
         query_rows, key_proj, value_proj, row, column, d_mixed, ratio, denominator, prior_two, prior_four,
         two, four,
@@ -740,11 +741,10 @@
         return head_part(work, d_query[:, s], d_key[:, s], d_value[:, s])
 
     up_a.line([d_query])
-    outcome(1, out_1, [up_a.whole])
-    out = PairFirst(d_branches, mixed_rows, (0, wide), [results[1], gate_b.sum])
-    in_0 = in_part(0, [out.sent])
-    down_b.end([in_0[0]])
-    in_1 = in_part(1, [down_b.sum])
+    out = PairFirst(d_branches, mixed_rows, (0, wide), [up_a.whole])
+    in_0 = in_part(0, [out.sent, gate_b.sum])
+    outcome(0, out_0, [in_0[0]])
+    in_1 = in_part(1, [results[0]])
     up_b.line([in_1[0]])
     qkv_right = flat(jnp.concatenate([d_query, d_key, d_value], -1))
 
@@ -760,10 +760,13 @@
         d_tokens.append(d_part)
         return d_gain
 
-    qkv = PairFirst([h_rows], [qkv_right], (0, qkv_right.shape[1]), [up_b.whole, up_a.sum])
-    d_gain_attn = first_back(0, in_0, [qkv.sent])
-    out.line([d_tokens[0]])
-    d_gain_attn = d_gain_attn + first_back(1, in_1, [out.whole, up_b.sum])
+    qkv = PairFirst([h_rows], [qkv_right], (0, qkv_right.shape[1]), [up_b.whole])
+    d_gain_attn = first_back(0, in_0, [qkv.sent, up_a.sum])
+    out_1 = out_part(1, [d_tokens[0]])
+    out.line([out_1[0]])
+    qkv.line([out.whole, up_b.sum])
+    d_gain_attn = d_gain_attn + first_back(1, in_1, [qkv.whole])
+    down_b.pair([d_tokens[1]])
     count = lax.axis_size("seq")
 
     def gain_blocks(d_gain_attn, d_gain_mlp):
@@ -781,8 +784,9 @@
         gains = along_line(add_after((gains[0], gains_came), [d_tokens[1]]))
     else:
         gains = lax.psum_scatter(gains, "seq", scatter_dimension=1, tiled=True)
-    qkv.line([gains])
-    output_weight_gradient = transposed_after(out.sum, [qkv.whole])
+    outcome(1, out_1, [d_tokens[1], out.sum])
+    down_b.end([results[1]])
+    output_weight_gradient = transposed_after([out.sum], [qkv.whole])
     qkv = qkv.sum
     result = jnp.concatenate(results, 1)
     d_tokens = jnp.concatenate(d_tokens, 1)

time: 789 us -> 765 us (0.970)
  waiting for transfers between devices: 175 us -> 154 us
  blocking collectives: 109 us -> 125 us
  starting transfers between devices: 64 us -> 50.5 us
    ppermute x11, waiting for transfers between devices: 5.98 us -> 40.9 us  [along_pair(): lax.ppermute(part, 'seq', [(k, k ^ 1) for k in range(lax.axis_size('seq'))])]
    ppermute x8, waiting for transfers between devices: 57.4 us -> 31.7 us  [swap(): return lax.ppermute(part, 'head', [(k, k ^ bit) for k in range(count)])]
    ppermute x6, waiting for transfers between devices: 43.9 us -> 26.8 us  [shift(): lax.ppermute(part, 'seq', [(k, k + by) for k in range(count) if 0 <= k +...]
    all_to_all x14 -> x16, blocking collectives: 97.8 us -> 114 us  [exchange(): lax.all_to_all(parts, 'head', 0, 0, axis_index_groups=groups, tiled=True)]
    all_to_all x3 -> x1, starting transfers between devices: 17.2 us -> 5.63 us  [exchange(): lax.all_to_all(parts, 'head', 0, 0, axis_index_groups=groups, tiled=True)]
    all_to_all x3 -> x1, waiting for transfers between devices: 10.6 us -> 2.44 us  [exchange(): lax.all_to_all(parts, 'head', 0, 0, axis_index_groups=groups, tiled=True)]
    unnamed x381 -> x368, local copies, waits for them, and re-layouts: 71.7 us -> 67.9 us
    pallas_call x8 -> x9, Pallas kernels: 30.3 us -> 33.5 us  [add_after(): pl.pallas_call(kernel, grid=(steps,), in_specs=[spec] * len(terms) + [pl....]
  transfers between devices with their start and end apart: 36 -> 34, of which waited for: 15 -> 11; matrix products, arithmetic and copies ran while one was open for 20% -> 20% of each run, Pallas kernels for 23% -> 24%
where the time goes in v4:
time: 765 us; the launch traced here: 755 us
  Pallas kernels  180 us (24%)
  waiting for transfers between devices  154 us (20%)
  blocking collectives  125 us (16%)
  other arithmetic  97 us (13%)
  local copies, waits for them, and re-layouts  92.2 us (12%)
  starting transfers between devices  50.5 us (7%)
  matrix products  39.8 us (5%)
  between operations  16.8 us (2%)
    all_to_all x16, blocking collectives, exchange(): lax.all_to_all(parts, 'head', 0, 0, axis_index_groups=groups, tiled=True)  114 us
    pallas_call x14, Pallas kernels, blocks_dot(): pl.pallas_call(kernel, grid_spec=pltpu.PrefetchScalarGridSpec(num_scalar_...  76 us
    unnamed x368, local copies, waits for them, and re-layouts  67.9 us
    reduce_scatter x8, waiting for transfers between devices, along_line(): lax.psum_scatter(parts, 'seq', scatter_dimension=0, axis_index_groups=gro...  51.9 us
    ppermute x11, waiting for transfers between devices, along_pair(): lax.ppermute(part, 'seq', [(k, k ^ 1) for k in range(lax.axis_size('seq'))])  40.9 us
    pallas_call x9, Pallas kernels, add_after(): pl.pallas_call(kernel, grid=(steps,), in_specs=[spec] * len(terms) + [pl....  33.5 us
    ppermute x8, waiting for transfers between devices, swap(): return lax.ppermute(part, 'head', [(k, k ^ bit) for k in range(count)])  31.7 us
    pallas_call x5, Pallas kernels, per_sequence(): pl.pallas_call(body, grid=(arrays[0].shape[0],), in_specs=[spec(a.shape)...  27.5 us
  transfers between devices with their start and end apart: 34, of which 11 were waited for; matrix products, arithmetic and copies ran while one was open for 20% of the time, Pallas kernels for 24%

profile of v4, /device:TPU:0, one launch (start us, length us, event | category | flops | bytes accessed | tf_op | source)
XLA Modules:
  0.0 755.3 jit_solution(2792795746376351056)
XLA Ops:
  88.5 7.1 all_to_all.85
  102.6 7.1 all_to_all.86
  112.7 31.7 %collective-permute-done.3 = f32[256,2048]{1,0:T(8,128)S(1)} collective-permute-done((f32[256,2048]{1,0:T(8,128)S(1)}, f32[256,2048]{1,0:T(8,128)S(1)}, u32[]{:S(2)}, u32[]{:S(2)}) %collective-permute-start.3) | collective-permute-done | bytes 2097184 | tf_op jit(solution)/shard_map/ppermute | solution.py:27
  145.2 7.7 %all_to_all.87 = f32[2,256,2048]{2,1,0:T(8,128)S(1)} all-to-all(f32[2,256,2048]{2,1,0:T(8,128)S(1)} %pad_maximum_fusion.1), channel_id=1, replica_groups={{0,1},{2,3},{4,5},{6,7},{8,9},{10,11},{12,13},{14,15},{16,17},{18,19},{..., dimensions={0} | all-to-all | bytes 8388608 | tf_op jit(solution)/shard_map/all_to_all | solution.py:601
  165.7 6.4 collective-permute-start.7
  174.3 9.4 %shard_map.206 = f32[512,2048]{1,0:T(8,128)S(1)} custom-call(bf16[512,1408]{1,0:T(8,128)(2,1)S(1)} %get-tuple-element.149.refs_0_.refs_2_, bf16[512,1408]{1,0:T(8,128)(2,1)S(1)} %get-tuple-element.150.refs_1_.refs_2_, bf16[2048,1408]{1,0:T(8,128)(2,1)} %refs_2_.1, bf16[2048,1408]{1,0:T(8,128)(2,1)} %refs_3_.3, ...), custom_call_target="tpu_custom_call" | custom-call | flops 549755813888 | bytes 1048576 | tf_op jit(solution)/shard_map/pallas_call | solution.py:410
  183.7 7.1 all_to_all.88
  197.0 7.6 %all_to_all.89 = f32[2,256,2048]{2,1,0:T(8,128)S(1)} all-to-all(f32[2,256,2048]{2,1,0:T(8,128)S(1)} %pad_maximum_fusion.2), channel_id=1, replica_groups={{0,1},{2,3},{4,5},{6,7},{8,9},{10,11},{12,13},{14,15},{16,17},{18,19},{..., dimensions={0} | all-to-all | bytes 8388608 | tf_op jit(solution)/shard_map/all_to_all | solution.py:601
  222.8 6.4 shard_map.207.refs_4_
  241.4 9.3 %shard_map.209 = f32[512,2048]{1,0:T(8,128)S(1)} custom-call(bf16[512,1408]{1,0:T(8,128)(2,1)S(1)} %copy-done.108, bf16[512,1408]{1,0:T(8,128)(2,1)S(1)} %copy-done.98, bf16[2048,1408]{1,0:T(8,128)(2,1)} %refs_2_.1, bf16[2048,1408]{1,0:T(8,128)(2,1)} %refs_3_.3, f32[1024,768]{1,0:T(8,128)} %shard_map.208.refs_4_), custom_call_target="tpu_custom_call" | custom-call | flops 549755813888 | bytes 1048576 | tf_op jit(solution)/shard_map/pallas_call | solution.py:410
  250.7 7.1 all_to_all.90
  263.2 7.1 collective-permute-done.8.refs_7_
  270.4 10.3 %shard_map.210.refs_2_ = f32[1024,1024]{1,0:T(8,128)} custom-call(s32[4]{0:T(128)S(1)} %broadcast_add_fusion.1.where_ref, bf16[512,2048]{1,0:T(8,128)(2,1)S(1)} %bitcast.166, bf16[512,2048]{1,0:T(8,128)(2,1)S(1)} %bitcast.162, f32[1024,1024]{1,0:T(8,128)} %collective-permute-done.4.refs_4_.refs_2_.refs_3_, ...), custom_call_target="tpu_custom_call" | custom-call | flops 549755813888 | bytes 1048576 | tf_op jit(solution)/shard_map/pallas_call | solution.py:301
  280.8 10.7 %reduce-scatter.9.cloned.1.call-done.refs_3_ = f32[512,384]{1,0:T(8,128)} async-done(((f32[2048,384]{1,0:T(8,128)}), f32[512,384]{1,0:T(8,128)}) %reduce-scatter.9.cloned.1.call-update) | async-done | bytes 786448 | tf_op jit(solution)/shard_map/reduce_scatter | solution.py:254
  300.1 7.5 all_to_all.91
  333.0 7.2 all_to_all.92
  362.9 19.5 %reduce-scatter.11.cloned.1.call-done.refs_5_ = f32[256,1024]{1,0:T(8,128)} async-done(((f32[1024,1024]{1,0:T(8,128)}), f32[256,1024]{1,0:T(8,128)}) %reduce-scatter.11.cloned.1.call-update) | async-done | bytes 1048592 | tf_op jit(solution)/shard_map/reduce_scatter | solution.py:254
  392.4 16.4 %collective-permute-done.12.refs_4_ = f32[1024,640]{1,0:T(8,128)} collective-permute-done((f32[1024,640]{1,0:T(8,128)}, f32[1024,640]{1,0:T(8,128)}, u32[]{:S(2)}, u32[]{:S(2)}) %collective-permute-start.12) | collective-permute-done | bytes 2621472 | tf_op jit(solution)/shard_map/ppermute | solution.py:249
  425.6 7.2 all_to_all.93
  444.9 21.9 %collective-permute-done.15.refs_11_ = f32[2,4,184,128]{3,2,1,0:T(8,128)} collective-permute-done((f32[2,4,184,128]{3,2,1,0:T(8,128)}, f32[2,4,184,128]{3,2,1,0:T(8,128)}, u32[]{:S(2)}, u32[]{:S(2)}) %collective-permute-start.15) | collective-permute-done | bytes 753696 | tf_op jit(solution)/shard_map/ppermute | solution.py:32
  472.7 12.8 %shard_map.221 = (bf16[2,512,64]{2,1,0:T(8,128)(2,1)S(1)}, bf16[2,512,64]{2,1,0:T(8,128)(2,1)S(1)}, bf16[2,512,512]{2,1,0:T(8,128)(2,1)}) custom-call(bf16[2,512,64]{2,1,0:T(8,128)(2,1)S(1)} %bitcast.181, bf16[2,512,64]{2,1,0:T(8,128)(2,1)S(1)} %bitcast.177, bf16[2,512,512]{2,1,0:T(8,128)(2,1)} %bitcast.187, f32[2,1,512]{2,1,0:T(1,128)S(1)} %copy-done.77, ...), custom_call_target="tpu_custom_call" | custom-call | flops 549755813888 | bytes 1048576 | tf_op jit(solution)/shard_map/pallas_call | solution.py:236
  505.9 18.2 %reduce-scatter.15.cloned.1.call-done.refs_7_ = f32[256,640]{1,0:T(8,128)} async-done(((f32[1024,640]{1,0:T(8,128)}), f32[256,640]{1,0:T(8,128)}) %reduce-scatter.15.cloned.1.call-update) | async-done | bytes 655376 | tf_op jit(solution)/shard_map/reduce_scatter | solution.py:254
  533.9 7.1 all_to_all.94
  551.0 7.4 all_to_all.95
  563.8 7.2 all_to_all.96
  600.6 7.2 all_to_all.97.refs_0_
  607.9 7.0 shard_map.230
  614.9 7.1 all_to_all.98
  630.8 17.4 %collective-permute-done.21.refs_2_ = f32[1024,640]{1,0:T(8,128)} collective-permute-done((f32[1024,640]{1,0:T(8,128)}, f32[1024,640]{1,0:T(8,128)}, u32[]{:S(2)}, u32[]{:S(2)}) %collective-permute-start.21) | collective-permute-done | bytes 2621472 | tf_op jit(solution)/shard_map/ppermute | solution.py:249
  667.3 8.2 %all_to_all.99.refs_2_.refs_1_ = f32[2,256,2048]{2,1,0:T(8,128)} all-to-all(f32[2,256,2048]{2,1,0:T(8,128)S(1)} %pad_maximum_fusion.7), channel_id=1, replica_groups={{0,1},{2,3},{4,5},{6,7},{8,9},{10,11},{12,13},{14,15},{16,17},{18,19},{..., dimensions={0} | all-to-all | bytes 8388608 | tf_op jit(solution)/shard_map/all_to_all | solution.py:601
  684.8 8.1 %pad_maximum_fusion = f32[2,512,2048]{2,1,0:T(8,128)} fusion(f32[2,256,2048]{2,1,0:T(8,128)} %all_to_all.99.refs_2_.refs_1_, f32[2,256,2048]{2,1,0:T(8,128)} %copy-done.2), kind=kLoop, calls=%fused_computation.5 | loop fusion | flops 2097152 | bytes 16777216 | tf_op jit(solution)/shard_map/concatenate | solution.py:792
  696.6 10.9 %all-reduce = f32[8,256]{1,0:T(8,128)S(1)} all-reduce(f32[8,256]{1,0:T(8,128)} %shard_map.235), channel_id=9, replica_groups={{0,8,16,24},{4,12,20,28},{1,9,17,25},{5,13,21,29},{2,10,18,26},{6,14,22..., use_global_device_ids=true, to_apply=%region_21.22.clone | all-reduce | flops 2048 | bytes 16384
  (590 shorter events, 404.9 us)
Async XLA Ops:
  7.2 284.3 %reduce-scatter.9.cloned.1.call-start = ((), (), s32[]{:S(2)}) async-start(), calls=%async_computation.25 | async-start | bytes 3932160 | tf_op jit(solution)/shard_map/reduce_scatter | solution.py:254
  21.0 34.2 %collective-permute-start = (f32[2,4,184,128]{3,2,1,0:T(8,128)}, f32[2,4,184,128]{3,2,1,0:T(8,128)}, u32[]{:S(2)}, u32[]{:S(2)}) collective-permute-start(f32[2,4,184,128]{3,2,1,0:T(8,128)} %shard_map.203), channel_id=1, source_target_pairs={{0,4},{4,8},{8,12},{12,16},{16,20},{20,24},{24,28},{1,5},{5,9},{9,... | collective-permute-start | bytes 2261000 | tf_op jit(solution)/shard_map/ppermute | solution.py:32
  26.7 28.4 %collective-permute-start.1 = (f32[2,4,184,128]{3,2,1,0:T(8,128)}, f32[2,4,184,128]{3,2,1,0:T(8,128)}, u32[]{:S(2)}, u32[]{:S(2)}) collective-permute-start(f32[2,4,184,128]{3,2,1,0:T(8,128)} %shard_map.203), channel_id=1, source_target_pairs={{0,8},{4,12},{8,16},{12,20},{16,24},{20,28},{1,9},{5,13},{9,17},{1... | collective-permute-start | bytes 2261000 | tf_op jit(solution)/shard_map/ppermute | solution.py:32
  45.1 129.2 %collective-permute-start.4 = (f32[1024,1024]{1,0:T(8,128)}, f32[1024,1024]{1,0:T(8,128)}, u32[]{:S(2)}, u32[]{:S(2)}) collective-permute-start(f32[1024,1024]{1,0:T(8,128)} %shard_map.205), channel_id=1, source_target_pairs={{0,4},{4,0},{8,12},{12,8},{16,20},{20,16},{24,28},{28,24},{1,5},{5... | collective-permute-start | bytes 12582920 | tf_op jit(solution)/shard_map/ppermute | solution.py:249
  58.4 18.0 %collective-permute-start.2 = (f32[2,4,184,128]{3,2,1,0:T(8,128)S(1)}, f32[2,4,184,128]{3,2,1,0:T(8,128)S(1)}, u32[]{:S(2)}, u32[]{:S(2)}) collective-permute-start(f32[2,4,184,128]{3,2,1,0:T(8,128)S(1)} %fusion.44.refs_5_.refs_8_), channel_id=1, source_target_pairs={{0,8},{4,12},{8,16},{12,20},{16,24},{20,28},{1,9},{5,13},{9,17},{1... | collective-permute-start | bytes 2261000 | tf_op jit(solution)/shard_map/ppermute | solution.py:32
  95.9 48.5 %collective-permute-start.3 = (f32[256,2048]{1,0:T(8,128)S(1)}, f32[256,2048]{1,0:T(8,128)S(1)}, u32[]{:S(2)}, u32[]{:S(2)}) collective-permute-start(f32[256,2048]{1,0:T(8,128)S(1)} %fusion.34), channel_id=1, source_target_pairs={{0,2},{1,3},{2,0},{3,1},{4,6},{5,7},{6,4},{7,5},{8,10},{9,11},{10,... | collective-permute-start | bytes 6291464 | tf_op jit(solution)/shard_map/ppermute | solution.py:27
  111.2 82.7 %collective-permute-start.6 = (f32[256,2048]{1,0:T(8,128)}, f32[256,2048]{1,0:T(8,128)}, u32[]{:S(2)}, u32[]{:S(2)}) collective-permute-start(f32[256,2048]{1,0:T(8,128)} %fusion.33), channel_id=1, source_target_pairs={{0,2},{1,3},{2,0},{3,1},{4,6},{5,7},{6,4},{7,5},{8,10},{9,11},{10,... | collective-permute-start | bytes 6291464 | tf_op jit(solution)/shard_map/ppermute | solution.py:27
  165.7 97.6 %collective-permute-start.7 = (f32[512,1024]{1,0:T(8,128)}, f32[512,1024]{1,0:T(8,128)}, u32[]{:S(2)}, u32[]{:S(2)}) collective-permute-start(f32[512,1024]{1,0:T(8,128)} %slice_convert_fusion.1), channel_id=1, source_target_pairs={{0,4},{4,0},{8,12},{12,8},{16,20},{20,16},{24,28},{28,24},{1,5},{5... | collective-permute-start | bytes 6291464 | tf_op jit(solution)/shard_map/ppermute | solution.py:249
  192.5 88.3 %collective-permute-start.5 = (f32[256,2048]{1,0:T(8,128)}, f32[256,2048]{1,0:T(8,128)}, u32[]{:S(2)}, u32[]{:S(2)}) collective-permute-start(f32[256,2048]{1,0:T(8,128)} %fusion.32.refs_0_), channel_id=1, source_target_pairs={{0,2},{1,3},{2,0},{3,1},{4,6},{5,7},{6,4},{7,5},{8,10},{9,11},{10,... | collective-permute-start | bytes 6291464 | tf_op jit(solution)/shard_map/ppermute | solution.py:27
  221.5 48.8 %collective-permute-start.8 = (f32[512,1024]{1,0:T(8,128)}, f32[512,1024]{1,0:T(8,128)}, u32[]{:S(2)}, u32[]{:S(2)}) collective-permute-start(f32[512,1024]{1,0:T(8,128)} %slice_convert_fusion.refs_4_), channel_id=1, source_target_pairs={{0,4},{4,0},{8,12},{12,8},{16,20},{20,16},{24,28},{28,24},{1,5},{5... | collective-permute-start | bytes 6291464 | tf_op jit(solution)/shard_map/ppermute | solution.py:249
  229.2 153.2 %reduce-scatter.11.cloned.1.call-start = ((), (), s32[]{:S(2)}) async-start(), calls=%async_computation.26 | async-start | bytes 5242880 | tf_op jit(solution)/shard_map/reduce_scatter | solution.py:254
  240.2 113.1 %collective-permute-start.13 = (f32[1024,768]{1,0:T(8,128)}, f32[1024,768]{1,0:T(8,128)}, u32[]{:S(2)}, u32[]{:S(2)}) collective-permute-start(f32[1024,768]{1,0:T(8,128)} %shard_map.208.refs_4_), channel_id=1, source_target_pairs={{0,4},{4,0},{8,12},{12,8},{16,20},{20,16},{24,28},{28,24},{1,5},{5... | collective-permute-start | bytes 9437192 | tf_op jit(solution)/shard_map/ppermute | solution.py:249
  259.5 64.7 %collective-permute-start.9 = (f32[256,2048]{1,0:T(8,128)}, f32[256,2048]{1,0:T(8,128)}, u32[]{:S(2)}, u32[]{:S(2)}) collective-permute-start(f32[256,2048]{1,0:T(8,128)} %fusion.31.refs_8_.refs_0_), channel_id=1, source_target_pairs={{0,2},{1,3},{2,0},{3,1},{4,6},{5,7},{6,4},{7,5},{8,10},{9,11},{10,... | collective-permute-start | bytes 6291464 | tf_op jit(solution)/shard_map/ppermute | solution.py:27
  280.7 189.8 %reduce-scatter.13.cloned.1.call-start = ((), (), s32[]{:S(2)}) async-start(), calls=%async_computation.27 | async-start | bytes 3932160 | tf_op jit(solution)/shard_map/reduce_scatter | solution.py:254
  318.8 90.0 %collective-permute-start.12 = (f32[1024,640]{1,0:T(8,128)}, f32[1024,640]{1,0:T(8,128)}, u32[]{:S(2)}, u32[]{:S(2)}) collective-permute-start(f32[1024,640]{1,0:T(8,128)} %shard_map.212.refs_2_), channel_id=1, source_target_pairs={{0,4},{4,0},{8,12},{12,8},{16,20},{20,16},{24,28},{28,24},{1,5},{5... | collective-permute-start | bytes 7864328 | tf_op jit(solution)/shard_map/ppermute | solution.py:249
  350.8 64.4 %collective-permute-start.10 = (f32[2,4,184,128]{3,2,1,0:T(8,128)}, f32[2,4,184,128]{3,2,1,0:T(8,128)}, u32[]{:S(2)}, u32[]{:S(2)}) collective-permute-start(f32[2,4,184,128]{3,2,1,0:T(8,128)} %shard_map.214.refs_5_), channel_id=1, source_target_pairs={{4,0},{8,4},{12,8},{16,12},{20,16},{24,20},{28,24},{5,1},{9,5},{13... | collective-permute-start | bytes 2261000 | tf_op jit(solution)/shard_map/ppermute | solution.py:32
  352.1 63.1 %collective-permute-start.11 = (f32[2,4,184,128]{3,2,1,0:T(8,128)}, f32[2,4,184,128]{3,2,1,0:T(8,128)}, u32[]{:S(2)}, u32[]{:S(2)}) collective-permute-start(f32[2,4,184,128]{3,2,1,0:T(8,128)} %shard_map.214.refs_5_), channel_id=1, source_target_pairs={{8,0},{12,4},{16,8},{20,12},{24,16},{28,20},{9,1},{13,5},{17,9},{2... | collective-permute-start | bytes 2261000 | tf_op jit(solution)/shard_map/ppermute | solution.py:32
  359.6 164.6 %reduce-scatter.15.cloned.1.call-start = ((), (), s32[]{:S(2)}) async-start(), calls=%async_computation.28 | async-start | bytes 3276800 | tf_op jit(solution)/shard_map/reduce_scatter | solution.py:254
  392.4 98.8 %collective-permute-start.16 = (f32[1024,768]{1,0:T(8,128)}, f32[1024,768]{1,0:T(8,128)}, u32[]{:S(2)}, u32[]{:S(2)}) collective-permute-start(f32[1024,768]{1,0:T(8,128)} %shard_map.216.refs_5_), channel_id=1, source_target_pairs={{0,4},{4,0},{8,12},{12,8},{16,20},{20,16},{24,28},{28,24},{1,5},{5... | collective-permute-start | bytes 9437192 | tf_op jit(solution)/shard_map/ppermute | solution.py:249
  419.4 47.4 %collective-permute-start.15 = (f32[2,4,184,128]{3,2,1,0:T(8,128)}, f32[2,4,184,128]{3,2,1,0:T(8,128)}, u32[]{:S(2)}, u32[]{:S(2)}) collective-permute-start(f32[2,4,184,128]{3,2,1,0:T(8,128)} %shard_map.218.refs_0_.refs_10_), channel_id=1, source_target_pairs={{8,0},{12,4},{16,8},{20,12},{24,16},{28,20},{9,1},{13,5},{17,9},{2... | collective-permute-start | bytes 2261000 | tf_op jit(solution)/shard_map/ppermute | solution.py:32
  440.5 103.7 %collective-permute-start.14 = (f32[256,2048]{1,0:T(8,128)}, f32[256,2048]{1,0:T(8,128)}, u32[]{:S(2)}, u32[]{:S(2)}) collective-permute-start(f32[256,2048]{1,0:T(8,128)} %fusion.26.refs_4_.refs_0_), channel_id=1, source_target_pairs={{0,2},{1,3},{2,0},{3,1},{4,6},{5,7},{6,4},{7,5},{8,10},{9,11},{10,... | collective-permute-start | bytes 6291464 | tf_op jit(solution)/shard_map/ppermute | solution.py:27
  442.1 150.1 %reduce-scatter.17.cloned.1.call-start = ((), (), s32[]{:S(2)}) async-start(), calls=%async_computation.29 | async-start | bytes 3932160 | tf_op jit(solution)/shard_map/reduce_scatter | solution.py:254
  442.3 130.9 %collective-permute-start.18 = (f32[1024,640]{1,0:T(8,128)}, f32[1024,640]{1,0:T(8,128)}, u32[]{:S(2)}, u32[]{:S(2)}) collective-permute-start(f32[1024,640]{1,0:T(8,128)} %shard_map.220.refs_12_), channel_id=1, source_target_pairs={{0,4},{4,0},{8,12},{12,8},{16,20},{20,16},{24,28},{28,24},{1,5},{5... | collective-permute-start | bytes 7864328 | tf_op jit(solution)/shard_map/ppermute | solution.py:249
  498.7 149.6 %reduce-scatter.19.cloned.1.call-start = ((), (), s32[]{:S(2)}) async-start(), calls=%async_computation.30 | async-start | bytes 3276800 | tf_op jit(solution)/shard_map/reduce_scatter | solution.py:254
  505.9 118.5 %collective-permute-start.22 = (f32[1024,512]{1,0:T(8,128)}, f32[1024,512]{1,0:T(8,128)}, u32[]{:S(2)}, u32[]{:S(2)}) collective-permute-start(f32[1024,512]{1,0:T(8,128)} %shard_map.223.refs_6_), channel_id=1, source_target_pairs={{0,4},{4,0},{8,12},{12,8},{16,20},{20,16},{24,28},{28,24},{1,5},{5... | collective-permute-start | bytes 6291464 | tf_op jit(solution)/shard_map/ppermute | solution.py:249
  542.8 49.4 %collective-permute-start.17 = (f32[256,2048]{1,0:T(8,128)}, f32[256,2048]{1,0:T(8,128)}, u32[]{:S(2)}, u32[]{:S(2)}) collective-permute-start(f32[256,2048]{1,0:T(8,128)} %fusion.25.refs_2_.refs_0_), channel_id=1, source_target_pairs={{0,2},{1,3},{2,0},{3,1},{4,6},{5,7},{6,4},{7,5},{8,10},{9,11},{10,... | collective-permute-start | bytes 6291464 | tf_op jit(solution)/shard_map/ppermute | solution.py:27
  572.8 86.3 %collective-permute-start.20 = (f32[256,2048]{1,0:T(8,128)}, f32[256,2048]{1,0:T(8,128)}, u32[]{:S(2)}, u32[]{:S(2)}) collective-permute-start(f32[256,2048]{1,0:T(8,128)} %fusion.24.refs_5_.refs_0_), channel_id=1, source_target_pairs={{0,2},{1,3},{2,0},{3,1},{4,6},{5,7},{6,4},{7,5},{8,10},{9,11},{10,... | collective-permute-start | bytes 6291464 | tf_op jit(solution)/shard_map/ppermute | solution.py:27
  589.0 59.2 %collective-permute-start.21 = (f32[1024,640]{1,0:T(8,128)}, f32[1024,640]{1,0:T(8,128)}, u32[]{:S(2)}, u32[]{:S(2)}) collective-permute-start(f32[1024,640]{1,0:T(8,128)} %shard_map.228.refs_2_), channel_id=1, source_target_pairs={{0,4},{4,0},{8,12},{12,8},{16,20},{20,16},{24,28},{28,24},{1,5},{5... | collective-permute-start | bytes 7864328 | tf_op jit(solution)/shard_map/ppermute | solution.py:249
  590.6 117.5 %reduce-scatter.21.cloned.1.call-start = ((), (), s32[]{:S(2)}) async-start(), calls=%async_computation.31 | async-start | bytes 2621440 | tf_op jit(solution)/shard_map/reduce_scatter | solution.py:254
  623.7 84.4 %collective-permute-start.19 = (f32[256,2048]{1,0:T(8,128)}, f32[256,2048]{1,0:T(8,128)}, u32[]{:S(2)}, u32[]{:S(2)}) collective-permute-start(f32[256,2048]{1,0:T(8,128)} %fusion.23.refs_5_.refs_0_), channel_id=1, source_target_pairs={{0,2},{1,3},{2,0},{3,1},{4,6},{5,7},{6,4},{7,5},{8,10},{9,11},{10,... | collective-permute-start | bytes 6291464 | tf_op jit(solution)/shard_map/ppermute | solution.py:27
  630.7 112.9 %reduce-scatter.23.cloned.1.call-start = ((), (), s32[]{:S(2)}) async-start(), calls=%async_computation.32 | async-start | bytes 3276800 | tf_op jit(solution)/shard_map/reduce_scatter | solution.py:254
  678.7 54.0 %collective-permute-start.24 = (f32[256,384]{1,0:T(8,128)}, f32[256,384]{1,0:T(8,128)}, u32[]{:S(2)}, u32[]{:S(2)}) collective-permute-start(f32[256,384]{1,0:T(8,128)} %shard_map.237), channel_id=1, source_target_pairs={{0,4},{4,0},{8,12},{12,8},{16,20},{20,16},{24,28},{28,24},{1,5},{5... | collective-permute-start | bytes 1179656 | tf_op jit(solution)/shard_map/ppermute | solution.py:249
  (183 other events, 1308.9 us)
Sparse Core Ops, SparseCore 0:
  229.4 62.0 reduce-scatter.8
  294.3 88.0 reduce-scatter.10
  384.8 85.5 reduce-scatter.12
  472.7 51.3 reduce-scatter.14
  527.0 59.8 reduce-scatter.16
  590.7 50.5 reduce-scatter.18
  643.7 43.5 reduce-scatter.20
  689.6 51.8 reduce-scatter.22

commit v5 on v4

--- a/solution.py
+++ b/solution.py
@@ -15,8 +15,8 @@
 
 MAPPED = 160
 NORM = MAPPED
-META = MAPPED + 16
-ROWS = META + 8
+META = MAPPED + 2
+ROWS = MAPPED + 8
 FIRST, LAST, CARRIED, NEXT = META, META + 1, META + 2, META + 3
 
 LONG = pl.CostEstimate(flops=1 << 39, bytes_accessed=1 << 20, transcendentals=0)
@@ -92,21 +92,20 @@
     return lax.dot_general(left, right, (((a,), (b,)), ((), ())), preferred_element_type=jnp.float32)
 
 
-def put_state(out_ref, h, mapped, right, weights):
+def put_state(out_ref, h, mapped, right, weights, meta):
     mapped = low(mapped)
     out_ref[0, h, :MAPPED, :] = dot_general(mapped, right, 1, 0)
     norm = dot_general(weights, mapped, 0, 1)
-    out_ref[0, h, NORM : NORM + 8, :] = norm[:, :128]
-    out_ref[0, h, NORM + 8 : NORM + 16, :] = jnp.concatenate(
-        [norm[:, 128:], jnp.zeros((8, 256 - MAPPED), jnp.float32)], 1
-    )
+    rest = jnp.concatenate([norm[:, 128:], jnp.zeros((8, 256 - MAPPED), jnp.float32)], 1)
+    at = lax.broadcasted_iota(jnp.int32, (8, HEAD_V), 0)
+    out_ref[0, h, NORM:, :] = jnp.where(at == 0, norm[:, :128], jnp.where(at == 1, rest, meta))
 
 
 def get_state(refs, h):
     two, four = refs
     joined = two[0, h] + two[0, h, NEXT : NEXT + 1, :1] * four[0, h, CARRIED : CARRIED + 1, :1] * four[0, h]
-    norm = jnp.concatenate([joined[NORM : NORM + 8], joined[NORM + 8 : NORM + 16, : MAPPED - 128]], 1)
-    return low(joined[:MAPPED]), low(norm)
+    norm = jnp.concatenate([joined[NORM : NORM + 1], joined[NORM + 1 : NORM + 2, : MAPPED - 128]], 1)
+    return low(joined[:MAPPED]), low(jnp.broadcast_to(norm, (8, MAPPED)))
 
 
 def transposed(ref):
@@ -121,8 +120,7 @@
     ones = jnp.ones((key_ref.shape[1], 8), jnp.bfloat16)
     for h in range(heads):
         mapped = features(key_t[FEAT * h : FEAT * (h + 1)]) * tail
-        put_state(out_ref, h, mapped, value_ref[0, :, HEAD_V * h : HEAD_V * (h + 1)], ones)
-        out_ref[0, h, META:, :] = meta_ref[0]
+        put_state(out_ref, h, mapped, value_ref[0, :, HEAD_V * h : HEAD_V * (h + 1)], ones, meta_ref[0])
 
 
 def seen(row_ref, column_ref):
@@ -170,8 +168,7 @@
     for h in range(heads):
         d_numer, d_denom = numer_back(h, d_mixed_ref, ratio_ref, denom_ref)
         mapped = features(query_t[FEAT * h : FEAT * (h + 1)]) * uses
-        put_state(out_ref, h, mapped, d_numer, low(jnp.broadcast_to(d_denom, (d_denom.shape[0], 8))))
-        out_ref[0, h, META:, :] = meta_ref[0]
+        put_state(out_ref, h, mapped, d_numer, low(jnp.broadcast_to(d_denom, (d_denom.shape[0], 8))), meta_ref[0])
 
 
 def join_back_kernel(near_ref, far_ref, carried_ref, out_ref):
@@ -539,7 +536,7 @@
         at = jnp.arange(8)[None, :, None]
         total = jnp.zeros((seq_count, 8, 128), jnp.float32)
         for k, value in enumerate(values):
-            total = jnp.where(at == k, value[:, None, None], total)
+            total = jnp.where(at == k + META - NORM, value[:, None, None], total)
         return total
 
     resid = tokens.astype(jnp.float32)
@@ -741,12 +738,12 @@
         return head_part(work, d_query[:, s], d_key[:, s], d_value[:, s])
 
     up_a.line([d_query])
-    out = PairFirst(d_branches, mixed_rows, (0, wide), [up_a.whole])
-    in_0 = in_part(0, [out.sent, gate_b.sum])
+    qkv_right = flat(jnp.concatenate([d_query, d_key, d_value], -1))
+    qkv = PairFirst([h_rows], [qkv_right], (0, qkv_right.shape[1]), [up_a.whole])
+    in_0 = in_part(0, [qkv.sent, gate_b.sum])
     outcome(0, out_0, [in_0[0]])
     in_1 = in_part(1, [results[0]])
     up_b.line([in_1[0]])
-    qkv_right = flat(jnp.concatenate([d_query, d_key, d_value], -1))
 
     d_tokens = []
 
@@ -760,12 +757,12 @@
         d_tokens.append(d_part)
         return d_gain
 
-    qkv = PairFirst([h_rows], [qkv_right], (0, qkv_right.shape[1]), [up_b.whole])
-    d_gain_attn = first_back(0, in_0, [qkv.sent, up_a.sum])
+    out = PairFirst(d_branches, mixed_rows, (0, wide), [up_b.whole])
+    d_gain_attn = first_back(0, in_0, [out.sent, up_a.sum])
     out_1 = out_part(1, [d_tokens[0]])
-    out.line([out_1[0]])
-    qkv.line([out.whole, up_b.sum])
-    d_gain_attn = d_gain_attn + first_back(1, in_1, [qkv.whole])
+    qkv.line([out_1[0]])
+    out.line([qkv.whole, up_b.sum])
+    d_gain_attn = d_gain_attn + first_back(1, in_1, [out.whole])
     down_b.pair([d_tokens[1]])
     count = lax.axis_size("seq")
 
@@ -784,9 +781,9 @@
         gains = along_line(add_after((gains[0], gains_came), [d_tokens[1]]))
     else:
         gains = lax.psum_scatter(gains, "seq", scatter_dimension=1, tiled=True)
-    outcome(1, out_1, [d_tokens[1], out.sum])
+    outcome(1, out_1, [d_tokens[1], qkv.sum])
     down_b.end([results[1]])
-    output_weight_gradient = transposed_after([out.sum], [qkv.whole])
+    output_weight_gradient = transposed_after([out.sum], [results[1]])
     qkv = qkv.sum
     result = jnp.concatenate(results, 1)
     d_tokens = jnp.concatenate(d_tokens, 1)

time: 765 us -> 753 us (0.984)
  other arithmetic: 97 us -> 89.2 us
    reduce_scatter x8, waiting for transfers between devices: 51.9 us -> 68.9 us  [along_line(): lax.psum_scatter(parts, 'seq', scatter_dimension=0, axis_index_groups=gro...]
    ppermute x11, waiting for transfers between devices: 40.9 us -> 28.8 us  [along_pair(): lax.ppermute(part, 'seq', [(k, k ^ 1) for k in range(lax.axis_size('seq'))])]
    all_to_all x16 -> x17, blocking collectives: 114 us -> 121 us  [exchange(): lax.all_to_all(parts, 'head', 0, 0, axis_index_groups=groups, tiled=True)]
    unnamed x368 -> x374, local copies, waits for them, and re-layouts: 67.9 us -> 65.1 us
  transfers between devices with their start and end apart: 34 -> 33, of which waited for: 11 -> 12; matrix products, arithmetic and copies ran while one was open for 20% -> 20% of each run, Pallas kernels for 24% -> 24%
where the time goes in v5:
time: 753 us; the launch traced here: 744 us
  Pallas kernels  180 us (24%)
  waiting for transfers between devices  152 us (20%)
  blocking collectives  132 us (18%)
  local copies, waits for them, and re-layouts  90.2 us (12%)
  other arithmetic  89.2 us (12%)
  starting transfers between devices  43.2 us (6%)
  matrix products  39.7 us (5%)
  between operations  16.8 us (2%)
    all_to_all x17, blocking collectives, exchange(): lax.all_to_all(parts, 'head', 0, 0, axis_index_groups=groups, tiled=True)  121 us
    pallas_call x14, Pallas kernels, blocks_dot(): pl.pallas_call(kernel, grid_spec=pltpu.PrefetchScalarGridSpec(num_scalar_...  75.9 us
    reduce_scatter x8, waiting for transfers between devices, along_line(): lax.psum_scatter(parts, 'seq', scatter_dimension=0, axis_index_groups=gro...  68.9 us
    unnamed x374, local copies, waits for them, and re-layouts  65.1 us
    pallas_call x9, Pallas kernels, add_after(): pl.pallas_call(kernel, grid=(steps,), in_specs=[spec] * len(terms) + [pl....  33.4 us
    ppermute x8, waiting for transfers between devices, swap(): return lax.ppermute(part, 'head', [(k, k ^ bit) for k in range(count)])  31.7 us
    ppermute x11, waiting for transfers between devices, along_pair(): lax.ppermute(part, 'seq', [(k, k ^ 1) for k in range(lax.axis_size('seq'))])  28.8 us
    pallas_call x5, Pallas kernels, per_sequence(): pl.pallas_call(body, grid=(arrays[0].shape[0],), in_specs=[spec(a.shape)...  27.4 us
  transfers between devices with their start and end apart: 33, of which 12 were waited for; matrix products, arithmetic and copies ran while one was open for 20% of the time, Pallas kernels for 24%

profile of v5, /device:TPU:0, one launch (start us, length us, event | category | flops | bytes accessed | tf_op | source)
XLA Modules:
  0.0 743.5 jit_solution(3952173589124206309)
XLA Ops:
  87.0 7.1 all_to_all.85
  101.1 7.1 all_to_all.86
  111.3 31.6 %collective-permute-done.3 = f32[256,2048]{1,0:T(8,128)S(1)} collective-permute-done((f32[256,2048]{1,0:T(8,128)S(1)}, f32[256,2048]{1,0:T(8,128)S(1)}, u32[]{:S(2)}, u32[]{:S(2)}) %collective-permute-start.3) | collective-permute-done | bytes 2097184 | tf_op jit(solution)/shard_map/ppermute | solution.py:27
  143.7 7.7 %all_to_all.87 = f32[2,256,2048]{2,1,0:T(8,128)S(1)} all-to-all(f32[2,256,2048]{2,1,0:T(8,128)S(1)} %pad_maximum_fusion.1), channel_id=1, replica_groups={{0,1},{2,3},{4,5},{6,7},{8,9},{10,11},{12,13},{14,15},{16,17},{18,19},{..., dimensions={0} | all-to-all | bytes 8388608 | tf_op jit(solution)/shard_map/all_to_all | solution.py:598
  170.0 9.4 %shard_map.206 = f32[512,2048]{1,0:T(8,128)S(1)} custom-call(bf16[512,1408]{1,0:T(8,128)(2,1)S(1)} %get-tuple-element.149.refs_0_.refs_2_, bf16[512,1408]{1,0:T(8,128)(2,1)S(1)} %get-tuple-element.150.refs_1_.refs_2_, bf16[2048,1408]{1,0:T(8,128)(2,1)} %refs_2_.1, bf16[2048,1408]{1,0:T(8,128)(2,1)} %refs_3_.3, ...), custom_call_target="tpu_custom_call" | custom-call | flops 549755813888 | bytes 1048576 | tf_op jit(solution)/shard_map/pallas_call | solution.py:407
  179.4 7.1 all_to_all.88
  192.7 7.6 %all_to_all.89 = f32[2,256,2048]{2,1,0:T(8,128)S(1)} all-to-all(f32[2,256,2048]{2,1,0:T(8,128)S(1)} %pad_maximum_fusion.2), channel_id=1, replica_groups={{0,1},{2,3},{4,5},{6,7},{8,9},{10,11},{12,13},{14,15},{16,17},{18,19},{..., dimensions={0} | all-to-all | bytes 8388608 | tf_op jit(solution)/shard_map/all_to_all | solution.py:598
  237.0 9.3 %shard_map.209 = f32[512,2048]{1,0:T(8,128)S(1)} custom-call(bf16[512,1408]{1,0:T(8,128)(2,1)S(1)} %copy-done.110, bf16[512,1408]{1,0:T(8,128)(2,1)S(1)} %copy-done.100, bf16[2048,1408]{1,0:T(8,128)(2,1)} %refs_2_.1, bf16[2048,1408]{1,0:T(8,128)(2,1)} %refs_3_.3, f32[1024,768]{1,0:T(8,128)} %shard_map.208.refs_4_), custom_call_target="tpu_custom_call" | custom-call | flops 549755813888 | bytes 1048576 | tf_op jit(solution)/shard_map/pallas_call | solution.py:407
  246.3 7.1 all_to_all.90
  258.9 7.2 collective-permute-done.8.refs_7_
  266.1 10.3 %shard_map.210.refs_2_ = f32[1024,1024]{1,0:T(8,128)} custom-call(s32[4]{0:T(128)S(1)} %broadcast_add_fusion.1.where_ref, bf16[512,2048]{1,0:T(8,128)(2,1)S(1)} %bitcast.166, bf16[512,2048]{1,0:T(8,128)(2,1)S(1)} %bitcast.162, f32[1024,1024]{1,0:T(8,128)} %collective-permute-done.4.refs_4_.refs_2_.refs_3_, ...), custom_call_target="tpu_custom_call" | custom-call | flops 549755813888 | bytes 1048576 | tf_op jit(solution)/shard_map/pallas_call | solution.py:298
  276.5 10.6 %reduce-scatter.9.cloned.1.call-done.refs_3_ = f32[512,384]{1,0:T(8,128)} async-done(((f32[2048,384]{1,0:T(8,128)}), f32[512,384]{1,0:T(8,128)}) %reduce-scatter.9.cloned.1.call-update) | async-done | bytes 786448 | tf_op jit(solution)/shard_map/reduce_scatter | solution.py:251
  295.8 7.5 %all_to_all.91 = f32[2,256,2048]{2,1,0:T(8,128)S(1)} all-to-all(f32[2,256,2048]{2,1,0:T(8,128)S(1)} %pad_maximum_fusion.3), channel_id=1, replica_groups={{0,1},{2,3},{4,5},{6,7},{8,9},{10,11},{12,13},{14,15},{16,17},{18,19},{..., dimensions={0} | all-to-all | bytes 8388608 | tf_op jit(solution)/shard_map/all_to_all | solution.py:598
  328.6 7.2 all_to_all.92
  358.5 19.7 %reduce-scatter.11.cloned.1.call-done.refs_5_ = f32[256,1024]{1,0:T(8,128)} async-done(((f32[1024,1024]{1,0:T(8,128)}), f32[256,1024]{1,0:T(8,128)}) %reduce-scatter.11.cloned.1.call-update) | async-done | bytes 1048592 | tf_op jit(solution)/shard_map/reduce_scatter | solution.py:251
  388.1 14.9 %collective-permute-done.12.refs_4_ = f32[1024,640]{1,0:T(8,128)} collective-permute-done((f32[1024,640]{1,0:T(8,128)}, f32[1024,640]{1,0:T(8,128)}, u32[]{:S(2)}, u32[]{:S(2)}) %collective-permute-start.12) | collective-permute-done | bytes 2621472 | tf_op jit(solution)/shard_map/ppermute | solution.py:246
  419.7 7.2 all_to_all.93
  439.1 19.1 %collective-permute-done.15.refs_11_ = f32[2,4,168,128]{3,2,1,0:T(8,128)} collective-permute-done((f32[2,4,168,128]{3,2,1,0:T(8,128)}, f32[2,4,168,128]{3,2,1,0:T(8,128)}, u32[]{:S(2)}, u32[]{:S(2)}) %collective-permute-start.15) | collective-permute-done | bytes 688160 | tf_op jit(solution)/shard_map/ppermute | solution.py:32
  464.2 12.7 %shard_map.221 = (bf16[2,512,64]{2,1,0:T(8,128)(2,1)S(1)}, bf16[2,512,64]{2,1,0:T(8,128)(2,1)S(1)}, bf16[2,512,512]{2,1,0:T(8,128)(2,1)}) custom-call(bf16[2,512,64]{2,1,0:T(8,128)(2,1)S(1)} %bitcast.181, bf16[2,512,64]{2,1,0:T(8,128)(2,1)S(1)} %bitcast.177, bf16[2,512,512]{2,1,0:T(8,128)(2,1)} %bitcast.187, f32[2,1,512]{2,1,0:T(1,128)S(1)} %copy-done.77, ...), custom_call_target="tpu_custom_call" | custom-call | flops 549755813888 | bytes 1048576 | tf_op jit(solution)/shard_map/pallas_call | solution.py:233
  498.4 17.3 %reduce-scatter.15.cloned.1.call-done.refs_7_ = f32[256,640]{1,0:T(8,128)} async-done(((f32[1024,640]{1,0:T(8,128)}), f32[256,640]{1,0:T(8,128)}) %reduce-scatter.15.cloned.1.call-update) | async-done | bytes 655376 | tf_op jit(solution)/shard_map/reduce_scatter | solution.py:251
  524.2 7.1 all_to_all.94
  541.2 7.4 all_to_all.95
  553.5 7.2 all_to_all.96
  590.4 7.2 all_to_all.97.refs_0_
  597.6 7.0 shard_map.230
  604.6 7.1 all_to_all.98
  621.6 6.7 collective-permute-done.21.refs_4_
  649.4 8.2 %all_to_all.99.refs_2_.refs_1_ = f32[2,256,2048]{2,1,0:T(8,128)} all-to-all(f32[2,256,2048]{2,1,0:T(8,128)S(1)} %pad_maximum_fusion.7), channel_id=1, replica_groups={{0,1},{2,3},{4,5},{6,7},{8,9},{10,11},{12,13},{14,15},{16,17},{18,19},{..., dimensions={0} | all-to-all | bytes 8388608 | tf_op jit(solution)/shard_map/all_to_all | solution.py:598
  666.8 8.0 %pad_maximum_fusion = f32[2,512,2048]{2,1,0:T(8,128)} fusion(f32[2,256,2048]{2,1,0:T(8,128)} %all_to_all.99.refs_2_.refs_1_, f32[2,256,2048]{2,1,0:T(8,128)} %copy-done.2), kind=kLoop, calls=%fused_computation.5 | loop fusion | flops 2097152 | bytes 16777216 | tf_op jit(solution)/shard_map/concatenate | solution.py:789
  678.6 10.9 %all-reduce = f32[8,256]{1,0:T(8,128)S(1)} all-reduce(f32[8,256]{1,0:T(8,128)} %shard_map.235), channel_id=9, replica_groups={{0,8,16,24},{4,12,20,28},{1,9,17,25},{5,13,21,29},{2,10,18,26},{6,14,22..., use_global_device_ids=true, to_apply=%region_21.22.clone | all-reduce | flops 2048 | bytes 16384
  696.9 7.4 all_to_all.101
  720.8 13.2 %reduce-scatter.23.cloned.1.call-done.refs_0_ = f32[256,512]{1,0:T(8,128)} async-done(((f32[1024,512]{1,0:T(8,128)}), f32[256,512]{1,0:T(8,128)}) %reduce-scatter.23.cloned.1.call-update) | async-done | bytes 524304 | tf_op jit(solution)/shard_map/reduce_scatter | solution.py:251
  (595 shorter events, 401.4 us)
Async XLA Ops:
  7.2 279.9 %reduce-scatter.9.cloned.1.call-start = ((), (), s32[]{:S(2)}) async-start(), calls=%async_computation.25 | async-start | bytes 3932160 | tf_op jit(solution)/shard_map/reduce_scatter | solution.py:251
  21.0 34.2 %collective-permute-start = (f32[2,4,168,128]{3,2,1,0:T(8,128)}, f32[2,4,168,128]{3,2,1,0:T(8,128)}, u32[]{:S(2)}, u32[]{:S(2)}) collective-permute-start(f32[2,4,168,128]{3,2,1,0:T(8,128)} %shard_map.203), channel_id=1, source_target_pairs={{0,4},{4,8},{8,12},{12,16},{16,20},{20,24},{24,28},{1,5},{5,9},{9,... | collective-permute-start | bytes 2064392 | tf_op jit(solution)/shard_map/ppermute | solution.py:32
  26.7 28.4 %collective-permute-start.1 = (f32[2,4,168,128]{3,2,1,0:T(8,128)}, f32[2,4,168,128]{3,2,1,0:T(8,128)}, u32[]{:S(2)}, u32[]{:S(2)}) collective-permute-start(f32[2,4,168,128]{3,2,1,0:T(8,128)} %shard_map.203), channel_id=1, source_target_pairs={{0,8},{4,12},{8,16},{12,20},{16,24},{20,28},{1,9},{5,13},{9,17},{1... | collective-permute-start | bytes 2064392 | tf_op jit(solution)/shard_map/ppermute | solution.py:32
  45.0 125.0 %collective-permute-start.4 = (f32[1024,1024]{1,0:T(8,128)}, f32[1024,1024]{1,0:T(8,128)}, u32[]{:S(2)}, u32[]{:S(2)}) collective-permute-start(f32[1024,1024]{1,0:T(8,128)} %shard_map.205), channel_id=1, source_target_pairs={{0,4},{4,0},{8,12},{12,8},{16,20},{20,16},{24,28},{28,24},{1,5},{5... | collective-permute-start | bytes 12582920 | tf_op jit(solution)/shard_map/ppermute | solution.py:246
  58.2 16.6 %collective-permute-start.2 = (f32[2,4,168,128]{3,2,1,0:T(8,128)S(1)}, f32[2,4,168,128]{3,2,1,0:T(8,128)S(1)}, u32[]{:S(2)}, u32[]{:S(2)}) collective-permute-start(f32[2,4,168,128]{3,2,1,0:T(8,128)S(1)} %fusion.44.refs_5_.refs_8_), channel_id=1, source_target_pairs={{0,8},{4,12},{8,16},{12,20},{16,24},{20,28},{1,9},{5,13},{9,17},{1... | collective-permute-start | bytes 2064392 | tf_op jit(solution)/shard_map/ppermute | solution.py:32
  94.4 48.5 %collective-permute-start.3 = (f32[256,2048]{1,0:T(8,128)S(1)}, f32[256,2048]{1,0:T(8,128)S(1)}, u32[]{:S(2)}, u32[]{:S(2)}) collective-permute-start(f32[256,2048]{1,0:T(8,128)S(1)} %fusion.34), channel_id=1, source_target_pairs={{0,2},{1,3},{2,0},{3,1},{4,6},{5,7},{6,4},{7,5},{8,10},{9,11},{10,... | collective-permute-start | bytes 6291464 | tf_op jit(solution)/shard_map/ppermute | solution.py:27
  109.8 79.9 %collective-permute-start.6 = (f32[256,2048]{1,0:T(8,128)}, f32[256,2048]{1,0:T(8,128)}, u32[]{:S(2)}, u32[]{:S(2)}) collective-permute-start(f32[256,2048]{1,0:T(8,128)} %fusion.33), channel_id=1, source_target_pairs={{0,2},{1,3},{2,0},{3,1},{4,6},{5,7},{6,4},{7,5},{8,10},{9,11},{10,... | collective-permute-start | bytes 6291464 | tf_op jit(solution)/shard_map/ppermute | solution.py:27
  164.2 94.7 %collective-permute-start.7 = (f32[512,1024]{1,0:T(8,128)}, f32[512,1024]{1,0:T(8,128)}, u32[]{:S(2)}, u32[]{:S(2)}) collective-permute-start(f32[512,1024]{1,0:T(8,128)} %slice_convert_fusion.1), channel_id=1, source_target_pairs={{0,4},{4,0},{8,12},{12,8},{16,20},{20,16},{24,28},{28,24},{1,5},{5... | collective-permute-start | bytes 6291464 | tf_op jit(solution)/shard_map/ppermute | solution.py:246
  188.2 88.3 %collective-permute-start.5 = (f32[256,2048]{1,0:T(8,128)}, f32[256,2048]{1,0:T(8,128)}, u32[]{:S(2)}, u32[]{:S(2)}) collective-permute-start(f32[256,2048]{1,0:T(8,128)} %fusion.32.refs_0_), channel_id=1, source_target_pairs={{0,2},{1,3},{2,0},{3,1},{4,6},{5,7},{6,4},{7,5},{8,10},{9,11},{10,... | collective-permute-start | bytes 6291464 | tf_op jit(solution)/shard_map/ppermute | solution.py:27
  217.3 48.8 %collective-permute-start.8 = (f32[512,1024]{1,0:T(8,128)}, f32[512,1024]{1,0:T(8,128)}, u32[]{:S(2)}, u32[]{:S(2)}) collective-permute-start(f32[512,1024]{1,0:T(8,128)} %slice_convert_fusion.refs_4_), channel_id=1, source_target_pairs={{0,4},{4,0},{8,12},{12,8},{16,20},{20,16},{24,28},{28,24},{1,5},{5... | collective-permute-start | bytes 6291464 | tf_op jit(solution)/shard_map/ppermute | solution.py:246
  224.9 153.2 %reduce-scatter.11.cloned.1.call-start = ((), (), s32[]{:S(2)}) async-start(), calls=%async_computation.26 | async-start | bytes 5242880 | tf_op jit(solution)/shard_map/reduce_scatter | solution.py:251
  235.9 113.1 %collective-permute-start.13 = (f32[1024,768]{1,0:T(8,128)}, f32[1024,768]{1,0:T(8,128)}, u32[]{:S(2)}, u32[]{:S(2)}) collective-permute-start(f32[1024,768]{1,0:T(8,128)} %shard_map.208.refs_4_), channel_id=1, source_target_pairs={{0,4},{4,0},{8,12},{12,8},{16,20},{20,16},{24,28},{28,24},{1,5},{5... | collective-permute-start | bytes 9437192 | tf_op jit(solution)/shard_map/ppermute | solution.py:246
  255.1 64.8 %collective-permute-start.9 = (f32[256,2048]{1,0:T(8,128)}, f32[256,2048]{1,0:T(8,128)}, u32[]{:S(2)}, u32[]{:S(2)}) collective-permute-start(f32[256,2048]{1,0:T(8,128)} %fusion.31.refs_8_.refs_0_), channel_id=1, source_target_pairs={{0,2},{1,3},{2,0},{3,1},{4,6},{5,7},{6,4},{7,5},{8,10},{9,11},{10,... | collective-permute-start | bytes 6291464 | tf_op jit(solution)/shard_map/ppermute | solution.py:27
  276.4 185.5 %reduce-scatter.13.cloned.1.call-start = ((), (), s32[]{:S(2)}) async-start(), calls=%async_computation.27 | async-start | bytes 3932160 | tf_op jit(solution)/shard_map/reduce_scatter | solution.py:251
  314.4 88.6 %collective-permute-start.12 = (f32[1024,640]{1,0:T(8,128)}, f32[1024,640]{1,0:T(8,128)}, u32[]{:S(2)}, u32[]{:S(2)}) collective-permute-start(f32[1024,640]{1,0:T(8,128)} %shard_map.212.refs_2_), channel_id=1, source_target_pairs={{0,4},{4,0},{8,12},{12,8},{16,20},{20,16},{24,28},{28,24},{1,5},{5... | collective-permute-start | bytes 7864328 | tf_op jit(solution)/shard_map/ppermute | solution.py:246
  346.4 63.1 %collective-permute-start.10 = (f32[2,4,168,128]{3,2,1,0:T(8,128)}, f32[2,4,168,128]{3,2,1,0:T(8,128)}, u32[]{:S(2)}, u32[]{:S(2)}) collective-permute-start(f32[2,4,168,128]{3,2,1,0:T(8,128)} %shard_map.214.refs_5_), channel_id=1, source_target_pairs={{4,0},{8,4},{12,8},{16,12},{20,16},{24,20},{28,24},{5,1},{9,5},{13... | collective-permute-start | bytes 2064392 | tf_op jit(solution)/shard_map/ppermute | solution.py:32
  347.7 61.8 %collective-permute-start.11 = (f32[2,4,168,128]{3,2,1,0:T(8,128)}, f32[2,4,168,128]{3,2,1,0:T(8,128)}, u32[]{:S(2)}, u32[]{:S(2)}) collective-permute-start(f32[2,4,168,128]{3,2,1,0:T(8,128)} %shard_map.214.refs_5_), channel_id=1, source_target_pairs={{8,0},{12,4},{16,8},{20,12},{24,16},{28,20},{9,1},{13,5},{17,9},{2... | collective-permute-start | bytes 2064392 | tf_op jit(solution)/shard_map/ppermute | solution.py:32
  355.2 160.5 %reduce-scatter.15.cloned.1.call-start = ((), (), s32[]{:S(2)}) async-start(), calls=%async_computation.28 | async-start | bytes 3276800 | tf_op jit(solution)/shard_map/reduce_scatter | solution.py:251
  388.1 94.1 %collective-permute-start.16 = (f32[1024,768]{1,0:T(8,128)}, f32[1024,768]{1,0:T(8,128)}, u32[]{:S(2)}, u32[]{:S(2)}) collective-permute-start(f32[1024,768]{1,0:T(8,128)} %shard_map.216.refs_5_), channel_id=1, source_target_pairs={{0,4},{4,0},{8,12},{12,8},{16,20},{20,16},{24,28},{28,24},{1,5},{5... | collective-permute-start | bytes 9437192 | tf_op jit(solution)/shard_map/ppermute | solution.py:246
  413.5 44.7 %collective-permute-start.15 = (f32[2,4,168,128]{3,2,1,0:T(8,128)}, f32[2,4,168,128]{3,2,1,0:T(8,128)}, u32[]{:S(2)}, u32[]{:S(2)}) collective-permute-start(f32[2,4,168,128]{3,2,1,0:T(8,128)} %shard_map.218.refs_0_.refs_10_), channel_id=1, source_target_pairs={{8,0},{12,4},{16,8},{20,12},{24,16},{28,20},{9,1},{13,5},{17,9},{2... | collective-permute-start | bytes 2064392 | tf_op jit(solution)/shard_map/ppermute | solution.py:32
  434.7 99.7 %collective-permute-start.14 = (f32[256,2048]{1,0:T(8,128)}, f32[256,2048]{1,0:T(8,128)}, u32[]{:S(2)}, u32[]{:S(2)}) collective-permute-start(f32[256,2048]{1,0:T(8,128)} %fusion.26.refs_4_.refs_0_), channel_id=1, source_target_pairs={{0,2},{1,3},{2,0},{3,1},{4,6},{5,7},{6,4},{7,5},{8,10},{9,11},{10,... | collective-permute-start | bytes 6291464 | tf_op jit(solution)/shard_map/ppermute | solution.py:27
  436.3 145.5 %reduce-scatter.17.cloned.1.call-start = ((), (), s32[]{:S(2)}) async-start(), calls=%async_computation.29 | async-start | bytes 3932160 | tf_op jit(solution)/shard_map/reduce_scatter | solution.py:251
  436.6 126.4 %collective-permute-start.18 = (f32[1024,640]{1,0:T(8,128)}, f32[1024,640]{1,0:T(8,128)}, u32[]{:S(2)}, u32[]{:S(2)}) collective-permute-start(f32[1024,640]{1,0:T(8,128)} %shard_map.220.refs_12_), channel_id=1, source_target_pairs={{0,4},{4,0},{8,12},{12,8},{16,20},{20,16},{24,28},{28,24},{1,5},{5... | collective-permute-start | bytes 7864328 | tf_op jit(solution)/shard_map/ppermute | solution.py:246
  498.3 134.6 %reduce-scatter.19.cloned.1.call-start = ((), (), s32[]{:S(2)}) async-start(), calls=%async_computation.30 | async-start | bytes 3276800 | tf_op jit(solution)/shard_map/reduce_scatter | solution.py:251
  498.3 116.7 %collective-permute-start.22 = (f32[1024,640]{1,0:T(8,128)}, f32[1024,640]{1,0:T(8,128)}, u32[]{:S(2)}, u32[]{:S(2)}) collective-permute-start(f32[1024,640]{1,0:T(8,128)} %copy-done.80), channel_id=1, source_target_pairs={{0,4},{4,0},{8,12},{12,8},{16,20},{20,16},{24,28},{28,24},{1,5},{5... | collective-permute-start | bytes 7864328 | tf_op jit(solution)/shard_map/ppermute | solution.py:246
  533.0 48.8 %collective-permute-start.17 = (f32[256,2048]{1,0:T(8,128)}, f32[256,2048]{1,0:T(8,128)}, u32[]{:S(2)}, u32[]{:S(2)}) collective-permute-start(f32[256,2048]{1,0:T(8,128)} %fusion.25.refs_2_.refs_0_), channel_id=1, source_target_pairs={{0,2},{1,3},{2,0},{3,1},{4,6},{5,7},{6,4},{7,5},{8,10},{9,11},{10,... | collective-permute-start | bytes 6291464 | tf_op jit(solution)/shard_map/ppermute | solution.py:27
  562.4 78.5 %collective-permute-start.20 = (f32[256,2048]{1,0:T(8,128)}, f32[256,2048]{1,0:T(8,128)}, u32[]{:S(2)}, u32[]{:S(2)}) collective-permute-start(f32[256,2048]{1,0:T(8,128)} %fusion.24.refs_5_.refs_0_), channel_id=1, source_target_pairs={{0,2},{1,3},{2,0},{3,1},{4,6},{5,7},{6,4},{7,5},{8,10},{9,11},{10,... | collective-permute-start | bytes 6291464 | tf_op jit(solution)/shard_map/ppermute | solution.py:27
  578.8 49.5 %collective-permute-start.21 = (f32[1024,512]{1,0:T(8,128)}, f32[1024,512]{1,0:T(8,128)}, u32[]{:S(2)}, u32[]{:S(2)}) collective-permute-start(f32[1024,512]{1,0:T(8,128)} %shard_map.228.refs_2_), channel_id=1, source_target_pairs={{0,4},{4,0},{8,12},{12,8},{16,20},{20,16},{24,28},{28,24},{1,5},{5... | collective-permute-start | bytes 6291464 | tf_op jit(solution)/shard_map/ppermute | solution.py:246
  580.3 109.8 %reduce-scatter.21.cloned.1.call-start = ((), (), s32[]{:S(2)}) async-start(), calls=%async_computation.31 | async-start | bytes 3276800 | tf_op jit(solution)/shard_map/reduce_scatter | solution.py:251
  613.4 76.6 %collective-permute-start.19 = (f32[256,2048]{1,0:T(8,128)}, f32[256,2048]{1,0:T(8,128)}, u32[]{:S(2)}, u32[]{:S(2)}) collective-permute-start(f32[256,2048]{1,0:T(8,128)} %fusion.23.refs_3_.refs_0_), channel_id=1, source_target_pairs={{0,2},{1,3},{2,0},{3,1},{4,6},{5,7},{6,4},{7,5},{8,10},{9,11},{10,... | collective-permute-start | bytes 6291464 | tf_op jit(solution)/shard_map/ppermute | solution.py:27
  621.6 112.5 %reduce-scatter.23.cloned.1.call-start = ((), (), s32[]{:S(2)}) async-start(), calls=%async_computation.32 | async-start | bytes 2621440 | tf_op jit(solution)/shard_map/reduce_scatter | solution.py:251
  660.8 45.5 %collective-permute-start.24 = (f32[256,384]{1,0:T(8,128)}, f32[256,384]{1,0:T(8,128)}, u32[]{:S(2)}, u32[]{:S(2)}) collective-permute-start(f32[256,384]{1,0:T(8,128)} %shard_map.237), channel_id=1, source_target_pairs={{0,4},{4,0},{8,12},{12,8},{16,20},{20,16},{24,28},{28,24},{1,5},{5... | collective-permute-start | bytes 1179656 | tf_op jit(solution)/shard_map/ppermute | solution.py:246
  (185 other events, 1371.3 us)
Sparse Core Ops, SparseCore 0:
  225.1 62.0 reduce-scatter.8
  290.0 88.1 reduce-scatter.10
  380.6 81.3 reduce-scatter.12
  464.2 51.3 reduce-scatter.14
  518.5 59.9 reduce-scatter.16
  580.7 52.1 reduce-scatter.18
  635.9 52.0 reduce-scatter.20
  690.4 43.6 reduce-scatter.22

commit v6 on v5

--- a/solution.py
+++ b/solution.py
@@ -123,26 +123,27 @@
         put_state(out_ref, h, mapped, value_ref[0, :, HEAD_V * h : HEAD_V * (h + 1)], ones, meta_ref[0])
 
 
-def seen(row_ref, column_ref):
-    row, column = row_ref[0], column_ref[0]
+def seen(row, column, start=0):
     shape = (column.shape[0], row.shape[1])
-    causal = lax.broadcasted_iota(jnp.int32, shape, 0) >= lax.broadcasted_iota(jnp.int32, shape, 1)
+    causal = lax.broadcasted_iota(jnp.int32, shape, 0) + start >= lax.broadcasted_iota(jnp.int32, shape, 1)
     return causal & (column == row)
 
 
 def forward_kernel(
-    query_ref, key_ref, value_ref, row_ref, column_ref, prior_ref, prior_four_ref, mixed_ref, ratio_ref, denom_ref
+    span, query_ref, key_ref, value_ref, row_ref, column_ref, prior_ref, prior_four_ref, mixed_ref, ratio_ref, denom_ref
 ):
     heads = key_ref.shape[2] // FEAT
-    visible = seen(row_ref, column_ref)
-    uses = jnp.where(column_ref[0] == prior_ref[0, 0, LAST : LAST + 1, :1], 1.0, 0.0)
-    query_t = transposed(query_ref)
-    ones = jnp.ones((key_ref.shape[1], HEAD_V), jnp.bfloat16)
+    begin, end = span
+    column = column_ref[0, begin:end]
+    visible = seen(row_ref[0, :, :end], column, begin)
+    uses = jnp.where(column == prior_ref[0, 0, LAST : LAST + 1, :1], 1.0, 0.0)
+    query_t = jnp.transpose(query_ref[0, begin:end].astype(jnp.float32))
+    ones = jnp.ones((end, HEAD_V), jnp.bfloat16)
     for h in range(heads):
         narrow, wide = slice(FEAT * h, FEAT * (h + 1)), slice(HEAD_V * h, HEAD_V * (h + 1))
-        kernel_dot = dot_general(query_ref[0, :, narrow], key_ref[0, :, narrow], 1, 1) * 0.25
+        kernel_dot = dot_general(query_ref[0, begin:end, narrow], key_ref[0, :end, narrow], 1, 1) * 0.25
         scores = low(jnp.where(visible, 1.0 + kernel_dot + 0.5 * kernel_dot * kernel_dot, 0.0))
-        both = dot(scores, jnp.concatenate([value_ref[0, :, wide], ones], 1))
+        both = dot(scores, jnp.concatenate([value_ref[0, :end, wide], ones], 1))
         mapped = low(features(query_t[narrow]))
         state, norm = get_state((prior_ref, prior_four_ref), h)
         numerator = both[:, :HEAD_V] + uses * dot_general(mapped, state, 0, 0)
@@ -185,8 +186,8 @@
     later_ref, later_four_ref, d_query_ref, d_key_ref, d_value_ref,
 ):
     heads = key_ref.shape[2] // FEAT
-    visible = seen(row_ref, column_ref)
     row, column = row_ref[0], column_ref[0]
+    visible = seen(row, column)
     uses = jnp.where(row == prior_ref[0, 0, LAST : LAST + 1, :1], 1.0, 0.0)
     end = row.shape[1] - 1
     tail = jnp.where(row == row[:, end:], 1.0, 0.0)
@@ -583,14 +584,15 @@
     d_hiddens = [run(dot_t, cot, down_weight) for cot in cots]
 
     block = (seq_count, tok_count)
-    mixed, ratio, denominator = run(
-        functools.partial(
-            per_sequence,
-            forward_kernel,
-            [(block + (wide,), jnp.bfloat16), (block + (wide,), jnp.float32), (block + (head_count,), jnp.float32)],
-        ),
-        query_rows, key_proj, value_proj, row, column, prior_two, prior_four,
-    )
+
+    def attend(s, after):
+        part = (seq_count, s.stop - s.start)
+        return per_sequence(
+            functools.partial(forward_kernel, (s.start, s.stop)),
+            [(part + (wide,), jnp.bfloat16), (part + (wide,), jnp.float32), (part + (head_count,), jnp.float32)],
+            query_rows, key_proj, value_proj, row, column, prior_two, prior_four, after=after,
+        )
+
     head_size = lax.axis_size("head")
 
     def exchange(parts):
@@ -630,7 +632,11 @@
     def branch_part(mixed, weight):
         return paired(dot(flat(mixed), weight))
 
-    branches = [head_part(branch_part, mixed[:, s], output_weight) for s in spans]
+    mixeds, ratios, denominators, branches = [], [], [], []
+    for s in spans:
+        for into, value in zip((mixeds, ratios, denominators), attend(s, [b[0] for b in branches])):
+            into.append(value)
+        branches.append(head_part(branch_part, mixeds[-1], output_weight))
 
     mids, normeds, scales, h_mlps, hiddens, d_gates, d_ups, d_hs = [], [], [], [], [], [], [], []
 
@@ -702,15 +708,18 @@
     d_gain_mlp = d_gain_mlp + middle_back(1, [gate_b.sent])
 
     d_mixed = jnp.concatenate(d_mixeds, 1)
+    ratio, denominator = jnp.concatenate(ratios, 1), jnp.concatenate(denominators, 1)
     d_state = run(
         functools.partial(per_sequence, state_back_kernel, [payload]),
         query_rows, d_mixed, ratio, denominator, row, prior_two, meta(first, last, carried),
     )
-    near, far = shift(d_state, -1), shift(d_state, -2)
+    far = shift(d_state, -2)
+    onward = run(lambda own, far: pick_by(lax.axis_index("seq") % 2, far, own), d_state, far)
+    near = along_pair(onward)
     gate_a.line([d_state])
-    up_a = PairFirst(h_mlps, d_ups, (0, cut), [gate_a.whole, down_a.sum])
+    up_a = PairFirst(h_mlps, d_ups, (0, cut), [gate_a.whole, down_a.sum, onward])
     gate_b.line([up_a.sent])
-    mixed_rows = [flat(mixed[:, s]) for s in spans]
+    mixed_rows = [flat(mixed) for mixed in mixeds]
 
     two = per_sequence(
         join_back_kernel, [payload], near, far, jnp.broadcast_to(carried[:, None, None], (seq_count, 1, HEAD_V)),
@@ -742,8 +751,7 @@
     qkv = PairFirst([h_rows], [qkv_right], (0, qkv_right.shape[1]), [up_a.whole])
     in_0 = in_part(0, [qkv.sent, gate_b.sum])
     outcome(0, out_0, [in_0[0]])
-    in_1 = in_part(1, [results[0]])
-    up_b.line([in_1[0]])
+    up_b.line([results[0]])
 
     d_tokens = []
 
@@ -758,7 +766,8 @@
         return d_gain
 
     out = PairFirst(d_branches, mixed_rows, (0, wide), [up_b.whole])
-    d_gain_attn = first_back(0, in_0, [out.sent, up_a.sum])
+    in_1 = in_part(1, [out.sent, up_a.sum])
+    d_gain_attn = first_back(0, in_0, [in_1[0]])
     out_1 = out_part(1, [d_tokens[0]])
     qkv.line([out_1[0]])
     out.line([qkv.whole, up_b.sum])

time: 753 us -> 748 us (level)
  waiting for transfers between devices: 152 us -> 126 us
  local copies, waits for them, and re-layouts: 90.2 us -> 109 us
    reduce_scatter x8, waiting for transfers between devices: 68.9 us -> 38.7 us  [along_line(): lax.psum_scatter(parts, 'seq', scatter_dimension=0, axis_index_groups=gro...]
    ppermute x6 -> x5, waiting for transfers between devices: 22.6 us -> 44 us  [shift(): lax.ppermute(part, 'seq', [(k, k + by) for k in range(count) if 0 <= k +...]
    ppermute x11 -> x12, waiting for transfers between devices: 28.8 us -> 12.8 us  [along_pair(): lax.ppermute(part, 'seq', [(k, k ^ 1) for k in range(lax.axis_size('seq'))])]
    unnamed x374 -> x393, local copies, waits for them, and re-layouts: 65.1 us -> 79.6 us
    ppermute x6 -> x5, starting transfers between devices: 16.2 us -> 15 us  [shift(): lax.ppermute(part, 'seq', [(k, k + by) for k in range(count) if 0 <= k +...]
    pallas_call x5 -> x6, Pallas kernels: 27.4 us -> 27.1 us  [per_sequence(): pl.pallas_call(body, grid=(arrays[0].shape[0],), in_specs=[spec(a.shape)...]
    ppermute x11 -> x12, starting transfers between devices: 15 us -> 15.1 us  [along_pair(): lax.ppermute(part, 'seq', [(k, k ^ 1) for k in range(lax.axis_size('seq'))])]
  transfers between devices with their start and end apart: 33 -> 33, of which waited for: 12 -> 11; matrix products, arithmetic and copies ran while one was open for 20% -> 22% of each run, Pallas kernels for 24% -> 24%
where the time goes in v6:
time: 748 us; the launch traced here: 738 us
  Pallas kernels  179 us (24%)
  blocking collectives  132 us (18%)
  waiting for transfers between devices  126 us (17%)
  local copies, waits for them, and re-layouts  109 us (15%)
  other arithmetic  94.7 us (13%)
  matrix products  42.3 us (6%)
  starting transfers between devices  38.4 us (5%)
  between operations  17 us (2%)
    all_to_all x17, blocking collectives, exchange(): lax.all_to_all(parts, 'head', 0, 0, axis_index_groups=groups, tiled=True)  121 us
    unnamed x393, local copies, waits for them, and re-layouts  79.6 us
    pallas_call x14, Pallas kernels, blocks_dot(): pl.pallas_call(kernel, grid_spec=pltpu.PrefetchScalarGridSpec(num_scalar_...  75 us
    ppermute x5, waiting for transfers between devices, shift(): lax.ppermute(part, 'seq', [(k, k + by) for k in range(count) if 0 <= k +...  44 us
    reduce_scatter x8, waiting for transfers between devices, along_line(): lax.psum_scatter(parts, 'seq', scatter_dimension=0, axis_index_groups=gro...  38.7 us
    pallas_call x9, Pallas kernels, add_after(): pl.pallas_call(kernel, grid=(steps,), in_specs=[spec] * len(terms) + [pl....  33.3 us
    ppermute x8, waiting for transfers between devices, swap(): return lax.ppermute(part, 'head', [(k, k ^ bit) for k in range(count)])  30 us
    pallas_call x6, Pallas kernels, per_sequence(): pl.pallas_call(body, grid=(arrays[0].shape[0],), in_specs=[spec(a.shape)...  27.1 us
  transfers between devices with their start and end apart: 33, of which 11 were waited for; matrix products, arithmetic and copies ran while one was open for 22% of the time, Pallas kernels for 24%

profile of v6, /device:TPU:0, one launch (start us, length us, event | category | flops | bytes accessed | tf_op | source)
XLA Modules:
  0.0 737.6 jit_solution(9305703732529230595)
XLA Ops:
  66.8 7.7 %fusion.60 = f32[512,1408]{1,0:T(8,128)} fusion(bf16[512,2048]{1,0:T(8,128)(2,1)S(1)} %bitcast.164, bf16[1408,2048]{1,0:T(8,128)(2,1)} %right_ref.1), kind=kOutput, calls=%fused_computation.169 | convolution fusion | flops 2952790016 | bytes 10747904 | tf_op jit(solution)/shard_map/dot_general | solution.py:40
  84.1 7.1 all_to_all.85
  98.4 7.1 all_to_all.86
  111.6 30.0 %collective-permute-done.3 = f32[256,2048]{1,0:T(8,128)} collective-permute-done((f32[256,2048]{1,0:T(8,128)}, f32[256,2048]{1,0:T(8,128)}, u32[]{:S(2)}, u32[]{:S(2)}) %collective-permute-start.3) | collective-permute-done | bytes 2097184 | tf_op jit(solution)/shard_map/ppermute | solution.py:27
  144.6 7.7 %all_to_all.87 = f32[2,256,2048]{2,1,0:T(8,128)S(1)} all-to-all(f32[2,256,2048]{2,1,0:T(8,128)S(1)} %pad_maximum_fusion.1), channel_id=1, replica_groups={{0,1},{2,3},{4,5},{6,7},{8,9},{10,11},{12,13},{14,15},{16,17},{18,19},{..., dimensions={0} | all-to-all | bytes 8388608 | tf_op jit(solution)/shard_map/all_to_all | solution.py:600
  167.7 9.4 %shard_map.207 = f32[512,2048]{1,0:T(8,128)S(1)} custom-call(bf16[512,1408]{1,0:T(8,128)(2,1)S(1)} %get-tuple-element.141.refs_0_.refs_2_, bf16[512,1408]{1,0:T(8,128)(2,1)S(1)} %get-tuple-element.142.refs_1_.refs_2_, bf16[2048,1408]{1,0:T(8,128)(2,1)} %refs_2_.1, bf16[2048,1408]{1,0:T(8,128)(2,1)} %refs_3_.3, ...), custom_call_target="tpu_custom_call" | custom-call | flops 549755813888 | bytes 1048576 | tf_op jit(solution)/shard_map/pallas_call | solution.py:408
  177.0 7.1 all_to_all.88
  190.3 7.6 %all_to_all.89 = f32[2,256,2048]{2,1,0:T(8,128)S(1)} all-to-all(f32[2,256,2048]{2,1,0:T(8,128)S(1)} %pad_maximum_fusion.2), channel_id=1, replica_groups={{0,1},{2,3},{4,5},{6,7},{8,9},{10,11},{12,13},{14,15},{16,17},{18,19},{..., dimensions={0} | all-to-all | bytes 8388608 | tf_op jit(solution)/shard_map/all_to_all | solution.py:600
  215.9 6.5 shard_map.208.refs_4_
  234.9 9.4 %shard_map.210 = f32[512,2048]{1,0:T(8,128)S(1)} custom-call(bf16[512,1408]{1,0:T(8,128)(2,1)S(1)} %copy-done.121, bf16[512,1408]{1,0:T(8,128)(2,1)S(1)} %copy-done.111, bf16[2048,1408]{1,0:T(8,128)(2,1)} %refs_2_.1, bf16[2048,1408]{1,0:T(8,128)(2,1)} %refs_3_.3, f32[1024,768]{1,0:T(8,128)} %shard_map.209.refs_4_), custom_call_target="tpu_custom_call" | custom-call | flops 549755813888 | bytes 1048576 | tf_op jit(solution)/shard_map/pallas_call | solution.py:408
  244.3 7.1 all_to_all.90
  256.1 7.0 collective-permute-done.8.refs_7_
  263.1 10.2 %shard_map.211.refs_2_ = f32[1024,1024]{1,0:T(8,128)} custom-call(s32[4]{0:T(128)S(1)} %broadcast_add_fusion.1.where_ref, bf16[512,2048]{1,0:T(8,128)(2,1)S(1)} %bitcast.166, bf16[512,2048]{1,0:T(8,128)(2,1)S(1)} %bitcast.162, f32[1024,1024]{1,0:T(8,128)} %collective-permute-done.4.refs_4_.refs_2_.refs_3_, ...), custom_call_target="tpu_custom_call" | custom-call | flops 549755813888 | bytes 1048576 | tf_op jit(solution)/shard_map/pallas_call | solution.py:299
  273.5 8.5 %reduce-scatter.9.cloned.1.call-done.refs_3_ = f32[512,384]{1,0:T(8,128)} async-done(((f32[2048,384]{1,0:T(8,128)}), f32[512,384]{1,0:T(8,128)}) %reduce-scatter.9.cloned.1.call-update) | async-done | bytes 786448 | tf_op jit(solution)/shard_map/reduce_scatter | solution.py:252
  290.7 7.5 %all_to_all.91 = f32[2,256,2048]{2,1,0:T(8,128)S(1)} all-to-all(f32[2,256,2048]{2,1,0:T(8,128)S(1)} %pad_maximum_fusion.3), channel_id=1, replica_groups={{0,1},{2,3},{4,5},{6,7},{8,9},{10,11},{12,13},{14,15},{16,17},{18,19},{..., dimensions={0} | all-to-all | bytes 8388608 | tf_op jit(solution)/shard_map/all_to_all | solution.py:600
  323.5 7.2 all_to_all.92
  353.0 22.1 %collective-permute-done.10.refs_1_ = f32[2,4,168,128]{3,2,1,0:T(8,128)} collective-permute-done((f32[2,4,168,128]{3,2,1,0:T(8,128)}, f32[2,4,168,128]{3,2,1,0:T(8,128)}, u32[]{:S(2)}, u32[]{:S(2)}) %collective-permute-start.10) | collective-permute-done | bytes 688160 | tf_op jit(solution)/shard_map/ppermute | solution.py:32
  411.7 7.2 all_to_all.93
  429.2 21.2 %collective-permute-done.15.refs_11_ = f32[2,4,168,128]{3,2,1,0:T(8,128)} collective-permute-done((f32[2,4,168,128]{3,2,1,0:T(8,128)}, f32[2,4,168,128]{3,2,1,0:T(8,128)}, u32[]{:S(2)}, u32[]{:S(2)}) %collective-permute-start.15) | collective-permute-done | bytes 688160 | tf_op jit(solution)/shard_map/ppermute | solution.py:32
  456.0 12.7 %shard_map.222 = (bf16[2,512,64]{2,1,0:T(8,128)(2,1)S(1)}, bf16[2,512,64]{2,1,0:T(8,128)(2,1)S(1)}, bf16[2,512,512]{2,1,0:T(8,128)(2,1)}) custom-call(bf16[2,512,64]{2,1,0:T(8,128)(2,1)S(1)} %bitcast.183, bf16[2,512,64]{2,1,0:T(8,128)(2,1)S(1)} %bitcast.178, bf16[2,512,512]{2,1,0:T(8,128)(2,1)} %bitcast.191, f32[2,1,512]{2,1,0:T(1,128)S(1)} %copy-done.89, ...), custom_call_target="tpu_custom_call" | custom-call | flops 549755813888 | bytes 1048576 | tf_op jit(solution)/shard_map/pallas_call | solution.py:234
  491.2 17.1 %reduce-scatter.15.cloned.1.call-done.refs_7_ = f32[256,640]{1,0:T(8,128)} async-done(((f32[1024,640]{1,0:T(8,128)}), f32[256,640]{1,0:T(8,128)}) %reduce-scatter.15.cloned.1.call-update) | async-done | bytes 655376 | tf_op jit(solution)/shard_map/reduce_scatter | solution.py:252
  519.1 7.1 all_to_all.94
  536.1 7.4 all_to_all.95
  580.9 7.3 all_to_all.96
  599.7 7.2 all_to_all.97.refs_0_
  606.9 7.0 shard_map.231
  614.0 7.1 all_to_all.98
  651.8 8.3 %all_to_all.99.refs_2_.refs_1_ = f32[2,256,2048]{2,1,0:T(8,128)} all-to-all(f32[2,256,2048]{2,1,0:T(8,128)S(1)} %pad_maximum_fusion.7), channel_id=1, replica_groups={{0,1},{2,3},{4,5},{6,7},{8,9},{10,11},{12,13},{14,15},{16,17},{18,19},{..., dimensions={0} | all-to-all | bytes 8388608 | tf_op jit(solution)/shard_map/all_to_all | solution.py:600
  669.2 8.0 %pad_maximum_fusion = f32[2,512,2048]{2,1,0:T(8,128)} fusion(f32[2,256,2048]{2,1,0:T(8,128)} %all_to_all.99.refs_2_.refs_1_, f32[2,256,2048]{2,1,0:T(8,128)} %copy-done.2), kind=kLoop, calls=%fused_computation.5 | loop fusion | flops 2097152 | bytes 16777216 | tf_op jit(solution)/shard_map/concatenate | solution.py:798
  679.8 10.7 %all-reduce = f32[8,256]{1,0:T(8,128)S(1)} all-reduce(f32[8,256]{1,0:T(8,128)} %shard_map.236), channel_id=9, replica_groups={{0,8,16,24},{4,12,20,28},{1,9,17,25},{5,13,21,29},{2,10,18,26},{6,14,22..., use_global_device_ids=true, to_apply=%region_21.22.clone | all-reduce | flops 2048 | bytes 16384
  697.8 7.4 all_to_all.101
  721.6 6.5 reduce-scatter.23.cloned.1.call-done.refs_0_
  (622 shorter events, 409.2 us)
Async XLA Ops:
  7.2 274.8 %reduce-scatter.9.cloned.1.call-start = ((), (), s32[]{:S(2)}) async-start(), calls=%async_computation.25 | async-start | bytes 3932160 | tf_op jit(solution)/shard_map/reduce_scatter | solution.py:252
  21.0 39.9 %collective-permute-start = (f32[2,4,168,128]{3,2,1,0:T(8,128)}, f32[2,4,168,128]{3,2,1,0:T(8,128)}, u32[]{:S(2)}, u32[]{:S(2)}) collective-permute-start(f32[2,4,168,128]{3,2,1,0:T(8,128)} %shard_map.203), channel_id=1, source_target_pairs={{0,4},{4,8},{8,12},{12,16},{16,20},{20,24},{24,28},{1,5},{5,9},{9,... | collective-permute-start | bytes 2064392 | tf_op jit(solution)/shard_map/ppermute | solution.py:32
  26.7 34.1 %collective-permute-start.1 = (f32[2,4,168,128]{3,2,1,0:T(8,128)}, f32[2,4,168,128]{3,2,1,0:T(8,128)}, u32[]{:S(2)}, u32[]{:S(2)}) collective-permute-start(f32[2,4,168,128]{3,2,1,0:T(8,128)} %shard_map.203), channel_id=1, source_target_pairs={{0,8},{4,12},{8,16},{12,20},{16,24},{20,28},{1,9},{5,13},{9,17},{1... | collective-permute-start | bytes 2064392 | tf_op jit(solution)/shard_map/ppermute | solution.py:32
  44.8 122.8 %collective-permute-start.4 = (f32[1024,1024]{1,0:T(8,128)}, f32[1024,1024]{1,0:T(8,128)}, u32[]{:S(2)}, u32[]{:S(2)}) collective-permute-start(f32[1024,1024]{1,0:T(8,128)} %shard_map.206), channel_id=1, source_target_pairs={{0,4},{4,0},{8,12},{12,8},{16,20},{20,16},{24,28},{28,24},{1,5},{5... | collective-permute-start | bytes 12582920 | tf_op jit(solution)/shard_map/ppermute | solution.py:247
  63.6 16.7 %collective-permute-start.2 = (f32[2,4,168,128]{3,2,1,0:T(8,128)S(1)}, f32[2,4,168,128]{3,2,1,0:T(8,128)S(1)}, u32[]{:S(2)}, u32[]{:S(2)}) collective-permute-start(f32[2,4,168,128]{3,2,1,0:T(8,128)S(1)} %fusion.44.refs_5_.refs_8_), channel_id=1, source_target_pairs={{0,8},{4,12},{8,16},{12,20},{16,24},{20,28},{1,9},{5,13},{9,17},{1... | collective-permute-start | bytes 2064392 | tf_op jit(solution)/shard_map/ppermute | solution.py:32
  92.8 48.8 %collective-permute-start.3 = (f32[256,2048]{1,0:T(8,128)}, f32[256,2048]{1,0:T(8,128)}, u32[]{:S(2)}, u32[]{:S(2)}) collective-permute-start(f32[256,2048]{1,0:T(8,128)} %fusion.34.refs_7_), channel_id=1, source_target_pairs={{0,2},{1,3},{2,0},{3,1},{4,6},{5,7},{6,4},{7,5},{8,10},{9,11},{10,... | collective-permute-start | bytes 6291464 | tf_op jit(solution)/shard_map/ppermute | solution.py:27
  107.3 80.1 %collective-permute-start.6 = (f32[256,2048]{1,0:T(8,128)}, f32[256,2048]{1,0:T(8,128)}, u32[]{:S(2)}, u32[]{:S(2)}) collective-permute-start(f32[256,2048]{1,0:T(8,128)} %fusion.33), channel_id=1, source_target_pairs={{0,2},{1,3},{2,0},{3,1},{4,6},{5,7},{6,4},{7,5},{8,10},{9,11},{10,... | collective-permute-start | bytes 6291464 | tf_op jit(solution)/shard_map/ppermute | solution.py:27
  165.0 91.1 %collective-permute-start.7 = (f32[512,1024]{1,0:T(8,128)}, f32[512,1024]{1,0:T(8,128)}, u32[]{:S(2)}, u32[]{:S(2)}) collective-permute-start(f32[512,1024]{1,0:T(8,128)} %slice_convert_fusion.1), channel_id=1, source_target_pairs={{0,4},{4,0},{8,12},{12,8},{16,20},{20,16},{24,28},{28,24},{1,5},{5... | collective-permute-start | bytes 6291464 | tf_op jit(solution)/shard_map/ppermute | solution.py:247
  185.8 87.7 %collective-permute-start.5 = (f32[256,2048]{1,0:T(8,128)}, f32[256,2048]{1,0:T(8,128)}, u32[]{:S(2)}, u32[]{:S(2)}) collective-permute-start(f32[256,2048]{1,0:T(8,128)} %fusion.32.refs_0_), channel_id=1, source_target_pairs={{0,2},{1,3},{2,0},{3,1},{4,6},{5,7},{6,4},{7,5},{8,10},{9,11},{10,... | collective-permute-start | bytes 6291464 | tf_op jit(solution)/shard_map/ppermute | solution.py:27
  214.3 48.8 %collective-permute-start.8 = (f32[512,1024]{1,0:T(8,128)}, f32[512,1024]{1,0:T(8,128)}, u32[]{:S(2)}, u32[]{:S(2)}) collective-permute-start(f32[512,1024]{1,0:T(8,128)} %slice_convert_fusion.refs_4_), channel_id=1, source_target_pairs={{0,4},{4,0},{8,12},{12,8},{16,20},{20,16},{24,28},{28,24},{1,5},{5... | collective-permute-start | bytes 6291464 | tf_op jit(solution)/shard_map/ppermute | solution.py:247
  222.4 156.3 %reduce-scatter.11.cloned.1.call-start = ((), (), s32[]{:S(2)}) async-start(), calls=%async_computation.26 | async-start | bytes 5242880 | tf_op jit(solution)/shard_map/reduce_scatter | solution.py:252
  233.5 110.0 %collective-permute-start.13 = (f32[1024,768]{1,0:T(8,128)}, f32[1024,768]{1,0:T(8,128)}, u32[]{:S(2)}, u32[]{:S(2)}) collective-permute-start(f32[1024,768]{1,0:T(8,128)} %shard_map.209.refs_4_), channel_id=1, source_target_pairs={{0,4},{4,0},{8,12},{12,8},{16,20},{20,16},{24,28},{28,24},{1,5},{5... | collective-permute-start | bytes 9437192 | tf_op jit(solution)/shard_map/ppermute | solution.py:247
  253.1 61.6 %collective-permute-start.9 = (f32[256,2048]{1,0:T(8,128)}, f32[256,2048]{1,0:T(8,128)}, u32[]{:S(2)}, u32[]{:S(2)}) collective-permute-start(f32[256,2048]{1,0:T(8,128)} %fusion.31.refs_8_.refs_0_), channel_id=1, source_target_pairs={{0,2},{1,3},{2,0},{3,1},{4,6},{5,7},{6,4},{7,5},{8,10},{9,11},{10,... | collective-permute-start | bytes 6291464 | tf_op jit(solution)/shard_map/ppermute | solution.py:27
  273.4 180.4 %reduce-scatter.13.cloned.1.call-start = ((), (), s32[]{:S(2)}) async-start(), calls=%async_computation.27 | async-start | bytes 3932160 | tf_op jit(solution)/shard_map/reduce_scatter | solution.py:252
  309.3 79.9 %collective-permute-start.12 = (f32[1024,640]{1,0:T(8,128)}, f32[1024,640]{1,0:T(8,128)}, u32[]{:S(2)}, u32[]{:S(2)}) collective-permute-start(f32[1024,640]{1,0:T(8,128)} %shard_map.213.refs_2_), channel_id=1, source_target_pairs={{0,4},{4,0},{8,12},{12,8},{16,20},{20,16},{24,28},{28,24},{1,5},{5... | collective-permute-start | bytes 7864328 | tf_op jit(solution)/shard_map/ppermute | solution.py:247
  342.2 33.0 %collective-permute-start.10 = (f32[2,4,168,128]{3,2,1,0:T(8,128)}, f32[2,4,168,128]{3,2,1,0:T(8,128)}, u32[]{:S(2)}, u32[]{:S(2)}) collective-permute-start(f32[2,4,168,128]{3,2,1,0:T(8,128)} %shard_map.215.refs_5_), channel_id=1, source_target_pairs={{8,0},{12,4},{16,8},{20,12},{24,16},{28,20},{9,1},{13,5},{17,9},{2... | collective-permute-start | bytes 2064392 | tf_op jit(solution)/shard_map/ppermute | solution.py:32
  349.7 158.6 %reduce-scatter.15.cloned.1.call-start = ((), (), s32[]{:S(2)}) async-start(), calls=%async_computation.28 | async-start | bytes 3276800 | tf_op jit(solution)/shard_map/reduce_scatter | solution.py:252
  377.2 24.3 %collective-permute-start.11 = (f32[2,4,168,128]{3,2,1,0:T(8,128)}, f32[2,4,168,128]{3,2,1,0:T(8,128)}, u32[]{:S(2)}, u32[]{:S(2)}) collective-permute-start(f32[2,4,168,128]{3,2,1,0:T(8,128)} %broadcast_select_fusion.refs_6_), channel_id=1, source_target_pairs={{0,4},{4,0},{8,12},{12,8},{16,20},{20,16},{24,28},{28,24},{1,5},{5... | collective-permute-start | bytes 2064392 | tf_op jit(solution)/shard_map/ppermute | solution.py:247
  388.6 85.5 %collective-permute-start.16 = (f32[1024,768]{1,0:T(8,128)}, f32[1024,768]{1,0:T(8,128)}, u32[]{:S(2)}, u32[]{:S(2)}) collective-permute-start(f32[1024,768]{1,0:T(8,128)} %shard_map.217.refs_5_), channel_id=1, source_target_pairs={{0,4},{4,0},{8,12},{12,8},{16,20},{20,16},{24,28},{28,24},{1,5},{5... | collective-permute-start | bytes 9437192 | tf_op jit(solution)/shard_map/ppermute | solution.py:247
  405.5 44.9 %collective-permute-start.15 = (f32[2,4,168,128]{3,2,1,0:T(8,128)}, f32[2,4,168,128]{3,2,1,0:T(8,128)}, u32[]{:S(2)}, u32[]{:S(2)}) collective-permute-start(f32[2,4,168,128]{3,2,1,0:T(8,128)} %shard_map.219.refs_0_.refs_10_), channel_id=1, source_target_pairs={{8,0},{12,4},{16,8},{20,12},{24,16},{28,20},{9,1},{13,5},{17,9},{2... | collective-permute-start | bytes 2064392 | tf_op jit(solution)/shard_map/ppermute | solution.py:32
  426.7 102.7 %collective-permute-start.14 = (f32[256,2048]{1,0:T(8,128)}, f32[256,2048]{1,0:T(8,128)}, u32[]{:S(2)}, u32[]{:S(2)}) collective-permute-start(f32[256,2048]{1,0:T(8,128)} %fusion.26.refs_4_.refs_0_), channel_id=1, source_target_pairs={{0,2},{1,3},{2,0},{3,1},{4,6},{5,7},{6,4},{7,5},{8,10},{9,11},{10,... | collective-permute-start | bytes 6291464 | tf_op jit(solution)/shard_map/ppermute | solution.py:27
  427.3 143.7 %reduce-scatter.17.cloned.1.call-start = ((), (), s32[]{:S(2)}) async-start(), calls=%async_computation.29 | async-start | bytes 3932160 | tf_op jit(solution)/shard_map/reduce_scatter | solution.py:252
  427.6 116.9 %collective-permute-start.18 = (f32[1024,640]{1,0:T(8,128)}, f32[1024,640]{1,0:T(8,128)}, u32[]{:S(2)}, u32[]{:S(2)}) collective-permute-start(f32[1024,640]{1,0:T(8,128)} %shard_map.221.refs_12_), channel_id=1, source_target_pairs={{0,4},{4,0},{8,12},{12,8},{16,20},{20,16},{24,28},{28,24},{1,5},{5... | collective-permute-start | bytes 7864328 | tf_op jit(solution)/shard_map/ppermute | solution.py:247
  489.6 140.3 %reduce-scatter.19.cloned.1.call-start = ((), (), s32[]{:S(2)}) async-start(), calls=%async_computation.30 | async-start | bytes 3276800 | tf_op jit(solution)/shard_map/reduce_scatter | solution.py:252
  489.6 133.6 %collective-permute-start.22 = (f32[1024,640]{1,0:T(8,128)}, f32[1024,640]{1,0:T(8,128)}, u32[]{:S(2)}, u32[]{:S(2)}) collective-permute-start(f32[1024,640]{1,0:T(8,128)} %copy-done.91), channel_id=1, source_target_pairs={{0,4},{4,0},{8,12},{12,8},{16,20},{20,16},{24,28},{28,24},{1,5},{5... | collective-permute-start | bytes 7864328 | tf_op jit(solution)/shard_map/ppermute | solution.py:247
  527.9 63.5 %collective-permute-start.17 = (f32[256,2048]{1,0:T(8,128)}, f32[256,2048]{1,0:T(8,128)}, u32[]{:S(2)}, u32[]{:S(2)}) collective-permute-start(f32[256,2048]{1,0:T(8,128)} %fusion.25.refs_2_.refs_0_), channel_id=1, source_target_pairs={{0,2},{1,3},{2,0},{3,1},{4,6},{5,7},{6,4},{7,5},{8,10},{9,11},{10,... | collective-permute-start | bytes 6291464 | tf_op jit(solution)/shard_map/ppermute | solution.py:27
  564.6 65.3 %collective-permute-start.21 = (f32[1024,512]{1,0:T(8,128)}, f32[1024,512]{1,0:T(8,128)}, u32[]{:S(2)}, u32[]{:S(2)}) collective-permute-start(f32[1024,512]{1,0:T(8,128)} %shard_map.228.refs_6_), channel_id=1, source_target_pairs={{0,4},{4,0},{8,12},{12,8},{16,20},{20,16},{24,28},{28,24},{1,5},{5... | collective-permute-start | bytes 6291464 | tf_op jit(solution)/shard_map/ppermute | solution.py:247
  566.1 125.0 %reduce-scatter.21.cloned.1.call-start = ((), (), s32[]{:S(2)}) async-start(), calls=%async_computation.31 | async-start | bytes 3276800 | tf_op jit(solution)/shard_map/reduce_scatter | solution.py:252
  589.9 53.6 %collective-permute-start.20 = (f32[256,2048]{1,0:T(8,128)}, f32[256,2048]{1,0:T(8,128)}, u32[]{:S(2)}, u32[]{:S(2)}) collective-permute-start(f32[256,2048]{1,0:T(8,128)} %fusion.24.refs_2_.refs_0_), channel_id=1, source_target_pairs={{0,2},{1,3},{2,0},{3,1},{4,6},{5,7},{6,4},{7,5},{8,10},{9,11},{10,... | collective-permute-start | bytes 6291464 | tf_op jit(solution)/shard_map/ppermute | solution.py:27
  622.7 68.3 %collective-permute-start.19 = (f32[256,2048]{1,0:T(8,128)}, f32[256,2048]{1,0:T(8,128)}, u32[]{:S(2)}, u32[]{:S(2)}) collective-permute-start(f32[256,2048]{1,0:T(8,128)} %fusion.23.refs_3_.refs_0_), channel_id=1, source_target_pairs={{0,2},{1,3},{2,0},{3,1},{4,6},{5,7},{6,4},{7,5},{8,10},{9,11},{10,... | collective-permute-start | bytes 6291464 | tf_op jit(solution)/shard_map/ppermute | solution.py:27
  629.8 98.3 %reduce-scatter.23.cloned.1.call-start = ((), (), s32[]{:S(2)}) async-start(), calls=%async_computation.32 | async-start | bytes 2621440 | tf_op jit(solution)/shard_map/reduce_scatter | solution.py:252
  663.2 43.9 %collective-permute-start.24 = (f32[256,384]{1,0:T(8,128)}, f32[256,384]{1,0:T(8,128)}, u32[]{:S(2)}, u32[]{:S(2)}) collective-permute-start(f32[256,384]{1,0:T(8,128)} %shard_map.238), channel_id=1, source_target_pairs={{0,4},{4,0},{8,12},{12,8},{16,20},{20,16},{24,28},{28,24},{1,5},{5... | collective-permute-start | bytes 1179656 | tf_op jit(solution)/shard_map/ppermute | solution.py:247
  (194 other events, 1319.5 us)
Sparse Core Ops, SparseCore 0:
  222.5 59.4 reduce-scatter.8
  284.8 87.1 reduce-scatter.10
  374.5 79.2 reduce-scatter.12
  456.1 52.1 reduce-scatter.14
  511.1 59.9 reduce-scatter.16
  573.3 52.1 reduce-scatter.18
  629.9 52.1 reduce-scatter.20
  684.5 43.5 reduce-scatter.22

commit v7 on v6

--- a/solution.py
+++ b/solution.py
@@ -222,7 +222,7 @@
     d_key_ref[0] = low(jnp.transpose(jnp.concatenate(d_keys, 0)))
 
 
-def per_sequence(kernel, out_shapes, *arrays, after=()):
+def per_sequence(kernel, out_shapes, *arrays, after=(), vmem=48):
     def spec(shape):
         rest = (0,) * (len(shape) - 1)
         return pl.BlockSpec((1,) + tuple(shape[1:]), lambda s: (s,) + rest)
@@ -238,7 +238,7 @@
         out_specs=[spec(o.shape) for o in outs],
         out_shape=outs,
         cost_estimate=LONG,
-        compiler_params=pltpu.CompilerParams(vmem_limit_bytes=48 << 20),
+        compiler_params=pltpu.CompilerParams(vmem_limit_bytes=vmem << 20),
     )(*arrays, *after)
     return result if len(outs) > 1 else result[0]
 
@@ -590,7 +590,7 @@
         return per_sequence(
             functools.partial(forward_kernel, (s.start, s.stop)),
             [(part + (wide,), jnp.bfloat16), (part + (wide,), jnp.float32), (part + (head_count,), jnp.float32)],
-            query_rows, key_proj, value_proj, row, column, prior_two, prior_four, after=after,
+            query_rows, key_proj, value_proj, row, column, prior_two, prior_four, after=after, vmem=60,
         )
 
     head_size = lax.axis_size("head")

time: 748 us -> 753 us (level)
    unnamed x393 -> x383, local copies, waits for them, and re-layouts: 79.6 us -> 81.6 us
where the time goes in v7:
time: 753 us; the launch traced here: 742 us
  Pallas kernels  184 us (24%)
  blocking collectives  132 us (18%)
  waiting for transfers between devices  121 us (16%)
  local copies, waits for them, and re-layouts  111 us (15%)
  other arithmetic  94.7 us (13%)
  matrix products  44.4 us (6%)
  starting transfers between devices  38.4 us (5%)
  between operations  16.9 us (2%)
    all_to_all x17, blocking collectives, exchange(): lax.all_to_all(parts, 'head', 0, 0, axis_index_groups=groups, tiled=True)  121 us
    unnamed x383, local copies, waits for them, and re-layouts  81.6 us
    pallas_call x14, Pallas kernels, blocks_dot(): pl.pallas_call(kernel, grid_spec=pltpu.PrefetchScalarGridSpec(num_scalar_...  75 us
    ppermute x5, waiting for transfers between devices, shift(): lax.ppermute(part, 'seq', [(k, k + by) for k in range(count) if 0 <= k +...  43.9 us
    reduce_scatter x8, waiting for transfers between devices, along_line(): lax.psum_scatter(parts, 'seq', scatter_dimension=0, axis_index_groups=gro...  38.8 us
    pallas_call x9, Pallas kernels, add_after(): pl.pallas_call(kernel, grid=(steps,), in_specs=[spec] * len(terms) + [pl....  33.3 us
    pallas_call x6, Pallas kernels, per_sequence(): pl.pallas_call(body, grid=(arrays[0].shape[0],), in_specs=[spec(a.shape)...  31.9 us
    dot_general x9, matrix products, dot(): return jnp.dot(left, right, preferred_element_type=jnp.float32)  29.1 us
  transfers between devices with their start and end apart: 33, of which 11 were waited for; matrix products, arithmetic and copies ran while one was open for 22% of the time, Pallas kernels for 24%

profile of v7, /device:TPU:0, one launch (start us, length us, event | category | flops | bytes accessed | tf_op | source)
XLA Modules:
  0.0 742.3 jit_solution(7023155241612281790)
XLA Ops:
  66.7 7.7 %fusion.60 = f32[512,1408]{1,0:T(8,128)} fusion(bf16[512,2048]{1,0:T(8,128)(2,1)S(1)} %bitcast.164, bf16[1408,2048]{1,0:T(8,128)(2,1)} %right_ref.1), kind=kOutput, calls=%fused_computation.169 | convolution fusion | flops 2952790016 | bytes 10747904 | tf_op jit(solution)/shard_map/dot_general | solution.py:40
  88.2 7.1 all_to_all.85
  105.9 7.1 all_to_all.86
  120.0 25.7 %collective-permute-done.3 = f32[256,2048]{1,0:T(8,128)} collective-permute-done((f32[256,2048]{1,0:T(8,128)}, f32[256,2048]{1,0:T(8,128)}, u32[]{:S(2)}, u32[]{:S(2)}) %collective-permute-start.3) | collective-permute-done | bytes 2097184 | tf_op jit(solution)/shard_map/ppermute | solution.py:27
  148.7 7.7 %all_to_all.87 = f32[2,256,2048]{2,1,0:T(8,128)S(1)} all-to-all(f32[2,256,2048]{2,1,0:T(8,128)S(1)} %pad_maximum_fusion.1), channel_id=1, replica_groups={{0,1},{2,3},{4,5},{6,7},{8,9},{10,11},{12,13},{14,15},{16,17},{18,19},{..., dimensions={0} | all-to-all | bytes 8388608 | tf_op jit(solution)/shard_map/all_to_all | solution.py:600
  171.9 9.4 %shard_map.207 = f32[512,2048]{1,0:T(8,128)S(1)} custom-call(bf16[512,1408]{1,0:T(8,128)(2,1)S(1)} %get-tuple-element.141.refs_0_.refs_2_, bf16[512,1408]{1,0:T(8,128)(2,1)S(1)} %get-tuple-element.142.refs_1_.refs_2_, bf16[2048,1408]{1,0:T(8,128)(2,1)} %refs_2_.1, bf16[2048,1408]{1,0:T(8,128)(2,1)} %refs_3_.3, ...), custom_call_target="tpu_custom_call" | custom-call | flops 549755813888 | bytes 1048576 | tf_op jit(solution)/shard_map/pallas_call | solution.py:408
  181.3 7.1 all_to_all.88
  194.6 7.6 %all_to_all.89 = f32[2,256,2048]{2,1,0:T(8,128)S(1)} all-to-all(f32[2,256,2048]{2,1,0:T(8,128)S(1)} %pad_maximum_fusion.2), channel_id=1, replica_groups={{0,1},{2,3},{4,5},{6,7},{8,9},{10,11},{12,13},{14,15},{16,17},{18,19},{..., dimensions={0} | all-to-all | bytes 8388608 | tf_op jit(solution)/shard_map/all_to_all | solution.py:600
  220.7 6.4 shard_map.208.refs_4_
  239.8 9.4 %shard_map.210 = f32[512,2048]{1,0:T(8,128)S(1)} custom-call(bf16[512,1408]{1,0:T(8,128)(2,1)S(1)} %copy-done.114, bf16[512,1408]{1,0:T(8,128)(2,1)S(1)} %copy-done.104, bf16[2048,1408]{1,0:T(8,128)(2,1)} %refs_2_.1, bf16[2048,1408]{1,0:T(8,128)(2,1)} %refs_3_.3, f32[1024,768]{1,0:T(8,128)} %shard_map.209.refs_4_), custom_call_target="tpu_custom_call" | custom-call | flops 549755813888 | bytes 1048576 | tf_op jit(solution)/shard_map/pallas_call | solution.py:408
  249.1 7.1 all_to_all.90
  260.9 7.0 collective-permute-done.8.refs_7_
  268.0 10.2 %shard_map.211.refs_2_ = f32[1024,1024]{1,0:T(8,128)} custom-call(s32[4]{0:T(128)S(1)} %broadcast_add_fusion.1.where_ref, bf16[512,2048]{1,0:T(8,128)(2,1)S(1)} %bitcast.166, bf16[512,2048]{1,0:T(8,128)(2,1)S(1)} %bitcast.162, f32[1024,1024]{1,0:T(8,128)} %collective-permute-done.4.refs_4_.refs_2_.refs_3_, ...), custom_call_target="tpu_custom_call" | custom-call | flops 549755813888 | bytes 1048576 | tf_op jit(solution)/shard_map/pallas_call | solution.py:299
  278.3 8.5 %reduce-scatter.9.cloned.1.call-done.refs_3_ = f32[512,384]{1,0:T(8,128)} async-done(((f32[2048,384]{1,0:T(8,128)}), f32[512,384]{1,0:T(8,128)}) %reduce-scatter.9.cloned.1.call-update) | async-done | bytes 786448 | tf_op jit(solution)/shard_map/reduce_scatter | solution.py:252
  295.5 7.5 %all_to_all.91 = f32[2,256,2048]{2,1,0:T(8,128)S(1)} all-to-all(f32[2,256,2048]{2,1,0:T(8,128)S(1)} %pad_maximum_fusion.3), channel_id=1, replica_groups={{0,1},{2,3},{4,5},{6,7},{8,9},{10,11},{12,13},{14,15},{16,17},{18,19},{..., dimensions={0} | all-to-all | bytes 8388608 | tf_op jit(solution)/shard_map/all_to_all | solution.py:600
  328.3 7.2 all_to_all.92
  357.9 22.1 %collective-permute-done.10.refs_1_ = f32[2,4,168,128]{3,2,1,0:T(8,128)} collective-permute-done((f32[2,4,168,128]{3,2,1,0:T(8,128)}, f32[2,4,168,128]{3,2,1,0:T(8,128)}, u32[]{:S(2)}, u32[]{:S(2)}) %collective-permute-start.10) | collective-permute-done | bytes 688160 | tf_op jit(solution)/shard_map/ppermute | solution.py:32
  416.5 7.2 all_to_all.93
  434.0 21.2 %collective-permute-done.15.refs_11_ = f32[2,4,168,128]{3,2,1,0:T(8,128)} collective-permute-done((f32[2,4,168,128]{3,2,1,0:T(8,128)}, f32[2,4,168,128]{3,2,1,0:T(8,128)}, u32[]{:S(2)}, u32[]{:S(2)}) %collective-permute-start.15) | collective-permute-done | bytes 688160 | tf_op jit(solution)/shard_map/ppermute | solution.py:32
  460.8 12.7 %shard_map.222 = (bf16[2,512,64]{2,1,0:T(8,128)(2,1)S(1)}, bf16[2,512,64]{2,1,0:T(8,128)(2,1)S(1)}, bf16[2,512,512]{2,1,0:T(8,128)(2,1)}) custom-call(bf16[2,512,64]{2,1,0:T(8,128)(2,1)S(1)} %bitcast.183, bf16[2,512,64]{2,1,0:T(8,128)(2,1)S(1)} %bitcast.178, bf16[2,512,512]{2,1,0:T(8,128)(2,1)} %bitcast.193, f32[2,1,512]{2,1,0:T(1,128)S(1)} %copy-done.80, ...), custom_call_target="tpu_custom_call" | custom-call | flops 549755813888 | bytes 1048576 | tf_op jit(solution)/shard_map/pallas_call | solution.py:234
  495.9 17.1 %reduce-scatter.15.cloned.1.call-done.refs_7_ = f32[256,640]{1,0:T(8,128)} async-done(((f32[1024,640]{1,0:T(8,128)}), f32[256,640]{1,0:T(8,128)}) %reduce-scatter.15.cloned.1.call-update) | async-done | bytes 655376 | tf_op jit(solution)/shard_map/reduce_scatter | solution.py:252
  523.8 7.1 all_to_all.94
  540.8 7.4 all_to_all.95
  585.6 7.3 all_to_all.96
  604.4 7.2 all_to_all.97.refs_0_
  611.7 7.0 shard_map.231
  618.7 7.1 all_to_all.98
  656.5 8.2 %all_to_all.99.refs_2_.refs_1_ = f32[2,256,2048]{2,1,0:T(8,128)} all-to-all(f32[2,256,2048]{2,1,0:T(8,128)S(1)} %pad_maximum_fusion.7), channel_id=1, replica_groups={{0,1},{2,3},{4,5},{6,7},{8,9},{10,11},{12,13},{14,15},{16,17},{18,19},{..., dimensions={0} | all-to-all | bytes 8388608 | tf_op jit(solution)/shard_map/all_to_all | solution.py:600
  673.9 8.0 %pad_maximum_fusion = f32[2,512,2048]{2,1,0:T(8,128)} fusion(f32[2,256,2048]{2,1,0:T(8,128)} %all_to_all.99.refs_2_.refs_1_, f32[2,256,2048]{2,1,0:T(8,128)} %copy-done.2), kind=kLoop, calls=%fused_computation.5 | loop fusion | flops 2097152 | bytes 16777216 | tf_op jit(solution)/shard_map/concatenate | solution.py:798
  684.4 10.7 %all-reduce = f32[8,256]{1,0:T(8,128)S(1)} all-reduce(f32[8,256]{1,0:T(8,128)} %shard_map.236), channel_id=9, replica_groups={{0,8,16,24},{4,12,20,28},{1,9,17,25},{5,13,21,29},{2,10,18,26},{6,14,22..., use_global_device_ids=true, to_apply=%region_21.22.clone | all-reduce | flops 2048 | bytes 16384
  702.4 7.4 all_to_all.101
  726.3 6.6 reduce-scatter.23.cloned.1.call-done.refs_0_
  (612 shorter events, 418.3 us)
Async XLA Ops:
  7.2 279.6 %reduce-scatter.9.cloned.1.call-start = ((), (), s32[]{:S(2)}) async-start(), calls=%async_computation.25 | async-start | bytes 3932160 | tf_op jit(solution)/shard_map/reduce_scatter | solution.py:252
  20.9 39.9 %collective-permute-start = (f32[2,4,168,128]{3,2,1,0:T(8,128)}, f32[2,4,168,128]{3,2,1,0:T(8,128)}, u32[]{:S(2)}, u32[]{:S(2)}) collective-permute-start(f32[2,4,168,128]{3,2,1,0:T(8,128)} %shard_map.203), channel_id=1, source_target_pairs={{0,4},{4,8},{8,12},{12,16},{16,20},{20,24},{24,28},{1,5},{5,9},{9,... | collective-permute-start | bytes 2064392 | tf_op jit(solution)/shard_map/ppermute | solution.py:32
  26.7 34.1 %collective-permute-start.1 = (f32[2,4,168,128]{3,2,1,0:T(8,128)}, f32[2,4,168,128]{3,2,1,0:T(8,128)}, u32[]{:S(2)}, u32[]{:S(2)}) collective-permute-start(f32[2,4,168,128]{3,2,1,0:T(8,128)} %shard_map.203), channel_id=1, source_target_pairs={{0,8},{4,12},{8,16},{12,20},{16,24},{20,28},{1,9},{5,13},{9,17},{1... | collective-permute-start | bytes 2064392 | tf_op jit(solution)/shard_map/ppermute | solution.py:32
  44.8 127.1 %collective-permute-start.4 = (f32[1024,1024]{1,0:T(8,128)}, f32[1024,1024]{1,0:T(8,128)}, u32[]{:S(2)}, u32[]{:S(2)}) collective-permute-start(f32[1024,1024]{1,0:T(8,128)} %shard_map.206), channel_id=1, source_target_pairs={{0,4},{4,0},{8,12},{12,8},{16,20},{20,16},{24,28},{28,24},{1,5},{5... | collective-permute-start | bytes 12582920 | tf_op jit(solution)/shard_map/ppermute | solution.py:247
  63.6 16.8 %collective-permute-start.2 = (f32[2,4,168,128]{3,2,1,0:T(8,128)S(1)}, f32[2,4,168,128]{3,2,1,0:T(8,128)S(1)}, u32[]{:S(2)}, u32[]{:S(2)}) collective-permute-start(f32[2,4,168,128]{3,2,1,0:T(8,128)S(1)} %fusion.44.refs_5_.refs_8_), channel_id=1, source_target_pairs={{0,8},{4,12},{8,16},{12,20},{16,24},{20,28},{1,9},{5,13},{9,17},{1... | collective-permute-start | bytes 2064392 | tf_op jit(solution)/shard_map/ppermute | solution.py:32
  96.9 48.8 %collective-permute-start.3 = (f32[256,2048]{1,0:T(8,128)}, f32[256,2048]{1,0:T(8,128)}, u32[]{:S(2)}, u32[]{:S(2)}) collective-permute-start(f32[256,2048]{1,0:T(8,128)} %fusion.34.refs_7_), channel_id=1, source_target_pairs={{0,2},{1,3},{2,0},{3,1},{4,6},{5,7},{6,4},{7,5},{8,10},{9,11},{10,... | collective-permute-start | bytes 6291464 | tf_op jit(solution)/shard_map/ppermute | solution.py:27
  114.6 77.0 %collective-permute-start.6 = (f32[256,2048]{1,0:T(8,128)}, f32[256,2048]{1,0:T(8,128)}, u32[]{:S(2)}, u32[]{:S(2)}) collective-permute-start(f32[256,2048]{1,0:T(8,128)} %fusion.33), channel_id=1, source_target_pairs={{0,2},{1,3},{2,0},{3,1},{4,6},{5,7},{6,4},{7,5},{8,10},{9,11},{10,... | collective-permute-start | bytes 6291464 | tf_op jit(solution)/shard_map/ppermute | solution.py:27
  169.2 91.8 %collective-permute-start.7 = (f32[512,1024]{1,0:T(8,128)}, f32[512,1024]{1,0:T(8,128)}, u32[]{:S(2)}, u32[]{:S(2)}) collective-permute-start(f32[512,1024]{1,0:T(8,128)} %slice_convert_fusion.1), channel_id=1, source_target_pairs={{0,4},{4,0},{8,12},{12,8},{16,20},{20,16},{24,28},{28,24},{1,5},{5... | collective-permute-start | bytes 6291464 | tf_op jit(solution)/shard_map/ppermute | solution.py:247
  190.1 88.2 %collective-permute-start.5 = (f32[256,2048]{1,0:T(8,128)}, f32[256,2048]{1,0:T(8,128)}, u32[]{:S(2)}, u32[]{:S(2)}) collective-permute-start(f32[256,2048]{1,0:T(8,128)} %fusion.32.refs_0_), channel_id=1, source_target_pairs={{0,2},{1,3},{2,0},{3,1},{4,6},{5,7},{6,4},{7,5},{8,10},{9,11},{10,... | collective-permute-start | bytes 6291464 | tf_op jit(solution)/shard_map/ppermute | solution.py:27
  219.2 48.8 %collective-permute-start.8 = (f32[512,1024]{1,0:T(8,128)}, f32[512,1024]{1,0:T(8,128)}, u32[]{:S(2)}, u32[]{:S(2)}) collective-permute-start(f32[512,1024]{1,0:T(8,128)} %slice_convert_fusion.refs_4_), channel_id=1, source_target_pairs={{0,4},{4,0},{8,12},{12,8},{16,20},{20,16},{24,28},{28,24},{1,5},{5... | collective-permute-start | bytes 6291464 | tf_op jit(solution)/shard_map/ppermute | solution.py:247
  227.2 156.3 %reduce-scatter.11.cloned.1.call-start = ((), (), s32[]{:S(2)}) async-start(), calls=%async_computation.26 | async-start | bytes 5242880 | tf_op jit(solution)/shard_map/reduce_scatter | solution.py:252
  238.3 110.0 %collective-permute-start.13 = (f32[1024,768]{1,0:T(8,128)}, f32[1024,768]{1,0:T(8,128)}, u32[]{:S(2)}, u32[]{:S(2)}) collective-permute-start(f32[1024,768]{1,0:T(8,128)} %shard_map.209.refs_4_), channel_id=1, source_target_pairs={{0,4},{4,0},{8,12},{12,8},{16,20},{20,16},{24,28},{28,24},{1,5},{5... | collective-permute-start | bytes 9437192 | tf_op jit(solution)/shard_map/ppermute | solution.py:247
  257.9 61.7 %collective-permute-start.9 = (f32[256,2048]{1,0:T(8,128)}, f32[256,2048]{1,0:T(8,128)}, u32[]{:S(2)}, u32[]{:S(2)}) collective-permute-start(f32[256,2048]{1,0:T(8,128)} %fusion.31.refs_8_.refs_0_), channel_id=1, source_target_pairs={{0,2},{1,3},{2,0},{3,1},{4,6},{5,7},{6,4},{7,5},{8,10},{9,11},{10,... | collective-permute-start | bytes 6291464 | tf_op jit(solution)/shard_map/ppermute | solution.py:27
  278.3 180.3 %reduce-scatter.13.cloned.1.call-start = ((), (), s32[]{:S(2)}) async-start(), calls=%async_computation.27 | async-start | bytes 3932160 | tf_op jit(solution)/shard_map/reduce_scatter | solution.py:252
  314.1 79.9 %collective-permute-start.12 = (f32[1024,640]{1,0:T(8,128)}, f32[1024,640]{1,0:T(8,128)}, u32[]{:S(2)}, u32[]{:S(2)}) collective-permute-start(f32[1024,640]{1,0:T(8,128)} %shard_map.213.refs_2_), channel_id=1, source_target_pairs={{0,4},{4,0},{8,12},{12,8},{16,20},{20,16},{24,28},{28,24},{1,5},{5... | collective-permute-start | bytes 7864328 | tf_op jit(solution)/shard_map/ppermute | solution.py:247
  347.0 32.9 %collective-permute-start.10 = (f32[2,4,168,128]{3,2,1,0:T(8,128)}, f32[2,4,168,128]{3,2,1,0:T(8,128)}, u32[]{:S(2)}, u32[]{:S(2)}) collective-permute-start(f32[2,4,168,128]{3,2,1,0:T(8,128)} %shard_map.215.refs_5_), channel_id=1, source_target_pairs={{8,0},{12,4},{16,8},{20,12},{24,16},{28,20},{9,1},{13,5},{17,9},{2... | collective-permute-start | bytes 2064392 | tf_op jit(solution)/shard_map/ppermute | solution.py:32
  354.5 158.5 %reduce-scatter.15.cloned.1.call-start = ((), (), s32[]{:S(2)}) async-start(), calls=%async_computation.28 | async-start | bytes 3276800 | tf_op jit(solution)/shard_map/reduce_scatter | solution.py:252
  382.0 24.3 %collective-permute-start.11 = (f32[2,4,168,128]{3,2,1,0:T(8,128)}, f32[2,4,168,128]{3,2,1,0:T(8,128)}, u32[]{:S(2)}, u32[]{:S(2)}) collective-permute-start(f32[2,4,168,128]{3,2,1,0:T(8,128)} %broadcast_select_fusion.refs_6_), channel_id=1, source_target_pairs={{0,4},{4,0},{8,12},{12,8},{16,20},{20,16},{24,28},{28,24},{1,5},{5... | collective-permute-start | bytes 2064392 | tf_op jit(solution)/shard_map/ppermute | solution.py:247
  393.4 85.4 %collective-permute-start.16 = (f32[1024,768]{1,0:T(8,128)}, f32[1024,768]{1,0:T(8,128)}, u32[]{:S(2)}, u32[]{:S(2)}) collective-permute-start(f32[1024,768]{1,0:T(8,128)} %shard_map.217.refs_5_), channel_id=1, source_target_pairs={{0,4},{4,0},{8,12},{12,8},{16,20},{20,16},{24,28},{28,24},{1,5},{5... | collective-permute-start | bytes 9437192 | tf_op jit(solution)/shard_map/ppermute | solution.py:247
  410.3 44.8 %collective-permute-start.15 = (f32[2,4,168,128]{3,2,1,0:T(8,128)}, f32[2,4,168,128]{3,2,1,0:T(8,128)}, u32[]{:S(2)}, u32[]{:S(2)}) collective-permute-start(f32[2,4,168,128]{3,2,1,0:T(8,128)} %shard_map.219.refs_0_.refs_10_), channel_id=1, source_target_pairs={{8,0},{12,4},{16,8},{20,12},{24,16},{28,20},{9,1},{13,5},{17,9},{2... | collective-permute-start | bytes 2064392 | tf_op jit(solution)/shard_map/ppermute | solution.py:32
  431.5 102.6 %collective-permute-start.14 = (f32[256,2048]{1,0:T(8,128)}, f32[256,2048]{1,0:T(8,128)}, u32[]{:S(2)}, u32[]{:S(2)}) collective-permute-start(f32[256,2048]{1,0:T(8,128)} %fusion.26.refs_4_.refs_0_), channel_id=1, source_target_pairs={{0,2},{1,3},{2,0},{3,1},{4,6},{5,7},{6,4},{7,5},{8,10},{9,11},{10,... | collective-permute-start | bytes 6291464 | tf_op jit(solution)/shard_map/ppermute | solution.py:27
  432.2 143.6 %reduce-scatter.17.cloned.1.call-start = ((), (), s32[]{:S(2)}) async-start(), calls=%async_computation.29 | async-start | bytes 3932160 | tf_op jit(solution)/shard_map/reduce_scatter | solution.py:252
  432.4 116.8 %collective-permute-start.18 = (f32[1024,640]{1,0:T(8,128)}, f32[1024,640]{1,0:T(8,128)}, u32[]{:S(2)}, u32[]{:S(2)}) collective-permute-start(f32[1024,640]{1,0:T(8,128)} %shard_map.221.refs_12_), channel_id=1, source_target_pairs={{0,4},{4,0},{8,12},{12,8},{16,20},{20,16},{24,28},{28,24},{1,5},{5... | collective-permute-start | bytes 7864328 | tf_op jit(solution)/shard_map/ppermute | solution.py:247
  494.4 140.3 %reduce-scatter.19.cloned.1.call-start = ((), (), s32[]{:S(2)}) async-start(), calls=%async_computation.30 | async-start | bytes 3276800 | tf_op jit(solution)/shard_map/reduce_scatter | solution.py:252
  494.4 133.6 %collective-permute-start.22 = (f32[1024,640]{1,0:T(8,128)}, f32[1024,640]{1,0:T(8,128)}, u32[]{:S(2)}, u32[]{:S(2)}) collective-permute-start(f32[1024,640]{1,0:T(8,128)} %copy-done.82), channel_id=1, source_target_pairs={{0,4},{4,0},{8,12},{12,8},{16,20},{20,16},{24,28},{28,24},{1,5},{5... | collective-permute-start | bytes 7864328 | tf_op jit(solution)/shard_map/ppermute | solution.py:247
  532.6 63.5 %collective-permute-start.17 = (f32[256,2048]{1,0:T(8,128)}, f32[256,2048]{1,0:T(8,128)}, u32[]{:S(2)}, u32[]{:S(2)}) collective-permute-start(f32[256,2048]{1,0:T(8,128)} %fusion.25.refs_2_.refs_0_), channel_id=1, source_target_pairs={{0,2},{1,3},{2,0},{3,1},{4,6},{5,7},{6,4},{7,5},{8,10},{9,11},{10,... | collective-permute-start | bytes 6291464 | tf_op jit(solution)/shard_map/ppermute | solution.py:27
  569.3 65.4 %collective-permute-start.21 = (f32[1024,512]{1,0:T(8,128)}, f32[1024,512]{1,0:T(8,128)}, u32[]{:S(2)}, u32[]{:S(2)}) collective-permute-start(f32[1024,512]{1,0:T(8,128)} %shard_map.228.refs_6_), channel_id=1, source_target_pairs={{0,4},{4,0},{8,12},{12,8},{16,20},{20,16},{24,28},{28,24},{1,5},{5... | collective-permute-start | bytes 6291464 | tf_op jit(solution)/shard_map/ppermute | solution.py:247
  570.8 124.9 %reduce-scatter.21.cloned.1.call-start = ((), (), s32[]{:S(2)}) async-start(), calls=%async_computation.31 | async-start | bytes 3276800 | tf_op jit(solution)/shard_map/reduce_scatter | solution.py:252
  594.6 53.6 %collective-permute-start.20 = (f32[256,2048]{1,0:T(8,128)}, f32[256,2048]{1,0:T(8,128)}, u32[]{:S(2)}, u32[]{:S(2)}) collective-permute-start(f32[256,2048]{1,0:T(8,128)} %fusion.24.refs_2_.refs_0_), channel_id=1, source_target_pairs={{0,2},{1,3},{2,0},{3,1},{4,6},{5,7},{6,4},{7,5},{8,10},{9,11},{10,... | collective-permute-start | bytes 6291464 | tf_op jit(solution)/shard_map/ppermute | solution.py:27
  627.4 68.2 %collective-permute-start.19 = (f32[256,2048]{1,0:T(8,128)}, f32[256,2048]{1,0:T(8,128)}, u32[]{:S(2)}, u32[]{:S(2)}) collective-permute-start(f32[256,2048]{1,0:T(8,128)} %fusion.23.refs_3_.refs_0_), channel_id=1, source_target_pairs={{0,2},{1,3},{2,0},{3,1},{4,6},{5,7},{6,4},{7,5},{8,10},{9,11},{10,... | collective-permute-start | bytes 6291464 | tf_op jit(solution)/shard_map/ppermute | solution.py:27
  634.6 98.3 %reduce-scatter.23.cloned.1.call-start = ((), (), s32[]{:S(2)}) async-start(), calls=%async_computation.32 | async-start | bytes 2621440 | tf_op jit(solution)/shard_map/reduce_scatter | solution.py:252
  667.9 43.9 %collective-permute-start.24 = (f32[256,384]{1,0:T(8,128)}, f32[256,384]{1,0:T(8,128)}, u32[]{:S(2)}, u32[]{:S(2)}) collective-permute-start(f32[256,384]{1,0:T(8,128)} %shard_map.238), channel_id=1, source_target_pairs={{0,4},{4,0},{8,12},{12,8},{16,20},{20,16},{24,28},{28,24},{1,5},{5... | collective-permute-start | bytes 1179656 | tf_op jit(solution)/shard_map/ppermute | solution.py:247
  (189 other events, 1173.5 us)
Sparse Core Ops, SparseCore 0:
  227.3 59.4 reduce-scatter.8
  289.6 87.1 reduce-scatter.10
  379.2 79.2 reduce-scatter.12
  460.8 52.1 reduce-scatter.14
  515.8 59.9 reduce-scatter.16
  578.1 52.1 reduce-scatter.18
  634.7 52.1 reduce-scatter.20
  689.2 43.5 reduce-scatter.22
